TPU v7x, 256 devices: a whole 4x4x8 slice. The times are simulated.
256 devices in a mesh: dp: 64 (over z, y, core), fsdp: 4 (over x).
Axes of the slice: x: 4, y: 4, z: 8, core: 2. Of those that a mesh axis runs over, the one named last changes fastest.
Arguments:
- x_rows: bfloat16 [4, 8192, 1024], P('fsdp', 'dp'), may hold values from -6 to 6
- cotangent: bfloat16 [4, 16384, 1024], P('fsdp', 'dp'), may hold values from -6 to 6
- w_in: bfloat16 [1024, 2048], P('fsdp'), may hold values from -0.1875 to 0.1875
- w_out: bfloat16 [512, 1024], P('fsdp'), may hold values from -0.5 to 0.5
- hist_blocks: int32 [4, 64], P('fsdp'), may hold values from 1 to 4, as said below
- owner: int32 [4, 64], P('fsdp'), may hold values from 0 to 63, as said below
Outputs:
- layer_out: bfloat16 [4, 16384, 1024], P('fsdp', 'dp')
- grad_x: bfloat16 [4, 8192, 1024], P('fsdp', 'dp')
- grad_w_in: float32 [1024, 2048], P('fsdp')
- grad_w_out: float32 [512, 1024], P('fsdp')
Inputs may be any that keep to these rules, and one draw needn't show every extreme that they name: `hist_blocks`: in each group the blocks of all histories sum to 128, and some history has exactly 4 blocks. In each group the histories of one owner have at most 4 blocks together, and some owner has exactly 4.
All inputs are finite; a program needn't handle non-finite values.
Results may differ from a plain program's by a relative error of at most 0.022.
Values may be sent and summed in bfloat16 or wider, within the bound.
No kernel may reach another device: no remote copies, remote signals or barrier semaphores. Data moves between devices by JAX's collectives and lax.ppermute only.
A program may use at most 128 MiB of HBM per device.

v0:
```python
import jax
import jax.numpy as jnp
from jax import lax
from jax.sharding import PartitionSpec as P

HEAD = 128


epsilon = 1e-06


def layer_rows(rows_in, w_in, w_out, segment):
    capacity = rows_in.shape[0]
    width = w_out.shape[0]
    values = rows_in.astype(jnp.float32)
    centred = values - jnp.mean(values, axis=1, keepdims=True)
    spread = jnp.mean(centred * centred, axis=1, keepdims=True)
    normed = (centred * lax.rsqrt(spread + epsilon)).astype(jnp.bfloat16)
    active = jax.nn.silu(jnp.dot(normed, w_in, preferred_element_type=jnp.float32)).astype(
        jnp.bfloat16
    )
    gate_u = active[:, :width]
    value_v = active[:, width : 2 * width]
    query = active[:, 2 * width : 3 * width]
    key_k = active[:, 3 * width :]
    positions = jnp.arange(capacity, dtype=jnp.int32)
    visible = (
        (segment[:, None] == segment[None, :])
        & (positions[None, :] <= positions[:, None])
        & (segment[:, None] >= 0)
    )
    pieces = []
    for head in range(width // HEAD):
        first = head * HEAD
        scores = lax.dot_general(
            query[:, first : first + HEAD],
            key_k[:, first : first + HEAD],
            (((1,), (1,)), ((), ())),
            preferred_element_type=jnp.float32,
        ) * HEAD ** (-0.5)
        weights = jnp.where(visible, jax.nn.silu(scores) / capacity, 0.0).astype(jnp.bfloat16)
        pieces.append(
            jnp.dot(weights, value_v[:, first : first + HEAD], preferred_element_type=jnp.float32)
        )
    attended = jnp.concatenate(pieces, axis=1)
    att_centred = attended - jnp.mean(attended, axis=1, keepdims=True)
    att_spread = jnp.mean(att_centred * att_centred, axis=1, keepdims=True)
    mixed = (gate_u.astype(jnp.float32) * (att_centred * lax.rsqrt(att_spread + epsilon))).astype(
        jnp.bfloat16
    )
    return (jnp.dot(mixed, w_out, preferred_element_type=jnp.float32) + values).astype(jnp.bfloat16)


def history_layout(blocks, owners):
    count = blocks.shape[0]
    start = jnp.cumsum(blocks) - blocks
    order_ids = jnp.arange(count, dtype=jnp.int32)
    earlier = (owners[:, None] == owners[None, :]) & (order_ids[None, :] < order_ids[:, None])
    before = jnp.sum(jnp.where(earlier, blocks[None, :], 0), axis=1)
    return (start, before)


def anchor_targets(start, before, row_count):
    row_ids = jnp.arange(row_count, dtype=jnp.int32)
    seq_of = jnp.sum((start[None, :] <= row_ids[:, None]).astype(jnp.int32), axis=1) - 1
    slot_index = before[seq_of] + row_ids - start[seq_of]
    return (seq_of, slot_index)


def owner_segment(blocks, owners, before, my_index, capacity, devices):
    count = blocks.shape[0]
    row_ids = jnp.arange(capacity, dtype=jnp.int32)[:, None]
    inside = (
        (owners[None, :] == my_index)
        & (row_ids >= before[None, :] * devices)
        & (row_ids < (before + blocks)[None, :] * devices)
    )
    labels = jnp.arange(count, dtype=jnp.int32)[None, :] + 1
    return jnp.sum(jnp.where(inside, labels, 0), axis=1) - 1


def on_device(x_rows, cotangent, w_in, w_out, hist_blocks, owner):
    device_count = lax.axis_size("dp")
    my_index = lax.axis_index("dp")
    rows_here = x_rows[0]
    cot_rows = cotangent[0]
    row_count = rows_here.shape[0]
    capacity = cot_rows.shape[0]
    slot_rows = capacity // device_count
    width_d = rows_here.shape[1]
    blocks = hist_blocks[0]
    owners = owner[0]
    start, before = history_layout(blocks, owners)
    seq_of, slot_index = anchor_targets(start, before, row_count)
    target = slot_index * device_count + owners[seq_of]
    source_of = (
        jnp.full((slot_rows * device_count,), row_count, jnp.int32)
        .at[target]
        .set(jnp.arange(row_count, dtype=jnp.int32))
    )
    padded = jnp.concatenate([rows_here, jnp.zeros((1, width_d), rows_here.dtype)], axis=0)
    outgoing = jnp.take(padded, source_of, axis=0).reshape(slot_rows, device_count, width_d)
    full_in, full_out = (
        lax.all_gather(w_in, "fsdp", axis=0, tiled=True),
        lax.all_gather(w_out, "fsdp", axis=0, tiled=True),
    )
    arrived = lax.all_to_all(outgoing, "dp", split_axis=1, concat_axis=1, tiled=True)
    owned = arrived.reshape(capacity, width_d)
    segment = owner_segment(blocks, owners, before, my_index, capacity, device_count)

    def forward(first_arg, second_arg, third_arg):
        return layer_rows(first_arg, second_arg, third_arg, segment)

    result, pullback = jax.vjp(forward, owned, full_in, full_out)
    d_owned, d_in, d_out = pullback(cot_rows)
    returned = lax.all_to_all(
        d_owned.reshape(slot_rows, device_count, width_d),
        "dp",
        split_axis=1,
        concat_axis=1,
        tiled=True,
    )
    grad_rows = jnp.take(returned.reshape(capacity, width_d), target, axis=0)
    term_in = d_in.astype(jnp.float32)
    term_out = d_out.astype(jnp.float32)
    shard_in, shard_out = (
        lax.psum_scatter(
            term_in.astype(jnp.bfloat16), "fsdp", scatter_dimension=0, tiled=True
        ).astype(jnp.float32),
        lax.psum_scatter(
            term_out.astype(jnp.bfloat16), "fsdp", scatter_dimension=0, tiled=True
        ).astype(jnp.float32),
    )
    summed_in, summed_out = lax.psum((shard_in, shard_out), "dp")
    factor = 1.0 / (device_count * lax.axis_size("fsdp"))
    return (result[None], grad_rows[None], summed_in * factor, summed_out * factor)


def solution(mesh):
    placed = (
        P("fsdp", "dp", None),
        P("fsdp", "dp", None),
        P("fsdp", None),
        P("fsdp", None),
        P("fsdp", None),
        P("fsdp", None),
    )
    return jax.shard_map(
        on_device,
        mesh=mesh,
        in_specs=placed,
        out_specs=(P("fsdp", "dp", None), P("fsdp", "dp", None), P("fsdp", None), P("fsdp", None)),
        check_vma=False,
    )
```

profile of v0, /device:TPU:1, one launch (start us, length us, event | category | flops | bytes accessed | tf_op | source)
XLA Modules:
  0.0 468.2 jit_solution(14349330107434732594)
XLA Ops:
  8.9 0.9 select_reduce_fusion.1
  10.6 1.6 gather_fusion.2
  12.2 1.2 gather_fusion
  13.4 1.2 gather_fusion.1
  14.7 1.0 scatter_custom_fusion
  16.0 1.2 gather_fusion.3
  17.2 1.3 copy_select_fusion
  18.5 13.2 %all-to-all-start = ((bf16[4,64,1024]{2,0,1:T(4,128)(2,1)}), bf16[4,64,1024]{2,0,1:T(4,128)(2,1)S(1)}, u32[]{:S(2)}, u32[]{:S(2)}) async-start(bf16[4,64,1024]{2,0,1:T(4,128)(2,1)} %copy_select_fusion), calls=%async_computation | async-start | bytes 1048576 | tf_op jit(solution)/shard_map/all_to_all | solution.py:107
  32.6 16.7 %all-to-all-done = bf16[4,64,1024]{2,0,1:T(4,128)(2,1)S(1)} async-done(((bf16[4,64,1024]{2,0,1:T(4,128)(2,1)}), bf16[4,64,1024]{2,0,1:T(4,128)(2,1)S(1)}, u32[]{:S(2)}, u32[]{:S(2)}) %all-to-all-start) | async-done | bytes 524320 | tf_op jit(solution)/shard_map/all_to_all | solution.py:107
  51.4 13.1 %all-gather.3.cloned.1.call-done = bf16[1024,2048]{1,0:T(8,128)(2,1)} async-done(((bf16[256,2048]{1,0:T(8,128)(2,1)}), bf16[1024,2048]{1,0:T(8,128)(2,1)}) %all-gather.3.cloned.1.call-update) | async-done | bytes 4194320 | tf_op jit(solution)/shard_map/all_gather | solution.py:104
  64.5 4.8 %multiply_convert_fusion = (bf16[256,2048]{1,0:T(8,128)(2,1)S(1)}, f32[256,2048]{1,0:T(8,128)}) fusion(bf16[256,1024]{1,0:T(8,128)(2,1)S(1)} %multiply_convert_fusion.1, bf16[1024,2048]{1,0:T(8,128)(2,1)} %all-gather.3.cloned.1.call-done), kind=kOutput, calls=%fused_computation.12 | convolution fusion | flops 1076363264 | bytes 7864320 | tf_op jit(solution)/shard_map/jvp()/dot_general | solution.py:19
  70.4 1.0 select_convert_fusion.2
  72.9 19.4 %all-gather.5.cloned.1.call-done = bf16[512,1024]{1,0:T(8,128)(2,1)} async-done(((bf16[128,1024]{1,0:T(8,128)(2,1)}), bf16[512,1024]{1,0:T(8,128)(2,1)}) %all-gather.5.cloned.1.call-update) | async-done | bytes 1048592 | tf_op jit(solution)/shard_map/all_gather | solution.py:105
  92.3 1.8 multiply_reduce_fusion.1
  94.2 0.9 fusion.88
  99.8 0.9 fusion.23
  100.7 1.5 convolution_convert_fusion.1
  102.3 1.7 convolution_convert_fusion.12
  104.0 1.2 fusion.29
  107.7 1.1 pad_add_fusion
  109.0 0.9 pad_add_fusion.1
  110.2 1.1 convolution_convert_fusion.17
  112.6 3.4 convolution_convert_fusion
  116.0 0.9 copy-done.21
  117.0 4.8 %fusion.17 = (f32[256]{0:T(256)S(1)}, bf16[256,1024]{1,0:T(8,128)(2,1)S(1)}) fusion(f32[4,64,1024]{2,1,0:T(8,128)S(1)} %copy.67, f32[256]{0:T(256)S(1)} %div.80, bf16[1024,2048]{1,0:T(8,128)(2,1)} %all-gather.3.cloned.1.call-done, f32[256,2048]{1,0:T(8,128)} %get-tuple-element.20, bf16[256,512]{1,0:T(8,128)(2,1)} %get-tuple-element.10, ...), kind=kOutput, calls=%fused_computation.56 | convolution fusion | flops 1083965184 | bytes 8914944 | tf_op jit(solution)/shard_map/transpose(jvp())/dot_general | solution.py:19
  122.6 1.2 copy.75
  123.8 11.8 %all-to-all-start.1 = ((bf16[4,64,1024]{2,0,1:T(4,128)(2,1)}), bf16[4,64,1024]{2,0,1:T(4,128)(2,1)S(1)}, u32[]{:S(2)}, u32[]{:S(2)}) async-start(bf16[4,64,1024]{2,0,1:T(4,128)(2,1)} %copy.75), calls=%async_computation.1 | async-start | bytes 1048576 | tf_op jit(solution)/shard_map/all_to_all | solution.py:116
  135.7 2.5 fusion.3
  138.2 15.1 %all-to-all-done.1 = bf16[4,64,1024]{2,0,1:T(4,128)(2,1)S(1)} async-done(((bf16[4,64,1024]{2,0,1:T(4,128)(2,1)}), bf16[4,64,1024]{2,0,1:T(4,128)(2,1)S(1)}, u32[]{:S(2)}, u32[]{:S(2)}) %all-to-all-start.1) | async-done | bytes 524320 | tf_op jit(solution)/shard_map/all_to_all | solution.py:116
  155.2 31.5 %reduce-scatter.3.cloned.1.call-done = bf16[256,2048]{1,0:T(8,128)(2,1)} async-done(((bf16[1024,2048]{1,0:T(8,128)(2,1)}), bf16[256,2048]{1,0:T(8,128)(2,1)}) %reduce-scatter.3.cloned.1.call-update) | async-done | bytes 1048592 | tf_op jit(solution)/shard_map/reduce_scatter | solution.py:127
  186.7 272.7 %all-reduce.19 = (f32[256,2048]{1,0:T(8,128)S(1)}, f32[128,1024]{1,0:T(8,128)S(1)}) all-reduce(bf16[256,2048]{1,0:T(8,128)(2,1)} %reduce-scatter.3.cloned.1.call-done, bf16[128,1024]{1,0:T(8,128)(2,1)} %reduce-scatter.5.cloned.1.call-done), channel_id=1, replica_groups=mesh['dp'=64,'fsdp'=4] {'dp'}, use_global_device_ids=true, to_apply=%region_17.18 | all-reduce | flops 655360 | bytes 3932160 | tf_op jit(solution)/shard_map/psum | solution.py:134
  459.3 1.5 broadcast_multiply_fusion
  (160 shorter events, 20.3 us)
Async XLA Ops:
  7.2 6.2 %copy-start.27 = (s32[1,64]{1,0:T(1,128)S(1)}, s32[1,64]{1,0:T(1,128)}, u32[]{:S(2)}) copy-start(s32[1,64]{1,0:T(1,128)} %param.10) | copy-start | bytes 772
  7.2 8.8 %copy-start.13 = (bf16[1,128,1024]{2,1,0:T(8,128)(2,1)S(1)}, bf16[1,128,1024]{2,1,0:T(8,128)(2,1)}, u32[]{:S(2)}) copy-start(bf16[1,128,1024]{2,1,0:T(8,128)(2,1)} %param.6) | copy-start | bytes 786436
  7.2 57.3 %all-gather.3.cloned.1.call-start = ((), (), s32[]{:S(2)}) async-start(), calls=%async_computation.4 | async-start | bytes 5242880 | tf_op jit(solution)/shard_map/all_gather | solution.py:104
  12.2 3.8 copy-start.28
  13.4 2.5 copy-start.30
  17.2 15.3 %copy-start = (s32[1,64]{1,0:T(1,128)S(1)}, s32[1,64]{1,0:T(1,128)}, u32[]{:S(2)}) copy-start(s32[1,64]{1,0:T(1,128)} %param.11) | copy-start | bytes 772
  18.5 30.9 %all-to-all-start = ((bf16[4,64,1024]{2,0,1:T(4,128)(2,1)}), bf16[4,64,1024]{2,0,1:T(4,128)(2,1)S(1)}, u32[]{:S(2)}, u32[]{:S(2)}) async-start(bf16[4,64,1024]{2,0,1:T(4,128)(2,1)} %copy_select_fusion), calls=%async_computation | async-start | bytes 1048576 | tf_op jit(solution)/shard_map/all_to_all | solution.py:107
  31.6 60.6 %all-gather.5.cloned.1.call-start = ((), (), s32[]{:S(2)}) async-start(), calls=%async_computation.5 | async-start | bytes 1310720 | tf_op jit(solution)/shard_map/all_gather | solution.py:105
  32.4 122.8 %reduce-scatter.5.cloned.1.call-start = ((), (), s32[]{:S(2)}) async-start(), calls=%async_computation.7 | async-start | bytes 1310720 | tf_op jit(solution)/shard_map/reduce_scatter | solution.py:130
  32.6 37.3 %copy-start.38 = (pred[256]{0:T(512)(128)(4,1)}, pred[256]{0:T(512)(128)(4,1)S(1)}, u32[]{:S(2)}) copy-start(pred[256]{0:T(512)(128)(4,1)S(1)} %broadcast_compare_fusion) | copy-start | bytes 772
  32.6 37.2 %copy-start.36 = (s32[256]{0:T(256)}, s32[256]{0:T(256)S(1)}, u32[]{:S(2)}) copy-start(s32[256]{0:T(256)S(1)} %broadcast_add_fusion.1) | copy-start | bytes 3076
  51.4 17.9 %copy-start.2 = (bf16[256,1024]{1,0:T(8,128)(2,1)}, bf16[256,1024]{1,0:T(8,128)(2,1)S(1)}, u32[]{:S(2)}) copy-start(bf16[256,1024]{1,0:T(8,128)(2,1)S(1)} %multiply_convert_fusion.1) | copy-start | bytes 1572868
  71.4 20.9 %copy-start.1 = (bf16[1,256,1024]{2,1,0:T(8,128)(2,1)S(1)}, bf16[1,256,1024]{2,1,0:T(8,128)(2,1)}, u32[]{:S(2)}) copy-start(bf16[1,256,1024]{2,1,0:T(8,128)(2,1)} %param.7) | copy-start | bytes 1572868
  94.1 2.0 copy-start.7
  94.1 2.8 copy-start.5
  94.1 4.5 copy-start.19
  94.1 4.5 copy-start.37
  94.1 4.5 copy-start.39
  95.1 4.4 copy-start.17
  105.8 3.0 copy-start.10
  105.8 4.1 copy-start.11
  107.4 79.2 %reduce-scatter.3.cloned.1.call-start = ((), (), s32[]{:S(2)}) async-start(), calls=%async_computation.6 | async-start | bytes 5242880 | tf_op jit(solution)/shard_map/reduce_scatter | solution.py:127
  107.7 4.9 %copy-start.3 = (bf16[256,1024]{1,0:T(8,128)(2,1)S(1)}, bf16[256,1024]{1,0:T(8,128)(2,1)}, u32[]{:S(2)}) copy-start(bf16[256,1024]{1,0:T(8,128)(2,1)} %copy-done.2) | copy-start | bytes 1572868
  107.7 4.9 %copy-start.24 = (bf16[256,512]{1,0:T(8,128)(2,1)S(1)}, bf16[256,512]{1,0:T(8,128)(2,1)}, u32[]{:S(2)}) copy-start(bf16[256,512]{1,0:T(8,128)(2,1)} %get-tuple-element.10) | copy-start | bytes 786436
  107.7 4.9 %copy-start.40 = (f32[256,2048]{1,0:T(8,128)S(1)}, f32[256,2048]{1,0:T(8,128)}, u32[]{:S(2)}) copy-start(f32[256,2048]{1,0:T(8,128)} %get-tuple-element.20) | copy-start | bytes 6291460
  108.8 3.0 copy-start.20
  117.0 4.8 %copy-start.26 = (f32[256]{0:T(256)S(1)}, f32[256]{0:T(256)}, u32[]{:S(2)}) copy-start(f32[256]{0:T(256)} %copy-done.25) | copy-start | bytes 3076
  122.2 13.5 %copy-start.35 = (s32[128]{0:T(128)S(1)}, s32[128]{0:T(128)}, u32[]{:S(2)}) copy-start(s32[128]{0:T(128)} %copy-done.34) | copy-start | bytes 1540
  122.2 13.5 %copy-start.29 = (s32[128]{0:T(128)S(1)}, s32[128]{0:T(128)}, u32[]{:S(2)}) copy-start(s32[128]{0:T(128)} %copy-done.28) | copy-start | bytes 1540
  122.2 13.5 %copy-start.31 = (s32[128]{0:T(128)S(1)}, s32[128]{0:T(128)}, u32[]{:S(2)}) copy-start(s32[128]{0:T(128)} %copy-done.30) | copy-start | bytes 1540
  122.2 13.5 %copy-start.33 = (s32[128]{0:T(128)S(1)}, s32[128]{0:T(128)}, u32[]{:S(2)}) copy-start(s32[128]{0:T(128)} %copy-done.32) | copy-start | bytes 1540
  123.8 29.5 %all-to-all-start.1 = ((bf16[4,64,1024]{2,0,1:T(4,128)(2,1)}), bf16[4,64,1024]{2,0,1:T(4,128)(2,1)S(1)}, u32[]{:S(2)}, u32[]{:S(2)}) async-start(bf16[4,64,1024]{2,0,1:T(4,128)(2,1)} %copy.75), calls=%async_computation.1 | async-start | bytes 1048576 | tf_op jit(solution)/shard_map/all_to_all | solution.py:116
  (15 other events, 15.0 us)
Sparse Core Ops, SparseCore 0:
  9.8 54.5 all-gather.2
  66.3 25.9 all-gather.4
  107.6 25.9 reduce-scatter.4
  136.1 50.4 reduce-scatter.2
where the time goes:
time: 472 us; the launch traced here: 468 us
  blocking collectives  273 us (58%)
  waiting for transfers between devices  97.2 us (21%)
  matrix products  33.4 us (7%)
  starting transfers between devices  25.3 us (5%)
  between operations  14.5 us (3%)
  local copies, waits for them, and re-layouts  13.7 us (3%)
  other arithmetic  11.4 us (2%)
    psum x1, blocking collectives, on_device(): summed_in, summed_out = lax.psum((shard_in, shard_out), 'dp')  273 us
    reduce_scatter x1, waiting for transfers between devices, on_device(): lax.psum_scatter(term_in.astype(jnp.bfloat16), 'fsdp', scatter_dimension=...  31.5 us
    all_gather x1, waiting for transfers between devices, on_device(): lax.all_gather(w_out, 'fsdp', axis=0, tiled=True)  19.4 us
    all_to_all x1, waiting for transfers between devices, on_device(): lax.all_to_all(outgoing, 'dp', split_axis=1, concat_axis=1, tiled=True)  16.7 us
    all_to_all x1, waiting for transfers between devices, on_device(): lax.all_to_all(d_owned.reshape(slot_rows, device_count, width_d), 'dp', s...  15.1 us
    all_to_all x1, starting transfers between devices, on_device(): lax.all_to_all(outgoing, 'dp', split_axis=1, concat_axis=1, tiled=True)  13.2 us
    all_gather x1, waiting for transfers between devices, on_device(): lax.all_gather(w_in, 'fsdp', axis=0, tiled=True)  13.1 us
    dot_general x3, matrix products, layer_rows(): jnp.dot(normed, w_in, preferred_element_type=jnp.float32)  13 us
  transfers between devices with their start and end apart: 6, of which 5 were waited for; matrix products, arithmetic and copies ran while one was open for 8% of the time, Pallas kernels for 0%

commit v1 on v0

v1 whole, which is shorter than its diff:
```python
import functools

import jax
import jax.numpy as jnp
from jax import lax
from jax.experimental import pallas as pl
from jax.experimental.pallas import tpu as pltpu
from jax.sharding import Mesh, PartitionSpec as P

F32 = jnp.float32
BF16 = jnp.bfloat16
EPS = 1e-06
HEAD = 128
DP = ("z", "y", "c")
NN = (((1,), (0,)), ((), ()))
NT = (((1,), (1,)), ((), ()))
TN = (((0,), (0,)), ((), ()))
VMEM_LIMIT = 56 * 1024 * 1024


def dot(a, b, dims=NN):
    return lax.dot_general(a, b, dims, preferred_element_type=F32)


def iota(shape, dim):
    return lax.broadcasted_iota(jnp.int32, shape, dim)


def call(body, outs, args, name, scratch=(), smem=0):
    return pl.pallas_call(
        body,
        out_shape=[jax.ShapeDtypeStruct(s, d) for s, d in outs],
        in_specs=[pl.BlockSpec(memory_space=pltpu.VMEM) for _ in args],
        out_specs=[pl.BlockSpec(memory_space=pltpu.VMEM) for _ in outs],
        scratch_shapes=[pltpu.VMEM(s, d) for s, d in scratch],
        compiler_params=pltpu.CompilerParams(vmem_limit_bytes=VMEM_LIMIT),
        name=name,
    )(*args)


def histories(blocks_ref, owners_ref):
    n_row = blocks_ref[...].astype(F32)
    o_row = owners_ref[...].astype(F32)
    count = n_row.shape[1]
    r, c = iota((count, count), 0), iota((count, count), 1)
    column = lambda cond, row: jnp.sum(jnp.where(cond, row, 0.0), axis=1, keepdims=True)
    n_col = column(r == c, n_row)
    o_col = column(r == c, o_row)
    start = column(c < r, n_row)
    same = o_col == o_row
    before_col = column((c < r) & same, n_row)
    before_row = jnp.sum(jnp.where((r < c) & same, n_col, 0.0), axis=0, keepdims=True)
    return n_row, o_row, n_col, o_col, start, before_col, before_row


def slots_of_rows(blocks_ref, owners_ref, count):
    _, _, n_col, o_col, start, before, _ = histories(blocks_ref, owners_ref)
    b = iota((n_col.shape[0], count), 1).astype(F32)
    inside = (start <= b) & (b < start + n_col)
    code = jnp.sum(jnp.where(inside, o_col * 4.0 + before - start, 0.0), axis=0, keepdims=True)
    return (code + b[:1]).astype(jnp.int32)


def prep_body(blocks_ref, owners_ref, x_ref, w_in_ref, w_out_ref, out_ref, pack_ref):
    half = lax.axis_index("c")
    pack_ref[:256, :] = w_in_ref[:, pl.ds(pl.multiple_of(half * 1024, 1024), 1024)]
    wo = w_out_ref[:, pl.ds(pl.multiple_of(half * 512, 512), 512)]
    pack_ref[256:, :512] = wo[:64]
    pack_ref[256:, 512:] = wo[64:]
    code = slots_of_rows(blocks_ref, owners_ref, 128)
    row = iota((1024, 128), 0)
    total = None
    for j in range(4):
        pick = (row == code * 4 + j).astype(F32).astype(BF16)
        part = dot(pick, x_ref[:, j * 256 : (j + 1) * 256])
        total = part if total is None else total + part
    out_ref[...] = total.astype(BF16)


def rows_back_body(blocks_ref, owners_ref, returned_ref, out_ref):
    code = slots_of_rows(blocks_ref, owners_ref, 128)
    eye = iota((128, 128), 0) == iota((128, 128), 1)
    column = jnp.sum(jnp.where(eye, code.astype(F32), 0.0), axis=1, keepdims=True).astype(jnp.int32)
    lane = iota((128, 1024), 1)
    for j in range(4):
        pick = (lane == column * 4 + j).astype(F32).astype(BF16)
        out_ref[:, j * 256 : (j + 1) * 256] = dot(pick, returned_ref[...]).astype(BF16)


def weights_of(x, half, refs):
    w_in, w_out, own, other = refs
    other_half = 1 - half

    def proj(k, is_own):
        if k == 0:
            h = half if is_own else other_half
            return w_in[:, pl.ds(pl.multiple_of(h * 1024, 1024), 1024)]
        return (own if is_own else other)[k - 1][:256, :]

    def back(k, is_own):
        if k == 0:
            h = half if is_own else other_half
            return w_out[:, pl.ds(pl.multiple_of(h * 512, 512), 512)]
        ref = (own if is_own else other)[k - 1]
        return jnp.concatenate([ref[256:, :512], ref[256:, 512:]], axis=0)

    return proj, back


def grad_chunks(x, y, half, nrm, dpre, mix, cot, out):
    right = cot[:, pl.ds(pl.multiple_of(half * 512, 512), 512)]
    for sx in range(4):
        block = (x + sx) % 4
        d_in = dot(nrm[block], dpre[half], TN).astype(BF16)
        d_out = dot(mix[block], right, TN).astype(BF16)
        tail = jnp.concatenate([d_out[:64], d_out[64:]], axis=1)
        for m in range(4):
            sy = (m + 4 - y) % 4
            if m < 3:
                rows = d_in[80 * m : 80 * m + 80]
            else:
                rows = jnp.concatenate([d_in[240:], tail], axis=0)
            out[0, sx, sy] = rows[:, :512]
            out[1, sy, sx] = rows[:, 512:]


CHUNK = 32


def layer_body(
    blocks_ref, owners_ref, arrived, cot, w_in, w_out, a1, b1, a2, b2, a3, b3,
    layer_out, gother, nrm, dpre, mix, rstd,
    owned, pre, act, att, att_rstd, weights, dscore, dmixed, datt,
):
    x, y, c = lax.axis_index("x"), lax.axis_index("y"), lax.axis_index("c")
    me = (lax.axis_index("z") * 4 + y) * 2 + c
    proj, back = weights_of(x, c, (w_in, w_out, (a1, a2, a3), (b1, b2, b3)))
    halves = ((True, c), (False, 1 - c))

    t = iota((256, 1024), 0)
    wanted = (t & 63) * 16 + (t >> 6) * 4
    lane = iota((256, 1024), 1)
    for j in range(4):
        pick = (lane == wanted + j).astype(F32).astype(BF16)
        owned[:, j * 256 : (j + 1) * 256] = dot(pick, arrived[...])

    def norm_rows(r, _):
        rows = pl.ds(pl.multiple_of(r * CHUNK, CHUNK), CHUNK)
        v = owned[rows, :]
        cen = v - jnp.sum(v, axis=1, keepdims=True) * (1.0 / 1024)
        rs = lax.rsqrt(jnp.sum(cen * cen, axis=1, keepdims=True) * (1.0 / 1024) + EPS)
        n = (cen * rs).astype(BF16)
        for j in range(4):
            nrm[j, rows, :] = n[:, j * 256 : (j + 1) * 256]
        rstd[rows, :] = jnp.broadcast_to(rs, (CHUNK, 128))
        return 0

    lax.fori_loop(0, 256 // CHUNK, norm_rows, 0)

    for is_own, h in halves:
        total = None
        for k in range(4):
            part = dot(nrm[(x + 4 - k) % 4], proj(k, is_own))
            total = part if total is None else total + part
        pre[h] = total

    def activate(r, _):
        rows = pl.ds(pl.multiple_of(r * CHUNK, CHUNK), CHUNK)
        for h in range(2):
            v = pre[h, rows, :]
            sig = jax.nn.sigmoid(v)
            act[h, rows, :] = (v * sig).astype(BF16)
            pre[h, rows, :] = sig * (1.0 + v * (1.0 - sig))
        return 0

    lax.fori_loop(0, 256 // CHUNK, activate, 0)

    n_row, o_row, n_col, o_col, _, before_col, before_row = histories(blocks_ref, owners_ref)
    mine = me.astype(F32)
    label = 1.0 + iota((64, 256), 0).astype(F32)
    at = iota((64, 256), 1).astype(F32)
    inside = (o_col == mine) & (at >= before_col * 64.0) & (at < (before_col + n_col) * 64.0)
    seg_row = jnp.sum(jnp.where(inside, label, 0.0), axis=0, keepdims=True)
    label = 1.0 + iota((256, 64), 1).astype(F32)
    at = iota((256, 64), 0).astype(F32)
    inside = (o_row == mine) & (at >= before_row * 64.0) & (at < (before_row + n_row) * 64.0)
    seg_col = jnp.sum(jnp.where(inside, label, 0.0), axis=1, keepdims=True)
    visible = (seg_row == seg_col) & (iota((256, 256), 1) <= iota((256, 256), 0)) & (seg_col > 0.0)
    mask = jnp.where(visible, 1.0 / 256.0, 0.0)

    scale = HEAD ** (-0.5)
    for h in range(4):
        lo, hi = h * HEAD, (h + 1) * HEAD
        s = dot(act[1, :, lo:hi], act[1, :, 512 + lo : 512 + hi], NT) * scale
        sig = jax.nn.sigmoid(s)
        w = (s * sig * mask).astype(BF16)
        weights[h] = w
        dscore[h] = mask * (sig * (1.0 + s * (1.0 - sig))) * scale
        att[:, lo:hi] = dot(w, act[0, :, 512 + lo : 512 + hi])

    def mix_rows(r, _):
        rows = pl.ds(pl.multiple_of(r * CHUNK, CHUNK), CHUNK)
        v = att[rows, :]
        cen = v - jnp.sum(v, axis=1, keepdims=True) * (1.0 / 512)
        rs = lax.rsqrt(jnp.sum(cen * cen, axis=1, keepdims=True) * (1.0 / 512) + EPS)
        hat = cen * rs
        mixed = (act[0, rows, :512].astype(F32) * hat).astype(BF16)
        for h in range(4):
            mix[h, rows, :] = mixed[:, h * HEAD : (h + 1) * HEAD]
        att[rows, :] = hat
        att_rstd[rows, :] = jnp.broadcast_to(rs, (CHUNK, 128))
        return 0

    lax.fori_loop(0, 256 // CHUNK, mix_rows, 0)

    for is_own, h in halves:
        columns = pl.ds(pl.multiple_of(h * 512, 512), 512)
        total = owned[:, columns]
        for k in range(4):
            total = total + dot(mix[(x + 4 - k) % 4], back(k, is_own))
        layer_out[:, columns] = total.astype(BF16)

    for k in range(4):
        total = None
        for is_own, h in halves:
            columns = pl.ds(pl.multiple_of(h * 512, 512), 512)
            part = dot(cot[:, columns], back(k, is_own), NT)
            total = part if total is None else total + part
        dmixed[(x + 4 - k) % 4] = total.astype(BF16)

    def unmix_rows(r, _):
        rows = pl.ds(pl.multiple_of(r * CHUNK, CHUNK), CHUNK)
        dm = jnp.concatenate([dmixed[h, rows, :] for h in range(4)], axis=1).astype(F32)
        hat = att[rows, :]
        du = (dm * hat).astype(BF16).astype(F32)
        dpre[0, rows, :512] = (du * pre[0, rows, :512]).astype(BF16)
        dh = dm * act[0, rows, :512].astype(F32)
        m1 = jnp.sum(dh, axis=1, keepdims=True) * (1.0 / 512)
        m2 = jnp.sum(dh * hat, axis=1, keepdims=True) * (1.0 / 512)
        datt[rows, :] = (att_rstd[rows, :1] * (dh - m1 - hat * m2)).astype(BF16)
        return 0

    lax.fori_loop(0, 256 // CHUNK, unmix_rows, 0)

    for h in range(4):
        lo, hi = h * HEAD, (h + 1) * HEAD
        d_h = datt[:, lo:hi]
        dw = dot(d_h, act[0, :, 512 + lo : 512 + hi], NT).astype(BF16).astype(F32)
        ds = (dw * dscore[h]).astype(BF16)
        dv = dot(weights[h], d_h, TN).astype(BF16).astype(F32)
        dq = dot(ds, act[1, :, 512 + lo : 512 + hi]).astype(BF16).astype(F32)
        dk = dot(ds, act[1, :, lo:hi], TN).astype(BF16).astype(F32)
        dpre[0, :, 512 + lo : 512 + hi] = (dv * pre[0, :, 512 + lo : 512 + hi]).astype(BF16)
        dpre[1, :, lo:hi] = (dq * pre[1, :, lo:hi]).astype(BF16)
        dpre[1, :, 512 + lo : 512 + hi] = (dk * pre[1, :, 512 + lo : 512 + hi]).astype(BF16)

    grad_chunks(x, y, 1 - c, nrm, dpre, mix, cot, gother)


def rest_body(
    nrm, dpre, mix, rstd, cot, w_in, w_out, a1, b1, a2, b2, a3, b3,
    gown, outgoing, dnorm, downed,
):
    x, y, c = lax.axis_index("x"), lax.axis_index("y"), lax.axis_index("c")
    proj, _ = weights_of(x, c, (w_in, w_out, (a1, a2, a3), (b1, b2, b3)))
    grad_chunks(x, y, c, nrm, dpre, mix, cot, gown)
    for k in range(4):
        total = None
        for is_own, h in ((True, c), (False, 1 - c)):
            part = dot(dpre[h], proj(k, is_own), NT)
            total = part if total is None else total + part
        dnorm[(x + 4 - k) % 4] = total.astype(BF16)

    def unnorm_rows(r, _):
        rows = pl.ds(pl.multiple_of(r * CHUNK, CHUNK), CHUNK)
        dn = jnp.concatenate([dnorm[j, rows, :] for j in range(4)], axis=1).astype(F32)
        hat = jnp.concatenate([nrm[j, rows, :] for j in range(4)], axis=1).astype(F32)
        m1 = jnp.sum(dn, axis=1, keepdims=True) * (1.0 / 1024)
        m2 = jnp.sum(dn * hat, axis=1, keepdims=True) * (1.0 / 1024)
        d = rstd[rows, :1] * (dn - m1 - hat * m2) + cot[rows, :].astype(F32)
        downed[rows, :] = d.astype(BF16)
        return 0

    lax.fori_loop(0, 256 // CHUNK, unnorm_rows, 0)
    t = iota((1024, 256), 1)
    wanted = (t & 63) * 16 + (t >> 6) * 4
    row = iota((1024, 256), 0)
    total = None
    for j in range(4):
        pick = (row == wanted + j).astype(F32).astype(BF16)
        part = dot(pick, downed[:, j * 256 : (j + 1) * 256])
        total = part if total is None else total + part
    outgoing[...] = total.astype(BF16)


def add_pair_body(own, other, *outs):
    for color in range(2):
        for s in range(4):
            both = own[color, s].astype(F32) + other[color, s].astype(F32)
            outs[color * 4 + s][...] = both.astype(BF16)


def add_four_body(a0, a1, a2, a3, b0, b1, b2, b3, *outs):
    for color, refs in enumerate(((a0, a1, a2, a3), (b0, b1, b2, b3))):
        for s in range(4):
            total = refs[0][s].astype(F32)
            for ref in refs[1:]:
                total = total + ref[s].astype(F32)
            outs[color * 4 + s][...] = total.astype(BF16)


def add_last_body(a0, a1, a2, a3, b0, b1, b2, b3, out):
    for color, refs in enumerate(((a0, a1, a2, a3), (b0, b1, b2, b3))):
        total = refs[0][...].astype(F32)
        for ref in refs[1:]:
            total = total + ref[...].astype(F32)
        total = total.astype(BF16)
        for j in range(4):
            out[color * 4 + j] = total[:, j * 128 : (j + 1) * 128]


def add_eight_body(parts, out):
    total = parts[0].astype(F32)
    for i in range(1, 8):
        total = total + parts[i].astype(F32)
    total = total.astype(BF16)
    for i in range(8):
        out[i] = total


def place_body(o0, o1, o2, o3, t0, t1, t2, t3, g_in, g_out, rows):
    y, c = lax.axis_index("y"), lax.axis_index("c")
    for refs, h in (((o0, o1, o2, o3), c), ((t0, t1, t2, t3), 1 - c)):
        for s in range(4):
            m = (y + 4 - s) % 4
            for j in range(8):
                rows[h, m, :, j * 128 : (j + 1) * 128] = refs[s][j]
    factor = 1.0 / 256.0
    for h in range(2):
        for m in range(3):
            g_in[80 * m : 80 * m + 80, h * 1024 : (h + 1) * 1024] = rows[h, m].astype(F32) * factor
        last = rows[h, 3].astype(F32) * factor
        g_in[240:, h * 1024 : (h + 1) * 1024] = last[:16]
        g_out[:64, h * 512 : (h + 1) * 512] = last[16:, :512]
        g_out[64:, h * 512 : (h + 1) * 512] = last[16:, 512:]


def shift(a, axis, n, s):
    return lax.ppermute(a, axis, [(i, (i + s) % n) for i in range(n)])


def on_device(x_rows, cotangent, w_in, w_out, hist_blocks, owner):
    cot = cotangent[0]
    outgoing, pack = call(
        prep_body,
        [((1024, 256), BF16), ((320, 1024), BF16)],
        (hist_blocks, owner, x_rows[0], w_in, w_out),
        "route_out",
    )
    own = [shift(pack, "x", 4, s) for s in (1, 2, 3)]
    other = [shift(a, "c", 2, 1) for a in own]
    arrived = lax.all_to_all(
        outgoing.reshape(64, 16, 256), DP, split_axis=0, concat_axis=0, tiled=True
    ).reshape(1024, 256)
    weights = (w_in, w_out, own[0], other[0], own[1], other[1], own[2], other[2])
    layer_out, gother, nrm, dpre, mix, rstd = call(
        layer_body,
        [
            ((256, 1024), BF16),
            ((2, 4, 4, 80, 512), BF16),
            ((4, 256, 256), BF16),
            ((2, 256, 1024), BF16),
            ((4, 256, 128), BF16),
            ((256, 128), F32),
        ],
        (hist_blocks, owner, arrived, cot) + weights,
        "layer",
        scratch=[
            ((256, 1024), F32),
            ((2, 256, 1024), F32),
            ((2, 256, 1024), BF16),
            ((256, 512), F32),
            ((256, 128), F32),
            ((4, 256, 256), BF16),
            ((4, 256, 256), F32),
            ((4, 256, 128), BF16),
            ((256, 512), BF16),
        ],
    )
    gfrom = shift(gother, "c", 2, 1)
    gown, backward = call(
        rest_body,
        [((2, 4, 4, 80, 512), BF16), ((1024, 256), BF16)],
        (nrm, dpre, mix, rstd, cot) + weights,
        "rest",
        scratch=[((4, 256, 256), BF16), ((256, 1024), BF16)],
    )
    big = call(add_pair_body, [((4, 80, 512), BF16)] * 8, (gown, gfrom), "add_pair")
    first = [big[0]] + [shift(big[s], "x", 4, s) for s in (1, 2, 3)]
    second = [big[4]] + [shift(big[4 + s], "y", 4, s) for s in (1, 2, 3)]
    returned = lax.all_to_all(
        backward.reshape(64, 16, 256), DP, split_axis=0, concat_axis=0, tiled=True
    ).reshape(1024, 256)
    (grad_rows,) = call(
        rows_back_body, [((128, 1024), BF16)], (hist_blocks, owner, returned), "route_back"
    )
    mid = call(add_four_body, [((80, 512), BF16)] * 8, (*first, *second), "add_four")
    first = [mid[0]] + [shift(mid[s], "y", 4, s) for s in (1, 2, 3)]
    second = [mid[4]] + [shift(mid[4 + s], "x", 4, s) for s in (1, 2, 3)]
    (columns,) = call(add_last_body, [((8, 80, 128), BF16)], (*first, *second), "add_last")
    parts = lax.all_to_all(columns, "z", split_axis=0, concat_axis=0, tiled=True)
    (summed,) = call(add_eight_body, [((8, 80, 128), BF16)], (parts,), "add_eight")
    mine = lax.all_to_all(summed, "z", split_axis=0, concat_axis=0, tiled=True)
    lines = [mine] + [shift(mine, "y", 4, s) for s in (1, 2, 3)]
    paired = [shift(a, "c", 2, 1) for a in lines]
    g_in, g_out = call(
        place_body,
        [((256, 2048), F32), ((128, 1024), F32)],
        (*lines, *paired),
        "place",
        scratch=[((2, 4, 80, 1024), BF16)],
    )
    return layer_out[None], grad_rows[None], g_in, g_out


def solution(mesh):
    fine = Mesh(mesh.devices.reshape(8, 4, 2, 4), ("z", "y", "c", "x"))
    placed = (
        P("x", DP, None),
        P("x", DP, None),
        P("x", None),
        P("x", None),
        P("x", None),
        P("x", None),
    )
    return jax.shard_map(
        on_device,
        mesh=fine,
        in_specs=placed,
        out_specs=(P("x", DP, None), P("x", DP, None), P("x", None), P("x", None)),
        check_vma=False,
    )
```

time: 472 us -> 178 us (0.38)
  blocking collectives: 273 us -> 28.2 us
  waiting for transfers between devices: 97.2 us -> 33.7 us
  Pallas kernels: 0 us -> 42.9 us
  starting transfers between devices: 25.3 us -> 66.6 us
  matrix products: 33.4 us -> 0 us
  between operations: 14.5 us -> 0.87 us
  other arithmetic: 11.4 us -> 0 us
  local copies, waits for them, and re-layouts: 13.7 us -> 5.21 us
    psum x1 -> x0, blocking collectives: 273 us -> none  [on_device(): summed_in, summed_out = lax.psum((shard_in, shard_out), 'dp')]
    ppermute x0 -> x26, starting transfers between devices: none -> 43.7 us  [shift(): return lax.ppermute(a, axis, [(i, (i + s) % n) for i in range(n)])]
    pallas_call x0 -> x9, Pallas kernels: none -> 42.9 us  [call(): pl.pallas_call(body, out_shape=[jax.ShapeDtypeStruct(s, d) for s, d in ou...]
    ppermute x0 -> x26, waiting for transfers between devices: none -> 33.7 us  [shift(): return lax.ppermute(a, axis, [(i, (i + s) % n) for i in range(n)])]
    dot_general x30 -> x0, matrix products: 33.4 us -> none  [the longest x3 13 us: layer_rows(): jnp.dot(normed, w_in, preferred_element_type=jnp.float32)]
    all_gather x2 -> x0, waiting for transfers between devices: 32.5 us -> none  [the longest x1 19.4 us: on_device(): lax.all_gather(w_out, 'fsdp', axis=0, tiled=True)]
    all_to_all x2, waiting for transfers between devices: 31.8 us -> 0.01 us  [the longest x1 0.01 us: on_device(): lax.all_to_all(outgoing.reshape(64, 16, 256), DP, split_axis=0, concat_ax...]
    reduce_scatter x2 -> x0, waiting for transfers between devices: 31.5 us -> none  [the longest x1 31.5 us: on_device(): lax.psum_scatter(term_in.astype(jnp.bfloat16), 'fsdp', scatter_dimension=...]
  transfers between devices with their start and end apart: 6 -> 28, of which waited for: 5 -> 10; matrix products, arithmetic and copies ran while one was open for 8% -> 0% of each run, Pallas kernels for 0% -> 6%
where the time goes in v1:
time: 178 us; the launch traced here: 177 us
  starting transfers between devices  66.6 us (37%)
  Pallas kernels  42.9 us (24%)
  waiting for transfers between devices  33.7 us (19%)
  blocking collectives  28.2 us (16%)
  local copies, waits for them, and re-layouts  5.21 us (3%)
    ppermute x26, starting transfers between devices, shift(): return lax.ppermute(a, axis, [(i, (i + s) % n) for i in range(n)])  43.7 us
    pallas_call x9, Pallas kernels, call(): pl.pallas_call(body, out_shape=[jax.ShapeDtypeStruct(s, d) for s, d in ou...  42.9 us
    ppermute x26, waiting for transfers between devices, shift(): return lax.ppermute(a, axis, [(i, (i + s) % n) for i in range(n)])  33.7 us
    all_to_all x1, blocking collectives, on_device(): lax.all_to_all(columns, 'z', split_axis=0, concat_axis=0, tiled=True)  16.7 us
    all_to_all x1, starting transfers between devices, on_device(): lax.all_to_all(outgoing.reshape(64, 16, 256), DP, split_axis=0, concat_ax...  13.4 us
    all_to_all x1, blocking collectives, on_device(): mine = lax.all_to_all(summed, 'z', split_axis=0, concat_axis=0, tiled=True)  11.6 us
    all_to_all x1, starting transfers between devices, on_device(): lax.all_to_all(backward.reshape(64, 16, 256), DP, split_axis=0, concat_ax...  9.48 us
    unnamed x54, local copies, waits for them, and re-layouts  5.21 us
  transfers between devices with their start and end apart: 28, of which 10 were waited for; matrix products, arithmetic and copies ran while one was open for 0% of the time, Pallas kernels for 6%

profile of v1, /device:TPU:1, one launch (start us, length us, event | category | flops | bytes accessed | tf_op | source)
XLA Modules:
  0.0 177.5 jit_solution(7596514367163201905)
XLA Ops:
  0.6 3.2 %route_out.1 = (bf16[1024,256]{1,0:T(8,128)(2,1)}, bf16[320,1024]{1,0:T(8,128)(2,1)}) custom-call(s32[1,64]{1,0:T(1,128)} %blocks_ref.5, s32[1,64]{1,0:T(1,128)} %owners_ref.5, bf16[128,1024]{1,0:T(8,128)(2,1)} %bitcast.13, bf16[256,2048]{1,0:T(8,128)(2,1)} %w_in.3, bf16[128,1024]{1,0:T(8,128)(2,1)} %w_out.3), custom_call_target="tpu_custom_call" | custom-call | tf_op jit(solution)/shard_map/route_out/pallas_call | solution.py:30
  3.9 3.3 %collective-permute-start.4 = (bf16[320,1024]{1,0:T(8,128)(2,1)}, bf16[320,1024]{1,0:T(8,128)(2,1)S(1)}, u32[]{:S(2)}, u32[]{:S(2)}) collective-permute-start(bf16[320,1024]{1,0:T(8,128)(2,1)} %get-tuple-element.33), channel_id=1, source_target_pairs={{0,3},{1,0},{2,1},{3,2},{4,7},{5,4},{6,5},{7,6},{8,11},{9,8},{10,9... | collective-permute-start | bytes 1966088 | tf_op jit(solution)/shard_map/ppermute | solution.py:349
  8.3 13.4 %all-to-all-start = ((bf16[64,16,256]{2,1,0:T(8,128)(2,1)}), bf16[64,16,256]{2,1,0:T(8,128)(2,1)}, u32[]{:S(2)}, u32[]{:S(2)}) async-start(bf16[64,16,256]{2,1,0:T(8,128)(2,1)} %bitcast.11), calls=%async_computation | async-start | bytes 1048576 | tf_op jit(solution)/shard_map/all_to_all | solution.py:362
  21.7 2.3 %collective-permute-done.4.a3 = bf16[320,1024]{1,0:T(8,128)(2,1)S(1)} collective-permute-done((bf16[320,1024]{1,0:T(8,128)(2,1)}, bf16[320,1024]{1,0:T(8,128)(2,1)S(1)}, u32[]{:S(2)}, u32[]{:S(2)}) %collective-permute-start.4) | collective-permute-done | bytes 655392 | tf_op jit(solution)/shard_map/ppermute | solution.py:349
  23.9 12.5 %collective-permute-start.5 = (bf16[320,1024]{1,0:T(8,128)(2,1)S(1)}, bf16[320,1024]{1,0:T(8,128)(2,1)S(1)}, u32[]{:S(2)}, u32[]{:S(2)}) collective-permute-start(bf16[320,1024]{1,0:T(8,128)(2,1)S(1)} %collective-permute-done.4.a3), channel_id=1, source_target_pairs={{0,4},{4,0},{1,5},{5,1},{2,6},{6,2},{3,7},{7,3},{8,12},{12,8},{9,1... | collective-permute-start | bytes 1966088 | tf_op jit(solution)/shard_map/ppermute | solution.py:349
  36.6 3.0 %collective-permute-done.a1 = bf16[320,1024]{1,0:T(8,128)(2,1)S(1)} collective-permute-done((bf16[320,1024]{1,0:T(8,128)(2,1)}, bf16[320,1024]{1,0:T(8,128)(2,1)S(1)}, u32[]{:S(2)}, u32[]{:S(2)}) %collective-permute-start) | collective-permute-done | bytes 655392 | tf_op jit(solution)/shard_map/ppermute | solution.py:349
  40.1 1.8 %collective-permute-done.1.b1 = bf16[320,1024]{1,0:T(8,128)(2,1)} collective-permute-done((bf16[320,1024]{1,0:T(8,128)(2,1)S(1)}, bf16[320,1024]{1,0:T(8,128)(2,1)}, u32[]{:S(2)}, u32[]{:S(2)}) %collective-permute-start.1) | collective-permute-done | bytes 655392 | tf_op jit(solution)/shard_map/ppermute | solution.py:349
  42.0 15.7 %layer.1 = (bf16[256,1024]{1,0:T(8,128)(2,1)}, bf16[2,4,4,80,512]{4,3,2,1,0:T(8,128)(2,1)}, bf16[4,256,256]{2,1,0:T(8,128)(2,1)}, bf16[2,256,1024]{2,1,0:T(8,128...) custom-call(s32[1,64]{1,0:T(1,128)} %blocks_ref.5, s32[1,64]{1,0:T(1,128)} %owners_ref.5, ...), custom_call_target="tpu_custom_call" | custom-call | tf_op jit(solution)/shard_map/layer/pallas_call | solution.py:30
  58.0 7.8 %rest.1 = (bf16[2,4,4,80,512]{4,3,2,1,0:T(8,128)(2,1)}, bf16[1024,256]{1,0:T(8,128)(2,1)}) custom-call(bf16[4,256,256]{2,1,0:T(8,128)(2,1)} %get-tuple-element.35.nrm, bf16[2,256,1024]{2,1,0:T(8,128)(2,1)} %get-tuple-element.36.dpre, bf16[4,256,128]{2,1,0:T(8,128)(2,1)} %get-tuple-element.37.mix, f32[256,128]{1,0:T(8,128)} %get-tuple-element.38.rstd, ...), custom_call_target="tpu_custom_call" | custom-call | tf_op jit(solution)/shard_map/rest/pallas_call | solution.py:30
  65.9 1.5 copy-done
  67.4 4.1 %add_pair.1 = (bf16[4,80,512]{2,1,0:T(8,128)(2,1)}, bf16[4,80,512]{2,1,0:T(8,128)(2,1)}, bf16[4,80,512]{2,1,0:T(8,128)(2,1)}, bf16[4,80,512]{2,1,0:T(8,128)(2,1)...) custom-call(bf16[2,4,4,80,512]{4,3,2,1,0:T(8,128)(2,1)} %get-tuple-e, ...), custom_call_target="tpu_custom_call" | custom-call | tf_op jit(solution)/shard_map/add_pair/pallas_call | solution.py:30
  71.5 3.5 %collective-permute-start.8 = (bf16[4,80,512]{2,1,0:T(8,128)(2,1)}, bf16[4,80,512]{2,1,0:T(8,128)(2,1)S(1)}, u32[]{:S(2)}, u32[]{:S(2)}) collective-permute-start(bf16[4,80,512]{2,1,0:T(8,128)(2,1)} %get-tuple-element.44), channel_id=1, source_target_pairs={{0,2},{1,3},{2,0},{3,1},{4,6},{5,7},{6,4},{7,5},{8,10},{9,11},{10,... | collective-permute-start | bytes 983048 | tf_op jit(solution)/shard_map/ppermute | solution.py:349
  76.3 2.6 %collective-permute-start.11 = (bf16[4,80,512]{2,1,0:T(8,128)(2,1)}, bf16[4,80,512]{2,1,0:T(8,128)(2,1)S(1)}, u32[]{:S(2)}, u32[]{:S(2)}) collective-permute-start(bf16[4,80,512]{2,1,0:T(8,128)(2,1)} %get-tuple-element.48), channel_id=1, source_target_pairs={{0,16},{8,24},{16,0},{24,8},{1,17},{9,25},{17,1},{25,9},{2,18},{10... | collective-permute-start | bytes 983048 | tf_op jit(solution)/shard_map/ppermute | solution.py:349
  78.9 3.3 %collective-permute-done.7.a1 = bf16[4,80,512]{2,1,0:T(8,128)(2,1)S(1)} collective-permute-done((bf16[4,80,512]{2,1,0:T(8,128)(2,1)}, bf16[4,80,512]{2,1,0:T(8,128)(2,1)S(1)}, u32[]{:S(2)}, u32[]{:S(2)}) %collective-permute-start.7) | collective-permute-done | bytes 327712 | tf_op jit(solution)/shard_map/ppermute | solution.py:349
  82.2 2.7 %collective-permute-start.12 = (bf16[4,80,512]{2,1,0:T(8,128)(2,1)}, bf16[4,80,512]{2,1,0:T(8,128)(2,1)S(1)}, u32[]{:S(2)}, u32[]{:S(2)}) collective-permute-start(bf16[4,80,512]{2,1,0:T(8,128)(2,1)} %get-tuple-element.49), channel_id=1, source_target_pairs={{0,24},{8,0},{16,8},{24,16},{1,25},{9,1},{17,9},{25,17},{2,26},{10... | collective-permute-start | bytes 983048 | tf_op jit(solution)/shard_map/ppermute | solution.py:349
  84.9 5.1 %collective-permute-done.8.a2 = bf16[4,80,512]{2,1,0:T(8,128)(2,1)S(1)} collective-permute-done((bf16[4,80,512]{2,1,0:T(8,128)(2,1)}, bf16[4,80,512]{2,1,0:T(8,128)(2,1)S(1)}, u32[]{:S(2)}, u32[]{:S(2)}) %collective-permute-start.8) | collective-permute-done | bytes 327712 | tf_op jit(solution)/shard_map/ppermute | solution.py:349
  90.0 3.3 %collective-permute-done.11.b2 = bf16[4,80,512]{2,1,0:T(8,128)(2,1)S(1)} collective-permute-done((bf16[4,80,512]{2,1,0:T(8,128)(2,1)}, bf16[4,80,512]{2,1,0:T(8,128)(2,1)S(1)}, u32[]{:S(2)}, u32[]{:S(2)}) %collective-permute-start.11) | collective-permute-done | bytes 327712 | tf_op jit(solution)/shard_map/ppermute | solution.py:349
  94.1 2.6 %add_four.1 = (bf16[80,512]{1,0:T(8,128)(2,1)}, bf16[80,512]{1,0:T(8,128)(2,1)}, bf16[80,512]{1,0:T(8,128)(2,1)}, bf16[80,512]{1,0:T(8,128)(2,1)}, bf16[80,512]{...) custom-call(bf16[4,80,512]{2,1,0:T(8,128)(2,1)} %get-tuple-element.42.a0, ...), custom_call_target="tpu_custom_call" | custom-call | tf_op jit(solution)/shard_map/add_four/pallas_call | solution.py:30
  96.8 2.5 %collective-permute-start.13 = (bf16[80,512]{1,0:T(8,128)(2,1)}, bf16[80,512]{1,0:T(8,128)(2,1)S(1)}, u32[]{:S(2)}, u32[]{:S(2)}) collective-permute-start(bf16[80,512]{1,0:T(8,128)(2,1)} %get-tuple-element.51), channel_id=1, source_target_pairs={{0,8},{8,16},{16,24},{24,0},{1,9},{9,17},{17,25},{25,1},{2,10},{10... | collective-permute-start | bytes 245768 | tf_op jit(solution)/shard_map/ppermute | solution.py:349
  101.8 1.5 collective-permute-start.16
  103.3 2.3 %collective-permute-start.18 = (bf16[80,512]{1,0:T(8,128)(2,1)}, bf16[80,512]{1,0:T(8,128)(2,1)S(1)}, u32[]{:S(2)}, u32[]{:S(2)}) collective-permute-start(bf16[80,512]{1,0:T(8,128)(2,1)} %get-tuple-element.57), channel_id=1, source_target_pairs={{0,3},{1,0},{2,1},{3,2},{4,7},{5,4},{6,5},{7,6},{8,11},{9,8},{10,9... | collective-permute-start | bytes 245768 | tf_op jit(solution)/shard_map/ppermute | solution.py:349
  106.5 1.8 %collective-permute-done.17.b2 = bf16[80,512]{1,0:T(8,128)(2,1)S(1)} collective-permute-done((bf16[80,512]{1,0:T(8,128)(2,1)}, bf16[80,512]{1,0:T(8,128)(2,1)S(1)}, u32[]{:S(2)}, u32[]{:S(2)}) %collective-permute-start.17) | collective-permute-done | bytes 81952 | tf_op jit(solution)/shard_map/ppermute | solution.py:349
  109.0 1.9 %add_last.1 = bf16[8,80,128]{2,1,0:T(8,128)(2,1)} custom-call(bf16[80,512]{1,0:T(8,128)(2,1)} %get-tuple-element.50.a0, bf16[80,512]{1,0:T(8,128)(2,1)} %copy-done.21, bf16[80,512]{1,0:T(8,128)(2,1)} %copy-done.22, bf16[80,512]{1,0:T(8,128)(2,1)} %copy-done.23, bf16[80,512]{1,0:T(8,128)(2,1)} %get-tuple-element.54.b0, bf16[80,512]{1,0:T(8,128)(2,1)} %copy-done.24, ...), custom_call_target="tpu_custom_call" | custom-call | tf_op jit(solution)/shard_map/add_last/pallas_call | solution.py:30
  110.9 16.7 %all_to_all.20.parts = bf16[8,80,128]{2,1,0:T(8,128)(2,1)} all-to-all(bf16[8,80,128]{2,1,0:T(8,128)(2,1)} %add_last.1), channel_id=1, replica_groups=mesh['z'=8,'y'=4,'c'=2,'x'=4] {'z'}, dimensions={0} | all-to-all | bytes 327680 | tf_op jit(solution)/shard_map/all_to_all | solution.py:411
  127.6 1.6 add_eight.1
  129.2 11.6 %all_to_all.21.o0 = bf16[8,80,128]{2,1,0:T(8,128)(2,1)S(1)} all-to-all(bf16[8,80,128]{2,1,0:T(8,128)(2,1)} %add_eight.1), channel_id=1, replica_groups=mesh['z'=8,'y'=4,'c'=2,'x'=4] {'z'}, dimensions={0} | all-to-all | bytes 327680 | tf_op jit(solution)/shard_map/all_to_all | solution.py:413
  140.8 9.5 %all-to-all-start.1 = ((bf16[64,16,256]{2,1,0:T(8,128)(2,1)}), bf16[64,16,256]{2,1,0:T(8,128)(2,1)S(1)}, u32[]{:S(2)}, u32[]{:S(2)}) async-start(bf16[64,16,256]{2,1,0:T(8,128)(2,1)} %bitcast.5), calls=%async_computation.1 | async-start | bytes 1048576 | tf_op jit(solution)/shard_map/all_to_all | solution.py:401
  150.2 2.7 %collective-permute-start.21 = (bf16[8,80,128]{2,1,0:T(8,128)(2,1)S(1)}, bf16[8,80,128]{2,1,0:T(8,128)(2,1)S(1)}, u32[]{:S(2)}, u32[]{:S(2)}) collective-permute-start(bf16[8,80,128]{2,1,0:T(8,128)(2,1)S(1)} %all_to_all.21.o0), channel_id=1, source_target_pairs={{0,24},{8,0},{16,8},{24,16},{1,25},{9,1},{17,9},{25,17},{2,26},{10... | collective-permute-start | bytes 491528 | tf_op jit(solution)/shard_map/ppermute | solution.py:349
  155.3 9.3 %collective-permute-done.21.o3 = bf16[8,80,128]{2,1,0:T(8,128)(2,1)S(1)} collective-permute-done((bf16[8,80,128]{2,1,0:T(8,128)(2,1)S(1)}, bf16[8,80,128]{2,1,0:T(8,128)(2,1)S(1)}, u32[]{:S(2)}, u32[]{:S(2)}) %collective-permute-start.21) | collective-permute-done | bytes 163872 | tf_op jit(solution)/shard_map/ppermute | solution.py:349
  165.8 3.0 %collective-permute-done.19.o1 = bf16[8,80,128]{2,1,0:T(8,128)(2,1)S(1)} collective-permute-done((bf16[8,80,128]{2,1,0:T(8,128)(2,1)S(1)}, bf16[8,80,128]{2,1,0:T(8,128)(2,1)S(1)}, u32[]{:S(2)}, u32[]{:S(2)}) %collective-permute-start.19) | collective-permute-done | bytes 163872 | tf_op jit(solution)/shard_map/ppermute | solution.py:349
  170.0 2.6 %route_back.1 = bf16[128,1024]{1,0:T(8,128)(2,1)} custom-call(s32[1,64]{1,0:T(1,128)} %blocks_ref.5, s32[1,64]{1,0:T(1,128)} %owners_ref.5, bf16[1024,256]{1,0:T(8,128)(2,1)} %bitcast.8), custom_call_target="tpu_custom_call" | custom-call | tf_op jit(solution)/shard_map/route_back/pallas_call | solution.py:30
  174.1 3.4 %place.1 = (f32[256,2048]{1,0:T(8,128)}, f32[128,1024]{1,0:T(8,128)}) custom-call(bf16[8,80,128]{2,1,0:T(8,128)(2,1)} %copy-done.7, bf16[8,80,128]{2,1,0:T(8,128)(2,1)} %copy-done.16, bf16[8,80,128]{2,1,0:T(8,128)(2,1)} %copy-done.15, bf16[8,80,128]{2,1,0:T(8,128)(2,1)} %copy-done.14, bf16[8,80,128]{2,1,0:T(8,128)(2,1)} %copy-done.17, ...), custom_call_target="tpu_custom_call" | custom-call | tf_op jit(solution)/shard_map/place/pallas_call | solution.py:30
  (89 shorter events, 14.6 us)
Async XLA Ops:
  3.9 20.1 %collective-permute-start.4 = (bf16[320,1024]{1,0:T(8,128)(2,1)}, bf16[320,1024]{1,0:T(8,128)(2,1)S(1)}, u32[]{:S(2)}, u32[]{:S(2)}) collective-permute-start(bf16[320,1024]{1,0:T(8,128)(2,1)} %get-tuple-element.33), channel_id=1, source_target_pairs={{0,3},{1,0},{2,1},{3,2},{4,7},{5,4},{6,5},{7,6},{8,11},{9,8},{10,9... | collective-permute-start | bytes 1966088 | tf_op jit(solution)/shard_map/ppermute | solution.py:349
  7.2 29.3 %collective-permute-start.2 = (bf16[320,1024]{1,0:T(8,128)(2,1)}, bf16[320,1024]{1,0:T(8,128)(2,1)S(1)}, u32[]{:S(2)}, u32[]{:S(2)}) collective-permute-start(bf16[320,1024]{1,0:T(8,128)(2,1)} %get-tuple-element.33), channel_id=1, source_target_pairs={{0,2},{1,3},{2,0},{3,1},{4,6},{5,7},{6,4},{7,5},{8,10},{9,11},{10,... | collective-permute-start | bytes 1966088 | tf_op jit(solution)/shard_map/ppermute | solution.py:349
  7.7 31.9 %collective-permute-start = (bf16[320,1024]{1,0:T(8,128)(2,1)}, bf16[320,1024]{1,0:T(8,128)(2,1)S(1)}, u32[]{:S(2)}, u32[]{:S(2)}) collective-permute-start(bf16[320,1024]{1,0:T(8,128)(2,1)} %get-tuple-element.33), channel_id=1, source_target_pairs={{0,1},{1,2},{2,3},{3,0},{4,5},{5,6},{6,7},{7,4},{8,9},{9,10},{10,1... | collective-permute-start | bytes 1966088 | tf_op jit(solution)/shard_map/ppermute | solution.py:349
  8.3 31.8 %all-to-all-start = ((bf16[64,16,256]{2,1,0:T(8,128)(2,1)}), bf16[64,16,256]{2,1,0:T(8,128)(2,1)}, u32[]{:S(2)}, u32[]{:S(2)}) async-start(bf16[64,16,256]{2,1,0:T(8,128)(2,1)} %bitcast.11), calls=%async_computation | async-start | bytes 1048576 | tf_op jit(solution)/shard_map/all_to_all | solution.py:362
  23.9 18.0 %copy-start.1 = (bf16[320,1024]{1,0:T(8,128)(2,1)}, bf16[320,1024]{1,0:T(8,128)(2,1)S(1)}, u32[]{:S(2)}) copy-start(bf16[320,1024]{1,0:T(8,128)(2,1)S(1)} %collective-permute-done.4.a3) | copy-start | bytes 1966084
  23.9 16.1 %collective-permute-start.5 = (bf16[320,1024]{1,0:T(8,128)(2,1)S(1)}, bf16[320,1024]{1,0:T(8,128)(2,1)S(1)}, u32[]{:S(2)}, u32[]{:S(2)}) collective-permute-start(bf16[320,1024]{1,0:T(8,128)(2,1)S(1)} %collective-permute-done.4.a3), channel_id=1, source_target_pairs={{0,4},{4,0},{1,5},{5,1},{2,6},{6,2},{3,7},{7,3},{8,12},{12,8},{9,1... | collective-permute-start | bytes 1966088 | tf_op jit(solution)/shard_map/ppermute | solution.py:349
  36.5 3.6 %collective-permute-start.3 = (bf16[320,1024]{1,0:T(8,128)(2,1)S(1)}, bf16[320,1024]{1,0:T(8,128)(2,1)S(1)}, u32[]{:S(2)}, u32[]{:S(2)}) collective-permute-start(bf16[320,1024]{1,0:T(8,128)(2,1)S(1)} %collective-permute-done.2.a2), channel_id=1, source_target_pairs={{0,4},{4,0},{1,5},{5,1},{2,6},{6,2},{3,7},{7,3},{8,12},{12,8},{9,1... | collective-permute-start | bytes 1966088 | tf_op jit(solution)/shard_map/ppermute | solution.py:349
  39.6 2.4 %collective-permute-start.1 = (bf16[320,1024]{1,0:T(8,128)(2,1)S(1)}, bf16[320,1024]{1,0:T(8,128)(2,1)}, u32[]{:S(2)}, u32[]{:S(2)}) collective-permute-start(bf16[320,1024]{1,0:T(8,128)(2,1)S(1)} %collective-permute-done.a1), channel_id=1, source_target_pairs={{0,4},{4,0},{1,5},{5,1},{2,6},{6,2},{3,7},{7,3},{8,12},{12,8},{9,1... | collective-permute-start | bytes 1966088 | tf_op jit(solution)/shard_map/ppermute | solution.py:349
  57.6 8.3 %collective-permute-start.6 = (bf16[2,4,4,80,512]{4,3,2,1,0:T(8,128)(2,1)}, bf16[2,4,4,80,512]{4,3,2,1,0:T(8,128)(2,1)S(1)}, u32[]{:S(2)}, u32[]{:S(2)}) collective-permute-start(bf16[2,4,4,80,512]{4,3,2,1,0:T(8,128)(2,1)} %get-tuple-element.41), channel_id=1, source_target_pairs={{0,4},{4,0},{1,5},{5,1},{2,6},{6,2},{3,7},{7,3},{8,12},{12,8},{9,1... | collective-permute-start | bytes 7864328 | tf_op jit(solution)/shard_map/ppermute | solution.py:349
  71.5 10.7 %collective-permute-start.7 = (bf16[4,80,512]{2,1,0:T(8,128)(2,1)}, bf16[4,80,512]{2,1,0:T(8,128)(2,1)S(1)}, u32[]{:S(2)}, u32[]{:S(2)}) collective-permute-start(bf16[4,80,512]{2,1,0:T(8,128)(2,1)} %get-tuple-element.43), channel_id=1, source_target_pairs={{0,1},{1,2},{2,3},{3,0},{4,5},{5,6},{6,7},{7,4},{8,9},{9,10},{10,1... | collective-permute-start | bytes 983048 | tf_op jit(solution)/shard_map/ppermute | solution.py:349
  71.5 18.5 %collective-permute-start.8 = (bf16[4,80,512]{2,1,0:T(8,128)(2,1)}, bf16[4,80,512]{2,1,0:T(8,128)(2,1)S(1)}, u32[]{:S(2)}, u32[]{:S(2)}) collective-permute-start(bf16[4,80,512]{2,1,0:T(8,128)(2,1)} %get-tuple-element.44), channel_id=1, source_target_pairs={{0,2},{1,3},{2,0},{3,1},{4,6},{5,7},{6,4},{7,5},{8,10},{9,11},{10,... | collective-permute-start | bytes 983048 | tf_op jit(solution)/shard_map/ppermute | solution.py:349
  75.0 15.0 %collective-permute-start.9 = (bf16[4,80,512]{2,1,0:T(8,128)(2,1)}, bf16[4,80,512]{2,1,0:T(8,128)(2,1)S(1)}, u32[]{:S(2)}, u32[]{:S(2)}) collective-permute-start(bf16[4,80,512]{2,1,0:T(8,128)(2,1)} %get-tuple-element.45), channel_id=1, source_target_pairs={{0,3},{1,0},{2,1},{3,2},{4,7},{5,4},{6,5},{7,6},{8,11},{9,8},{10,9... | collective-permute-start | bytes 983048 | tf_op jit(solution)/shard_map/ppermute | solution.py:349
  75.0 15.0 %collective-permute-start.10 = (bf16[4,80,512]{2,1,0:T(8,128)(2,1)}, bf16[4,80,512]{2,1,0:T(8,128)(2,1)S(1)}, u32[]{:S(2)}, u32[]{:S(2)}) collective-permute-start(bf16[4,80,512]{2,1,0:T(8,128)(2,1)} %get-tuple-element.47), channel_id=1, source_target_pairs={{0,8},{8,16},{16,24},{24,0},{1,9},{9,17},{17,25},{25,1},{2,10},{10... | collective-permute-start | bytes 983048 | tf_op jit(solution)/shard_map/ppermute | solution.py:349
  76.3 17.0 %collective-permute-start.11 = (bf16[4,80,512]{2,1,0:T(8,128)(2,1)}, bf16[4,80,512]{2,1,0:T(8,128)(2,1)S(1)}, u32[]{:S(2)}, u32[]{:S(2)}) collective-permute-start(bf16[4,80,512]{2,1,0:T(8,128)(2,1)} %get-tuple-element.48), channel_id=1, source_target_pairs={{0,16},{8,24},{16,0},{24,8},{1,17},{9,25},{17,1},{25,9},{2,18},{10... | collective-permute-start | bytes 983048 | tf_op jit(solution)/shard_map/ppermute | solution.py:349
  82.2 11.1 %copy-start.8 = (bf16[4,80,512]{2,1,0:T(8,128)(2,1)}, bf16[4,80,512]{2,1,0:T(8,128)(2,1)S(1)}, u32[]{:S(2)}) copy-start(bf16[4,80,512]{2,1,0:T(8,128)(2,1)S(1)} %collective-permute-done.7.a1) | copy-start | bytes 983044
  82.2 11.1 %collective-permute-start.12 = (bf16[4,80,512]{2,1,0:T(8,128)(2,1)}, bf16[4,80,512]{2,1,0:T(8,128)(2,1)S(1)}, u32[]{:S(2)}, u32[]{:S(2)}) collective-permute-start(bf16[4,80,512]{2,1,0:T(8,128)(2,1)} %get-tuple-element.49), channel_id=1, source_target_pairs={{0,24},{8,0},{16,8},{24,16},{1,25},{9,1},{17,9},{25,17},{2,26},{10... | collective-permute-start | bytes 983048 | tf_op jit(solution)/shard_map/ppermute | solution.py:349
  96.8 6.6 %collective-permute-start.13 = (bf16[80,512]{1,0:T(8,128)(2,1)}, bf16[80,512]{1,0:T(8,128)(2,1)S(1)}, u32[]{:S(2)}, u32[]{:S(2)}) collective-permute-start(bf16[80,512]{1,0:T(8,128)(2,1)} %get-tuple-element.51), channel_id=1, source_target_pairs={{0,8},{8,16},{16,24},{24,0},{1,9},{9,17},{17,25},{25,1},{2,10},{10... | collective-permute-start | bytes 245768 | tf_op jit(solution)/shard_map/ppermute | solution.py:349
  99.3 6.3 %collective-permute-start.14 = (bf16[80,512]{1,0:T(8,128)(2,1)}, bf16[80,512]{1,0:T(8,128)(2,1)S(1)}, u32[]{:S(2)}, u32[]{:S(2)}) collective-permute-start(bf16[80,512]{1,0:T(8,128)(2,1)} %get-tuple-element.52), channel_id=1, source_target_pairs={{0,16},{8,24},{16,0},{24,8},{1,17},{9,25},{17,1},{25,9},{2,18},{10... | collective-permute-start | bytes 245768 | tf_op jit(solution)/shard_map/ppermute | solution.py:349
  100.6 5.0 %collective-permute-start.15 = (bf16[80,512]{1,0:T(8,128)(2,1)}, bf16[80,512]{1,0:T(8,128)(2,1)S(1)}, u32[]{:S(2)}, u32[]{:S(2)}) collective-permute-start(bf16[80,512]{1,0:T(8,128)(2,1)} %get-tuple-element.53), channel_id=1, source_target_pairs={{0,24},{8,0},{16,8},{24,16},{1,25},{9,1},{17,9},{25,17},{2,26},{10... | collective-permute-start | bytes 245768 | tf_op jit(solution)/shard_map/ppermute | solution.py:349
  101.8 4.7 %collective-permute-start.16 = (bf16[80,512]{1,0:T(8,128)(2,1)}, bf16[80,512]{1,0:T(8,128)(2,1)S(1)}, u32[]{:S(2)}, u32[]{:S(2)}) collective-permute-start(bf16[80,512]{1,0:T(8,128)(2,1)} %get-tuple-element.55), channel_id=1, source_target_pairs={{0,1},{1,2},{2,3},{3,0},{4,5},{5,6},{6,7},{7,4},{8,9},{9,10},{10,1... | collective-permute-start | bytes 245768 | tf_op jit(solution)/shard_map/ppermute | solution.py:349
  103.2 5.1 %collective-permute-start.17 = (bf16[80,512]{1,0:T(8,128)(2,1)}, bf16[80,512]{1,0:T(8,128)(2,1)S(1)}, u32[]{:S(2)}, u32[]{:S(2)}) collective-permute-start(bf16[80,512]{1,0:T(8,128)(2,1)} %get-tuple-element.56), channel_id=1, source_target_pairs={{0,2},{1,3},{2,0},{3,1},{4,6},{5,7},{6,4},{7,5},{8,10},{9,11},{10,... | collective-permute-start | bytes 245768 | tf_op jit(solution)/shard_map/ppermute | solution.py:349
  103.3 5.0 %collective-permute-start.18 = (bf16[80,512]{1,0:T(8,128)(2,1)}, bf16[80,512]{1,0:T(8,128)(2,1)S(1)}, u32[]{:S(2)}, u32[]{:S(2)}) collective-permute-start(bf16[80,512]{1,0:T(8,128)(2,1)} %get-tuple-element.57), channel_id=1, source_target_pairs={{0,3},{1,0},{2,1},{3,2},{4,7},{5,4},{6,5},{7,6},{8,11},{9,8},{10,9... | collective-permute-start | bytes 245768 | tf_op jit(solution)/shard_map/ppermute | solution.py:349
  140.8 31.9 %copy-start.7 = (bf16[8,80,128]{2,1,0:T(8,128)(2,1)}, bf16[8,80,128]{2,1,0:T(8,128)(2,1)S(1)}, u32[]{:S(2)}) copy-start(bf16[8,80,128]{2,1,0:T(8,128)(2,1)S(1)} %all_to_all.21.o0) | copy-start | bytes 491524
  140.8 28.5 %all-to-all-start.1 = ((bf16[64,16,256]{2,1,0:T(8,128)(2,1)}), bf16[64,16,256]{2,1,0:T(8,128)(2,1)S(1)}, u32[]{:S(2)}, u32[]{:S(2)}) async-start(bf16[64,16,256]{2,1,0:T(8,128)(2,1)} %bitcast.5), calls=%async_computation.1 | async-start | bytes 1048576 | tf_op jit(solution)/shard_map/all_to_all | solution.py:401
  150.2 14.3 %collective-permute-start.21 = (bf16[8,80,128]{2,1,0:T(8,128)(2,1)S(1)}, bf16[8,80,128]{2,1,0:T(8,128)(2,1)S(1)}, u32[]{:S(2)}, u32[]{:S(2)}) collective-permute-start(bf16[8,80,128]{2,1,0:T(8,128)(2,1)S(1)} %all_to_all.21.o0), channel_id=1, source_target_pairs={{0,24},{8,0},{16,8},{24,16},{1,25},{9,1},{17,9},{25,17},{2,26},{10... | collective-permute-start | bytes 491528 | tf_op jit(solution)/shard_map/ppermute | solution.py:349
  153.0 12.8 %collective-permute-start.20 = (bf16[8,80,128]{2,1,0:T(8,128)(2,1)S(1)}, bf16[8,80,128]{2,1,0:T(8,128)(2,1)S(1)}, u32[]{:S(2)}, u32[]{:S(2)}) collective-permute-start(bf16[8,80,128]{2,1,0:T(8,128)(2,1)S(1)} %all_to_all.21.o0), channel_id=1, source_target_pairs={{0,16},{8,24},{16,0},{24,8},{1,17},{9,25},{17,1},{25,9},{2,18},{10... | collective-permute-start | bytes 491528 | tf_op jit(solution)/shard_map/ppermute | solution.py:349
  153.5 15.3 %collective-permute-start.19 = (bf16[8,80,128]{2,1,0:T(8,128)(2,1)S(1)}, bf16[8,80,128]{2,1,0:T(8,128)(2,1)S(1)}, u32[]{:S(2)}, u32[]{:S(2)}) collective-permute-start(bf16[8,80,128]{2,1,0:T(8,128)(2,1)S(1)} %all_to_all.21.o0), channel_id=1, source_target_pairs={{0,8},{8,16},{16,24},{24,0},{1,9},{9,17},{17,25},{25,1},{2,10},{10... | collective-permute-start | bytes 491528 | tf_op jit(solution)/shard_map/ppermute | solution.py:349
  154.1 18.5 %collective-permute-start.22 = (bf16[8,80,128]{2,1,0:T(8,128)(2,1)S(1)}, bf16[8,80,128]{2,1,0:T(8,128)(2,1)S(1)}, u32[]{:S(2)}, u32[]{:S(2)}) collective-permute-start(bf16[8,80,128]{2,1,0:T(8,128)(2,1)S(1)} %all_to_all.21.o0), channel_id=1, source_target_pairs={{0,4},{4,0},{1,5},{5,1},{2,6},{6,2},{3,7},{7,3},{8,12},{12,8},{9,1... | collective-permute-start | bytes 491528 | tf_op jit(solution)/shard_map/ppermute | solution.py:349
  164.6 8.1 %copy-start.14 = (bf16[8,80,128]{2,1,0:T(8,128)(2,1)}, bf16[8,80,128]{2,1,0:T(8,128)(2,1)S(1)}, u32[]{:S(2)}) copy-start(bf16[8,80,128]{2,1,0:T(8,128)(2,1)S(1)} %collective-permute-done.21.o3) | copy-start | bytes 491524
  164.6 8.0 %collective-permute-start.25 = (bf16[8,80,128]{2,1,0:T(8,128)(2,1)S(1)}, bf16[8,80,128]{2,1,0:T(8,128)(2,1)S(1)}, u32[]{:S(2)}, u32[]{:S(2)}) collective-permute-start(bf16[8,80,128]{2,1,0:T(8,128)(2,1)S(1)} %collective-permute-done.21.o3), channel_id=1, source_target_pairs={{0,4},{4,0},{1,5},{5,1},{2,6},{6,2},{3,7},{7,3},{8,12},{12,8},{9,1... | collective-permute-start | bytes 491528 | tf_op jit(solution)/shard_map/ppermute | solution.py:349
  165.7 6.9 %collective-permute-start.24 = (bf16[8,80,128]{2,1,0:T(8,128)(2,1)S(1)}, bf16[8,80,128]{2,1,0:T(8,128)(2,1)S(1)}, u32[]{:S(2)}, u32[]{:S(2)}) collective-permute-start(bf16[8,80,128]{2,1,0:T(8,128)(2,1)S(1)} %collective-permute-done.20.o2), channel_id=1, source_target_pairs={{0,4},{4,0},{1,5},{5,1},{2,6},{6,2},{3,7},{7,3},{8,12},{12,8},{9,1... | collective-permute-start | bytes 491528 | tf_op jit(solution)/shard_map/ppermute | solution.py:349
  168.8 3.9 %collective-permute-start.23 = (bf16[8,80,128]{2,1,0:T(8,128)(2,1)S(1)}, bf16[8,80,128]{2,1,0:T(8,128)(2,1)S(1)}, u32[]{:S(2)}, u32[]{:S(2)}) collective-permute-start(bf16[8,80,128]{2,1,0:T(8,128)(2,1)S(1)} %collective-permute-done.19.o1), channel_id=1, source_target_pairs={{0,4},{4,0},{1,5},{5,1},{2,6},{6,2},{3,7},{7,3},{8,12},{12,8},{9,1... | collective-permute-start | bytes 491528 | tf_op jit(solution)/shard_map/ppermute | solution.py:349
  (23 other events, 52.6 us)

commit v2 on v1

--- a/solution.py
+++ b/solution.py
@@ -15,7 +15,7 @@
 NN = (((1,), (0,)), ((), ()))
 NT = (((1,), (1,)), ((), ()))
 TN = (((0,), (0,)), ((), ()))
-VMEM_LIMIT = 56 * 1024 * 1024
+VMEM_LIMIT = 24 * 1024 * 1024
 
 
 def dot(a, b, dims=NN):
@@ -61,12 +61,15 @@
     return (code + b[:1]).astype(jnp.int32)
 
 
-def prep_body(blocks_ref, owners_ref, x_ref, w_in_ref, w_out_ref, out_ref, pack_ref):
+def pack_body(w_in_ref, w_out_ref, pack_ref):
     half = lax.axis_index("c")
     pack_ref[:256, :] = w_in_ref[:, pl.ds(pl.multiple_of(half * 1024, 1024), 1024)]
     wo = w_out_ref[:, pl.ds(pl.multiple_of(half * 512, 512), 512)]
     pack_ref[256:, :512] = wo[:64]
     pack_ref[256:, 512:] = wo[64:]
+
+
+def rows_out_body(blocks_ref, owners_ref, x_ref, out_ref):
     code = slots_of_rows(blocks_ref, owners_ref, 128)
     row = iota((1024, 128), 0)
     total = None
@@ -77,7 +80,7 @@
     out_ref[...] = total.astype(BF16)
 
 
-def rows_back_body(blocks_ref, owners_ref, returned_ref, out_ref):
+def rows_back(blocks_ref, owners_ref, returned_ref, out_ref):
     code = slots_of_rows(blocks_ref, owners_ref, 128)
     eye = iota((128, 128), 0) == iota((128, 128), 1)
     column = jnp.sum(jnp.where(eye, code.astype(F32), 0.0), axis=1, keepdims=True).astype(jnp.int32)
@@ -95,19 +98,23 @@
         if k == 0:
             h = half if is_own else other_half
             return w_in[:, pl.ds(pl.multiple_of(h * 1024, 1024), 1024)]
-        return (own if is_own else other)[k - 1][:256, :]
+        left, right, top, low = own if is_own else other
+        if k == 2:
+            return jnp.concatenate([top[...], low[:96, :]], axis=0)
+        return (left if k == 1 else right)[:256, :]
 
     def back(k, is_own):
         if k == 0:
             h = half if is_own else other_half
             return w_out[:, pl.ds(pl.multiple_of(h * 512, 512), 512)]
-        ref = (own if is_own else other)[k - 1]
-        return jnp.concatenate([ref[256:, :512], ref[256:, 512:]], axis=0)
+        left, right, top, low = own if is_own else other
+        part = low[96:, :] if k == 2 else (left if k == 1 else right)[256:, :]
+        return jnp.concatenate([part[:, :512], part[:, 512:]], axis=0)
 
     return proj, back
 
 
-def grad_chunks(x, y, half, nrm, dpre, mix, cot, out):
+def grad_chunks(x, y, half, nrm, dpre, mix, cot, put):
     right = cot[:, pl.ds(pl.multiple_of(half * 512, 512), 512)]
     for sx in range(4):
         block = (x + sx) % 4
@@ -115,26 +122,24 @@
         d_out = dot(mix[block], right, TN).astype(BF16)
         tail = jnp.concatenate([d_out[:64], d_out[64:]], axis=1)
         for m in range(4):
-            sy = (m + 4 - y) % 4
             if m < 3:
                 rows = d_in[80 * m : 80 * m + 80]
             else:
                 rows = jnp.concatenate([d_in[240:], tail], axis=0)
-            out[0, sx, sy] = rows[:, :512]
-            out[1, sy, sx] = rows[:, 512:]
+            put(sx, (m + 4 - y) % 4, rows)
 
 
 CHUNK = 32
 
 
 def layer_body(
-    blocks_ref, owners_ref, arrived, cot, w_in, w_out, a1, b1, a2, b2, a3, b3,
+    blocks_ref, owners_ref, arrived, cot, w_in, w_out, a1, a2, a3, a4, b1, b2, b3, b4,
     layer_out, gother, nrm, dpre, mix, rstd,
     owned, pre, act, att, att_rstd, weights, dscore, dmixed, datt,
 ):
     x, y, c = lax.axis_index("x"), lax.axis_index("y"), lax.axis_index("c")
     me = (lax.axis_index("z") * 4 + y) * 2 + c
-    proj, back = weights_of(x, c, (w_in, w_out, (a1, a2, a3), (b1, b2, b3)))
+    proj, back = weights_of(x, c, (w_in, w_out, (a1, a2, a3, a4), (b1, b2, b3, b4)))
     halves = ((True, c), (False, 1 - c))
 
     t = iota((256, 1024), 0)
@@ -254,16 +259,19 @@
         dpre[1, :, lo:hi] = (dq * pre[1, :, lo:hi]).astype(BF16)
         dpre[1, :, 512 + lo : 512 + hi] = (dk * pre[1, :, 512 + lo : 512 + hi]).astype(BF16)
 
-    grad_chunks(x, y, 1 - c, nrm, dpre, mix, cot, gother)
+    def put(sx, sy, rows):
+        gother[0, sx, sy] = rows[:, :512]
+        gother[1, sy, sx] = rows[:, 512:]
+
+    grad_chunks(x, y, 1 - c, nrm, dpre, mix, cot, put)
 
 
 def rest_body(
-    nrm, dpre, mix, rstd, cot, w_in, w_out, a1, b1, a2, b2, a3, b3,
-    gown, outgoing, dnorm, downed,
+    nrm, dpre, rstd, cot, w_in, w_out, a1, a2, a3, a4, b1, b2, b3, b4,
+    downed, dnorm,
 ):
-    x, y, c = lax.axis_index("x"), lax.axis_index("y"), lax.axis_index("c")
-    proj, _ = weights_of(x, c, (w_in, w_out, (a1, a2, a3), (b1, b2, b3)))
-    grad_chunks(x, y, c, nrm, dpre, mix, cot, gown)
+    x, c = lax.axis_index("x"), lax.axis_index("c")
+    proj, _ = weights_of(x, c, (w_in, w_out, (a1, a2, a3, a4), (b1, b2, b3, b4)))
     for k in range(4):
         total = None
         for is_own, h in ((True, c), (False, 1 - c)):
@@ -282,6 +290,19 @@
         return 0
 
     lax.fori_loop(0, 256 // CHUNK, unnorm_rows, 0)
+
+def sum_pair_body(nrm, dpre, mix, cot, downed, gfrom, *refs):
+    outs, outgoing, held = refs[:8], refs[8], refs[9]
+    x, y, c = lax.axis_index("x"), lax.axis_index("y"), lax.axis_index("c")
+
+    def put(sx, sy, rows):
+        rows = rows.astype(F32)
+        outs[sx][sy] = (rows[:, :512] + gfrom[0, sx, sy].astype(F32)).astype(BF16)
+        held[sy, sx] = (rows[:, 512:] + gfrom[1, sy, sx].astype(F32)).astype(BF16)
+
+    grad_chunks(x, y, c, nrm, dpre, mix, cot, put)
+    for sy in range(4):
+        outs[4 + sy][...] = held[sy]
     t = iota((1024, 256), 1)
     wanted = (t & 63) * 16 + (t >> 6) * 4
     row = iota((1024, 256), 0)
@@ -293,14 +314,8 @@
     outgoing[...] = total.astype(BF16)
 
 
-def add_pair_body(own, other, *outs):
-    for color in range(2):
-        for s in range(4):
-            both = own[color, s].astype(F32) + other[color, s].astype(F32)
-            outs[color * 4 + s][...] = both.astype(BF16)
-
-
-def add_four_body(a0, a1, a2, a3, b0, b1, b2, b3, *outs):
+def add_four_body(a0, a1, a2, a3, b0, b1, b2, b3, blocks, owners, returned, rows, *outs):
+    rows_back(blocks, owners, returned, rows)
     for color, refs in enumerate(((a0, a1, a2, a3), (b0, b1, b2, b3))):
         for s in range(4):
             total = refs[0][s].astype(F32)
@@ -351,18 +366,16 @@
 
 def on_device(x_rows, cotangent, w_in, w_out, hist_blocks, owner):
     cot = cotangent[0]
-    outgoing, pack = call(
-        prep_body,
-        [((1024, 256), BF16), ((320, 1024), BF16)],
-        (hist_blocks, owner, x_rows[0], w_in, w_out),
-        "route_out",
-    )
-    own = [shift(pack, "x", 4, s) for s in (1, 2, 3)]
-    other = [shift(a, "c", 2, 1) for a in own]
+    (pack,) = call(pack_body, [((320, 1024), BF16)], (w_in, w_out), "pack")
+    left, right = shift(pack, "x", 4, 1), shift(pack, "x", 4, 3)
+    (outgoing,) = call(
+        rows_out_body, [((1024, 256), BF16)], (hist_blocks, owner, x_rows[0]), "rows_out"
+    )
     arrived = lax.all_to_all(
         outgoing.reshape(64, 16, 256), DP, split_axis=0, concat_axis=0, tiled=True
     ).reshape(1024, 256)
-    weights = (w_in, w_out, own[0], other[0], own[1], other[1], own[2], other[2])
+    own = [left, right, shift(left[:160], "x", 4, 1), shift(right[160:], "x", 4, 3)]
+    weights = (w_in, w_out, *own, *[shift(a, "c", 2, 1) for a in own])
     layer_out, gother, nrm, dpre, mix, rstd = call(
         layer_body,
         [
@@ -388,23 +401,31 @@
         ],
     )
     gfrom = shift(gother, "c", 2, 1)
-    gown, backward = call(
+    (downed,) = call(
         rest_body,
-        [((2, 4, 4, 80, 512), BF16), ((1024, 256), BF16)],
-        (nrm, dpre, mix, rstd, cot) + weights,
+        [((256, 1024), BF16)],
+        (nrm, dpre, rstd, cot) + weights,
         "rest",
-        scratch=[((4, 256, 256), BF16), ((256, 1024), BF16)],
-    )
-    big = call(add_pair_body, [((4, 80, 512), BF16)] * 8, (gown, gfrom), "add_pair")
+        scratch=[((4, 256, 256), BF16)],
+    )
+    *big, backward = call(
+        sum_pair_body,
+        [((4, 80, 512), BF16)] * 8 + [((1024, 256), BF16)],
+        (nrm, dpre, mix, cot, downed, gfrom),
+        "sum_pair",
+        scratch=[((4, 4, 80, 512), BF16)],
+    )
     first = [big[0]] + [shift(big[s], "x", 4, s) for s in (1, 2, 3)]
     second = [big[4]] + [shift(big[4 + s], "y", 4, s) for s in (1, 2, 3)]
     returned = lax.all_to_all(
         backward.reshape(64, 16, 256), DP, split_axis=0, concat_axis=0, tiled=True
     ).reshape(1024, 256)
-    (grad_rows,) = call(
-        rows_back_body, [((128, 1024), BF16)], (hist_blocks, owner, returned), "route_back"
-    )
-    mid = call(add_four_body, [((80, 512), BF16)] * 8, (*first, *second), "add_four")
+    grad_rows, *mid = call(
+        add_four_body,
+        [((128, 1024), BF16)] + [((80, 512), BF16)] * 8,
+        (*first, *second, hist_blocks, owner, returned),
+        "add_four",
+    )
     first = [mid[0]] + [shift(mid[s], "y", 4, s) for s in (1, 2, 3)]
     second = [mid[4]] + [shift(mid[4 + s], "x", 4, s) for s in (1, 2, 3)]
     (columns,) = call(add_last_body, [((8, 80, 128), BF16)], (*first, *second), "add_last")

time: 178 us -> 155 us (0.87)
  Pallas kernels: 42.9 us -> 24.7 us
  blocking collectives: 28.2 us -> 25.2 us
    pallas_call x9, Pallas kernels: 42.9 us -> 24.7 us  [call(): pl.pallas_call(body, out_shape=[jax.ShapeDtypeStruct(s, d) for s, d in ou...]
    ppermute x26 -> x28, waiting for transfers between devices: 33.7 us -> 29.7 us  [shift(): return lax.ppermute(a, axis, [(i, (i + s) % n) for i in range(n)])]
    all_to_all x1, waiting for transfers between devices: 0.01 us -> 3.01 us  [on_device(): lax.all_to_all(outgoing.reshape(64, 16, 256), DP, split_axis=0, concat_ax...]
    all_to_all x1, blocking collectives: 16.7 us -> 14.6 us  [on_device(): lax.all_to_all(columns, 'z', split_axis=0, concat_axis=0, tiled=True)]
    unnamed x54 -> x22, local copies, waits for them, and re-layouts: 5.21 us -> 5.39 us
    ppermute x26 -> x28, starting transfers between devices: 43.7 us -> 43.9 us  [shift(): return lax.ppermute(a, axis, [(i, (i + s) % n) for i in range(n)])]
  transfers between devices with their start and end apart: 28 -> 30, of which waited for: 10 -> 14; matrix products, arithmetic and copies ran while one was open for 0% -> 0% of each run, Pallas kernels for 6% -> 4%
where the time goes in v2:
time: 155 us; the launch traced here: 154 us
  starting transfers between devices  65.5 us (42%)
  waiting for transfers between devices  32.7 us (21%)
  blocking collectives  25.2 us (16%)
  Pallas kernels  24.7 us (16%)
  local copies, waits for them, and re-layouts  5.44 us (4%)
    ppermute x28, starting transfers between devices, shift(): return lax.ppermute(a, axis, [(i, (i + s) % n) for i in range(n)])  43.9 us
    ppermute x28, waiting for transfers between devices, shift(): return lax.ppermute(a, axis, [(i, (i + s) % n) for i in range(n)])  29.7 us
    pallas_call x9, Pallas kernels, call(): pl.pallas_call(body, out_shape=[jax.ShapeDtypeStruct(s, d) for s, d in ou...  24.7 us
    all_to_all x1, blocking collectives, on_device(): lax.all_to_all(columns, 'z', split_axis=0, concat_axis=0, tiled=True)  14.6 us
    all_to_all x1, starting transfers between devices, on_device(): lax.all_to_all(outgoing.reshape(64, 16, 256), DP, split_axis=0, concat_ax...  12.8 us
    all_to_all x1, blocking collectives, on_device(): mine = lax.all_to_all(summed, 'z', split_axis=0, concat_axis=0, tiled=True)  10.7 us
    all_to_all x1, starting transfers between devices, on_device(): lax.all_to_all(backward.reshape(64, 16, 256), DP, split_axis=0, concat_ax...  8.84 us
    unnamed x22, local copies, waits for them, and re-layouts  5.39 us
  transfers between devices with their start and end apart: 30, of which 14 were waited for; matrix products, arithmetic and copies ran while one was open for 0% of the time, Pallas kernels for 4%

profile of v2, /device:TPU:1, one launch (start us, length us, event | category | flops | bytes accessed | tf_op | source)
XLA Modules:
  0.0 154.4 jit_solution(13769663100278113002)
XLA Ops:
  0.6 1.2 copy-done
  2.9 3.4 %collective-permute-start.1 = (bf16[320,1024]{1,0:T(8,128)(2,1)S(1)}, bf16[320,1024]{1,0:T(8,128)(2,1)S(1)}, u32[]{:S(2)}, u32[]{:S(2)}) collective-permute-start(bf16[320,1024]{1,0:T(8,128)(2,1)S(1)} %pack.1), channel_id=1, source_target_pairs={{0,3},{1,0},{2,1},{3,2},{4,7},{5,4},{6,5},{7,6},{8,11},{9,8},{10,9... | collective-permute-start | bytes 1966088 | tf_op jit(solution)/shard_map/ppermute | solution.py:364
  8.5 1.6 %rows_out.1 = bf16[1024,256]{1,0:T(8,128)(2,1)} custom-call(s32[1,64]{1,0:T(1,128)S(1)} %copy-done.7, s32[1,64]{1,0:T(1,128)S(1)} %copy-done.9, bf16[128,1024]{1,0:T(8,128)(2,1)S(1)} %bitcast.12), custom_call_target="tpu_custom_call" | custom-call | tf_op jit(solution)/shard_map/rows_out/pallas_call | solution.py:30
  10.2 12.8 %all-to-all-start = ((bf16[64,16,256]{2,1,0:T(8,128)(2,1)}), bf16[64,16,256]{2,1,0:T(8,128)(2,1)}, u32[]{:S(2)}, u32[]{:S(2)}) async-start(bf16[64,16,256]{2,1,0:T(8,128)(2,1)} %bitcast.1), calls=%async_computation | async-start | bytes 1048576 | tf_op jit(solution)/shard_map/all_to_all | solution.py:374
  23.0 3.0 %collective-permute-start.3 = (bf16[160,1024]{1,0:T(8,128)(2,1)S(1)}, bf16[160,1024]{1,0:T(8,128)(2,1)}, u32[]{:S(2)}, u32[]{:S(2)}) collective-permute-start(bf16[160,1024]{1,0:T(8,128)(2,1)S(1)} %slice.9), channel_id=1, source_target_pairs={{0,3},{1,0},{2,1},{3,2},{4,7},{5,4},{6,5},{7,6},{8,11},{9,8},{10,9... | collective-permute-start | bytes 983048 | tf_op jit(solution)/shard_map/ppermute | solution.py:364
  27.2 5.4 %collective-permute-done.3.a4 = bf16[160,1024]{1,0:T(8,128)(2,1)} collective-permute-done((bf16[160,1024]{1,0:T(8,128)(2,1)S(1)}, bf16[160,1024]{1,0:T(8,128)(2,1)}, u32[]{:S(2)}, u32[]{:S(2)}) %collective-permute-start.3) | collective-permute-done | bytes 327712 | tf_op jit(solution)/shard_map/ppermute | solution.py:364
  32.6 1.4 collective-permute-start.7
  34.0 1.9 %collective-permute-done.2.a3 = bf16[160,1024]{1,0:T(8,128)(2,1)} collective-permute-done((bf16[160,1024]{1,0:T(8,128)(2,1)S(1)}, bf16[160,1024]{1,0:T(8,128)(2,1)}, u32[]{:S(2)}, u32[]{:S(2)}) %collective-permute-start.2) | collective-permute-done | bytes 327712 | tf_op jit(solution)/shard_map/ppermute | solution.py:364
  35.9 1.7 %collective-permute-start.6 = (bf16[160,1024]{1,0:T(8,128)(2,1)}, bf16[160,1024]{1,0:T(8,128)(2,1)}, u32[]{:S(2)}, u32[]{:S(2)}) collective-permute-start(bf16[160,1024]{1,0:T(8,128)(2,1)} %collective-permute-done.2.a3), channel_id=1, source_target_pairs={{0,4},{4,0},{1,5},{5,1},{2,6},{6,2},{3,7},{7,3},{8,12},{12,8},{9,1... | collective-permute-start | bytes 983048 | tf_op jit(solution)/shard_map/ppermute | solution.py:364
  37.6 3.0 %all-to-all-done = bf16[64,16,256]{2,1,0:T(8,128)(2,1)} async-done(((bf16[64,16,256]{2,1,0:T(8,128)(2,1)}), bf16[64,16,256]{2,1,0:T(8,128)(2,1)}, u32[]{:S(2)}, u32[]{:S(2)}) %all-to-all-start) | async-done | bytes 524320 | tf_op jit(solution)/shard_map/all_to_all | solution.py:374
  41.6 12.9 %layer.1 = (bf16[256,1024]{1,0:T(8,128)(2,1)}, bf16[2,4,4,80,512]{4,3,2,1,0:T(8,128)(2,1)S(1)}, bf16[4,256,256]{2,1,0:T(8,128)(2,1)S(1)}, bf16[2,256,1024]{2,1,0...) custom-call(s32[1,64]{1,0:T(1,128)S(1)} %copy-done.8, s32[1,64]{1,0:T(1,128)S(1)} %copy-done.10, ...), custom_call_target="tpu_custom_call" | custom-call | tf_op jit(solution)/shard_map/layer/pallas_call | solution.py:30
  55.0 3.8 %rest.1.downed = bf16[256,1024]{1,0:T(8,128)(2,1)S(1)} custom-call(bf16[4,256,256]{2,1,0:T(8,128)(2,1)S(1)} %get-tuple-element.31.nrm, bf16[2,256,1024]{2,1,0:T(8,128)(2,1)S(1)} %get-tuple-element.32.dpre, f32[256,128]{1,0:T(8,128)S(1)} %get-tuple-element.34.rstd, bf16[256,1024]{1,0:T(8,128)(2,1)S(1)} %bitcast.9, bf16[256,2048]{1,0:T(8,128)(2,1)S(1)} %copy-done.1, ...), custom_call_target="tpu_custom_call" | custom-call | tf_op jit(solution)/shard_map/rest/pallas_call | solution.py:30
  59.6 2.5 %sum_pair.1 = (bf16[4,80,512]{2,1,0:T(8,128)(2,1)S(1)}, bf16[4,80,512]{2,1,0:T(8,128)(2,1)S(1)}, bf16[4,80,512]{2,1,0:T(8,128)(2,1)}, bf16[4,80,512]{2,1,0:T(8,1...) custom-call(bf16[4,256,256]{2,1,0:T(8,128)(2,1)S(1)} %get-tuple-elem, ...), custom_call_target="tpu_custom_call" | custom-call | tf_op jit(solution)/shard_map/sum_pair/pallas_call | solution.py:30
  62.1 8.8 %all-to-all-start.1 = ((bf16[64,16,256]{2,1,0:T(8,128)(2,1)}), bf16[64,16,256]{2,1,0:T(8,128)(2,1)S(1)}, u32[]{:S(2)}, u32[]{:S(2)}) async-start(bf16[64,16,256]{2,1,0:T(8,128)(2,1)} %bitcast.5), calls=%async_computation.1 | async-start | bytes 1048576 | tf_op jit(solution)/shard_map/all_to_all | solution.py:420
  71.0 1.5 collective-permute-start.10
  73.7 1.4 collective-permute-start.12
  75.0 2.4 %collective-permute-start.13 = (bf16[4,80,512]{2,1,0:T(8,128)(2,1)}, bf16[4,80,512]{2,1,0:T(8,128)(2,1)S(1)}, u32[]{:S(2)}, u32[]{:S(2)}) collective-permute-start(bf16[4,80,512]{2,1,0:T(8,128)(2,1)} %get-tuple-element.42), channel_id=1, source_target_pairs={{0,16},{8,24},{16,0},{24,8},{1,17},{9,25},{17,1},{25,9},{2,18},{10... | collective-permute-start | bytes 983048 | tf_op jit(solution)/shard_map/ppermute | solution.py:364
  77.4 10.6 %collective-permute-done.9.a1 = bf16[4,80,512]{2,1,0:T(8,128)(2,1)S(1)} collective-permute-done((bf16[4,80,512]{2,1,0:T(8,128)(2,1)S(1)}, bf16[4,80,512]{2,1,0:T(8,128)(2,1)S(1)}, u32[]{:S(2)}, u32[]{:S(2)}) %collective-permute-start.9) | collective-permute-done | bytes 327712 | tf_op jit(solution)/shard_map/ppermute | solution.py:364
  88.0 2.7 %collective-permute-start.14 = (bf16[4,80,512]{2,1,0:T(8,128)(2,1)S(1)}, bf16[4,80,512]{2,1,0:T(8,128)(2,1)S(1)}, u32[]{:S(2)}, u32[]{:S(2)}) collective-permute-start(bf16[4,80,512]{2,1,0:T(8,128)(2,1)S(1)} %get-tuple-element.43), channel_id=1, source_target_pairs={{0,24},{8,0},{16,8},{24,16},{1,25},{9,1},{17,9},{25,17},{2,26},{10... | collective-permute-start | bytes 983048 | tf_op jit(solution)/shard_map/ppermute | solution.py:364
  90.8 5.5 %collective-permute-done.13.b2 = bf16[4,80,512]{2,1,0:T(8,128)(2,1)S(1)} collective-permute-done((bf16[4,80,512]{2,1,0:T(8,128)(2,1)}, bf16[4,80,512]{2,1,0:T(8,128)(2,1)S(1)}, u32[]{:S(2)}, u32[]{:S(2)}) %collective-permute-start.13) | collective-permute-done | bytes 327712 | tf_op jit(solution)/shard_map/ppermute | solution.py:364
  96.6 1.6 %add_four.1 = (bf16[128,1024]{1,0:T(8,128)(2,1)}, bf16[80,512]{1,0:T(8,128)(2,1)S(1)}, bf16[80,512]{1,0:T(8,128)(2,1)S(1)}, bf16[80,512]{1,0:T(8,128)(2,1)S(1)},...) custom-call(bf16[4,80,512]{2,1,0:T(8,128)(2,1)S(1)} %get-tuple-eleme, ...), custom_call_target="tpu_custom_call" | custom-call | tf_op jit(solution)/shard_map/add_four/pallas_call | solution.py:30
  99.1 3.6 %collective-permute-start.16 = (bf16[80,512]{1,0:T(8,128)(2,1)S(1)}, bf16[80,512]{1,0:T(8,128)(2,1)S(1)}, u32[]{:S(2)}, u32[]{:S(2)}) collective-permute-start(bf16[80,512]{1,0:T(8,128)(2,1)S(1)} %get-tuple-element.48), channel_id=1, source_target_pairs={{0,16},{8,24},{16,0},{24,8},{1,17},{9,25},{17,1},{25,9},{2,18},{10... | collective-permute-start | bytes 245768 | tf_op jit(solution)/shard_map/ppermute | solution.py:364
  103.4 2.0 %collective-permute-start.20 = (bf16[80,512]{1,0:T(8,128)(2,1)S(1)}, bf16[80,512]{1,0:T(8,128)(2,1)S(1)}, u32[]{:S(2)}, u32[]{:S(2)}) collective-permute-start(bf16[80,512]{1,0:T(8,128)(2,1)S(1)} %get-tuple-element.53), channel_id=1, source_target_pairs={{0,3},{1,0},{2,1},{3,2},{4,7},{5,4},{6,5},{7,6},{8,11},{9,8},{10,9... | collective-permute-start | bytes 245768 | tf_op jit(solution)/shard_map/ppermute | solution.py:364
  106.6 1.5 collective-permute-done.18.b1
  109.1 14.6 %all_to_all.20.parts = bf16[8,80,128]{2,1,0:T(8,128)(2,1)S(1)} all-to-all(bf16[8,80,128]{2,1,0:T(8,128)(2,1)S(1)} %add_last.1), channel_id=1, replica_groups=mesh['z'=8,'y'=4,'c'=2,'x'=4] {'z'}, dimensions={0} | all-to-all | bytes 327680 | tf_op jit(solution)/shard_map/all_to_all | solution.py:432
  123.7 10.7 %all_to_all.21.o0 = bf16[8,80,128]{2,1,0:T(8,128)(2,1)S(1)} all-to-all(bf16[8,80,128]{2,1,0:T(8,128)(2,1)S(1)} %add_eight.1), channel_id=1, replica_groups=mesh['z'=8,'y'=4,'c'=2,'x'=4] {'z'}, dimensions={0} | all-to-all | bytes 327680 | tf_op jit(solution)/shard_map/all_to_all | solution.py:434
  134.7 2.7 %collective-permute-start.22 = (bf16[8,80,128]{2,1,0:T(8,128)(2,1)S(1)}, bf16[8,80,128]{2,1,0:T(8,128)(2,1)S(1)}, u32[]{:S(2)}, u32[]{:S(2)}) collective-permute-start(bf16[8,80,128]{2,1,0:T(8,128)(2,1)S(1)} %all_to_all.21.o0), channel_id=1, source_target_pairs={{0,16},{8,24},{16,0},{24,8},{1,17},{9,25},{17,1},{25,9},{2,18},{10... | collective-permute-start | bytes 491528 | tf_op jit(solution)/shard_map/ppermute | solution.py:364
  137.3 7.5 %collective-permute-start.24 = (bf16[8,80,128]{2,1,0:T(8,128)(2,1)S(1)}, bf16[8,80,128]{2,1,0:T(8,128)(2,1)S(1)}, u32[]{:S(2)}, u32[]{:S(2)}) collective-permute-start(bf16[8,80,128]{2,1,0:T(8,128)(2,1)S(1)} %all_to_all.21.o0), channel_id=1, source_target_pairs={{0,4},{4,0},{1,5},{5,1},{2,6},{6,2},{3,7},{7,3},{8,12},{12,8},{9,1... | collective-permute-start | bytes 491528 | tf_op jit(solution)/shard_map/ppermute | solution.py:364
  144.9 1.5 collective-permute-start.27
  146.3 1.8 %collective-permute-start.26 = (bf16[8,80,128]{2,1,0:T(8,128)(2,1)S(1)}, bf16[8,80,128]{2,1,0:T(8,128)(2,1)S(1)}, u32[]{:S(2)}, u32[]{:S(2)}) collective-permute-start(bf16[8,80,128]{2,1,0:T(8,128)(2,1)S(1)} %collective-permute-done.22.o2), channel_id=1, source_target_pairs={{0,4},{4,0},{1,5},{5,1},{2,6},{6,2},{3,7},{7,3},{8,12},{12,8},{9,1... | collective-permute-start | bytes 491528 | tf_op jit(solution)/shard_map/ppermute | solution.py:364
  148.2 3.2 %collective-permute-start.25 = (bf16[8,80,128]{2,1,0:T(8,128)(2,1)S(1)}, bf16[8,80,128]{2,1,0:T(8,128)(2,1)S(1)}, u32[]{:S(2)}, u32[]{:S(2)}) collective-permute-start(bf16[8,80,128]{2,1,0:T(8,128)(2,1)S(1)} %collective-permute-done.21.o1), channel_id=1, source_target_pairs={{0,4},{4,0},{1,5},{5,1},{2,6},{6,2},{3,7},{7,3},{8,12},{12,8},{9,1... | collective-permute-start | bytes 491528 | tf_op jit(solution)/shard_map/ppermute | solution.py:364
  152.4 2.0 %place.1 = (f32[256,2048]{1,0:T(8,128)}, f32[128,1024]{1,0:T(8,128)}) custom-call(bf16[8,80,128]{2,1,0:T(8,128)(2,1)S(1)} %all_to_all.21.o0, bf16[8,80,128]{2,1,0:T(8,128)(2,1)S(1)} %collective-permute-done.21.o1, bf16[8,80,128]{2,1,0:T(8,128)(2,1)S(1)} %collective-permute-done.22.o2, bf16[8,80,128]{2,1,0:T(8,128)(2,1)S(1)} %collective-permute-done.23.o3, ...), custom_call_target="tpu_custom_call" | custom-call | tf_op jit(solution)/shard_map/place/pallas_call | solution.py:30
  (63 shorter events, 13.2 us)
Async XLA Ops:
  2.8 37.9 %copy-start.8 = (s32[1,64]{1,0:T(1,128)S(1)}, s32[1,64]{1,0:T(1,128)}, u32[]{:S(2)}) copy-start(s32[1,64]{1,0:T(1,128)} %blocks.1) | copy-start | bytes 772
  2.8 37.9 %copy-start.10 = (s32[1,64]{1,0:T(1,128)S(1)}, s32[1,64]{1,0:T(1,128)}, u32[]{:S(2)}) copy-start(s32[1,64]{1,0:T(1,128)} %owners.1) | copy-start | bytes 772
  2.9 20.1 %collective-permute-start.1 = (bf16[320,1024]{1,0:T(8,128)(2,1)S(1)}, bf16[320,1024]{1,0:T(8,128)(2,1)S(1)}, u32[]{:S(2)}, u32[]{:S(2)}) collective-permute-start(bf16[320,1024]{1,0:T(8,128)(2,1)S(1)} %pack.1), channel_id=1, source_target_pairs={{0,3},{1,0},{2,1},{3,2},{4,7},{5,4},{6,5},{7,6},{8,11},{9,8},{10,9... | collective-permute-start | bytes 1966088 | tf_op jit(solution)/shard_map/ppermute | solution.py:364
  6.3 19.8 %collective-permute-start = (bf16[320,1024]{1,0:T(8,128)(2,1)S(1)}, bf16[320,1024]{1,0:T(8,128)(2,1)S(1)}, u32[]{:S(2)}, u32[]{:S(2)}) collective-permute-start(bf16[320,1024]{1,0:T(8,128)(2,1)S(1)} %pack.1), channel_id=1, source_target_pairs={{0,1},{1,2},{2,3},{3,0},{4,5},{5,6},{6,7},{7,4},{8,9},{9,10},{10,1... | collective-permute-start | bytes 1966088 | tf_op jit(solution)/shard_map/ppermute | solution.py:364
  10.2 30.4 %all-to-all-start = ((bf16[64,16,256]{2,1,0:T(8,128)(2,1)}), bf16[64,16,256]{2,1,0:T(8,128)(2,1)}, u32[]{:S(2)}, u32[]{:S(2)}) async-start(bf16[64,16,256]{2,1,0:T(8,128)(2,1)} %bitcast.1), calls=%async_computation | async-start | bytes 1048576 | tf_op jit(solution)/shard_map/all_to_all | solution.py:374
  23.0 9.6 %collective-permute-start.3 = (bf16[160,1024]{1,0:T(8,128)(2,1)S(1)}, bf16[160,1024]{1,0:T(8,128)(2,1)}, u32[]{:S(2)}, u32[]{:S(2)}) collective-permute-start(bf16[160,1024]{1,0:T(8,128)(2,1)S(1)} %slice.9), channel_id=1, source_target_pairs={{0,3},{1,0},{2,1},{3,2},{4,7},{5,4},{6,5},{7,6},{8,11},{9,8},{10,9... | collective-permute-start | bytes 983048 | tf_op jit(solution)/shard_map/ppermute | solution.py:364
  26.1 9.8 %collective-permute-start.2 = (bf16[160,1024]{1,0:T(8,128)(2,1)S(1)}, bf16[160,1024]{1,0:T(8,128)(2,1)}, u32[]{:S(2)}, u32[]{:S(2)}) collective-permute-start(bf16[160,1024]{1,0:T(8,128)(2,1)S(1)} %slice.8), channel_id=1, source_target_pairs={{0,1},{1,2},{2,3},{3,0},{4,5},{5,6},{6,7},{7,4},{8,9},{9,10},{10,1... | collective-permute-start | bytes 983048 | tf_op jit(solution)/shard_map/ppermute | solution.py:364
  26.2 14.4 %collective-permute-start.5 = (bf16[320,1024]{1,0:T(8,128)(2,1)S(1)}, bf16[320,1024]{1,0:T(8,128)(2,1)S(1)}, u32[]{:S(2)}, u32[]{:S(2)}) collective-permute-start(bf16[320,1024]{1,0:T(8,128)(2,1)S(1)} %collective-permute-done.1.a2), channel_id=1, source_target_pairs={{0,4},{4,0},{1,5},{5,1},{2,6},{6,2},{3,7},{7,3},{8,12},{12,8},{9,1... | collective-permute-start | bytes 1966088 | tf_op jit(solution)/shard_map/ppermute | solution.py:364
  27.1 13.6 %collective-permute-start.4 = (bf16[320,1024]{1,0:T(8,128)(2,1)S(1)}, bf16[320,1024]{1,0:T(8,128)(2,1)}, u32[]{:S(2)}, u32[]{:S(2)}) collective-permute-start(bf16[320,1024]{1,0:T(8,128)(2,1)S(1)} %collective-permute-done.a1), channel_id=1, source_target_pairs={{0,4},{4,0},{1,5},{5,1},{2,6},{6,2},{3,7},{7,3},{8,12},{12,8},{9,1... | collective-permute-start | bytes 1966088 | tf_op jit(solution)/shard_map/ppermute | solution.py:364
  32.6 8.0 %collective-permute-start.7 = (bf16[160,1024]{1,0:T(8,128)(2,1)}, bf16[160,1024]{1,0:T(8,128)(2,1)}, u32[]{:S(2)}, u32[]{:S(2)}) collective-permute-start(bf16[160,1024]{1,0:T(8,128)(2,1)} %collective-permute-done.3.a4), channel_id=1, source_target_pairs={{0,4},{4,0},{1,5},{5,1},{2,6},{6,2},{3,7},{7,3},{8,12},{12,8},{9,1... | collective-permute-start | bytes 983048 | tf_op jit(solution)/shard_map/ppermute | solution.py:364
  35.9 4.7 %collective-permute-start.6 = (bf16[160,1024]{1,0:T(8,128)(2,1)}, bf16[160,1024]{1,0:T(8,128)(2,1)}, u32[]{:S(2)}, u32[]{:S(2)}) collective-permute-start(bf16[160,1024]{1,0:T(8,128)(2,1)} %collective-permute-done.2.a3), channel_id=1, source_target_pairs={{0,4},{4,0},{1,5},{5,1},{2,6},{6,2},{3,7},{7,3},{8,12},{12,8},{9,1... | collective-permute-start | bytes 983048 | tf_op jit(solution)/shard_map/ppermute | solution.py:364
  54.6 5.0 %collective-permute-start.8 = (bf16[2,4,4,80,512]{4,3,2,1,0:T(8,128)(2,1)S(1)}, bf16[2,4,4,80,512]{4,3,2,1,0:T(8,128)(2,1)S(1)}, u32[]{:S(2)}, u32[]{:S(2)}) collective-permute-start(bf16[2,4,4,80,512]{4,3,2,1,0:T(8,128)(2,1)S(1)} %get-tuple-element.35), channel_id=1, source_target_pairs={{0,4},{4,0},{1,5},{5,1},{2,6},{6,2},{3,7},{7,3},{8,12},{12,8},{9,1... | collective-permute-start | bytes 7864328 | tf_op jit(solution)/shard_map/ppermute | solution.py:364
  62.1 34.5 %all-to-all-start.1 = ((bf16[64,16,256]{2,1,0:T(8,128)(2,1)}), bf16[64,16,256]{2,1,0:T(8,128)(2,1)S(1)}, u32[]{:S(2)}, u32[]{:S(2)}) async-start(bf16[64,16,256]{2,1,0:T(8,128)(2,1)} %bitcast.5), calls=%async_computation.1 | async-start | bytes 1048576 | tf_op jit(solution)/shard_map/all_to_all | solution.py:420
  70.9 17.1 %collective-permute-start.9 = (bf16[4,80,512]{2,1,0:T(8,128)(2,1)S(1)}, bf16[4,80,512]{2,1,0:T(8,128)(2,1)S(1)}, u32[]{:S(2)}, u32[]{:S(2)}) collective-permute-start(bf16[4,80,512]{2,1,0:T(8,128)(2,1)S(1)} %get-tuple-element.37), channel_id=1, source_target_pairs={{0,1},{1,2},{2,3},{3,0},{4,5},{5,6},{6,7},{7,4},{8,9},{9,10},{10,1... | collective-permute-start | bytes 983048 | tf_op jit(solution)/shard_map/ppermute | solution.py:364
  71.0 19.8 %collective-permute-start.10 = (bf16[4,80,512]{2,1,0:T(8,128)(2,1)}, bf16[4,80,512]{2,1,0:T(8,128)(2,1)S(1)}, u32[]{:S(2)}, u32[]{:S(2)}) collective-permute-start(bf16[4,80,512]{2,1,0:T(8,128)(2,1)} %get-tuple-element.38), channel_id=1, source_target_pairs={{0,2},{1,3},{2,0},{3,1},{4,6},{5,7},{6,4},{7,5},{8,10},{9,11},{10,... | collective-permute-start | bytes 983048 | tf_op jit(solution)/shard_map/ppermute | solution.py:364
  72.5 18.2 %collective-permute-start.11 = (bf16[4,80,512]{2,1,0:T(8,128)(2,1)}, bf16[4,80,512]{2,1,0:T(8,128)(2,1)S(1)}, u32[]{:S(2)}, u32[]{:S(2)}) collective-permute-start(bf16[4,80,512]{2,1,0:T(8,128)(2,1)} %get-tuple-element.39), channel_id=1, source_target_pairs={{0,3},{1,0},{2,1},{3,2},{4,7},{5,4},{6,5},{7,6},{8,11},{9,8},{10,9... | collective-permute-start | bytes 983048 | tf_op jit(solution)/shard_map/ppermute | solution.py:364
  73.7 17.1 %collective-permute-start.12 = (bf16[4,80,512]{2,1,0:T(8,128)(2,1)}, bf16[4,80,512]{2,1,0:T(8,128)(2,1)S(1)}, u32[]{:S(2)}, u32[]{:S(2)}) collective-permute-start(bf16[4,80,512]{2,1,0:T(8,128)(2,1)} %get-tuple-element.41), channel_id=1, source_target_pairs={{0,8},{8,16},{16,24},{24,0},{1,9},{9,17},{17,25},{25,1},{2,10},{10... | collective-permute-start | bytes 983048 | tf_op jit(solution)/shard_map/ppermute | solution.py:364
  75.0 21.2 %collective-permute-start.13 = (bf16[4,80,512]{2,1,0:T(8,128)(2,1)}, bf16[4,80,512]{2,1,0:T(8,128)(2,1)S(1)}, u32[]{:S(2)}, u32[]{:S(2)}) collective-permute-start(bf16[4,80,512]{2,1,0:T(8,128)(2,1)} %get-tuple-element.42), channel_id=1, source_target_pairs={{0,16},{8,24},{16,0},{24,8},{1,17},{9,25},{17,1},{25,9},{2,18},{10... | collective-permute-start | bytes 983048 | tf_op jit(solution)/shard_map/ppermute | solution.py:364
  88.0 8.5 %collective-permute-start.14 = (bf16[4,80,512]{2,1,0:T(8,128)(2,1)S(1)}, bf16[4,80,512]{2,1,0:T(8,128)(2,1)S(1)}, u32[]{:S(2)}, u32[]{:S(2)}) collective-permute-start(bf16[4,80,512]{2,1,0:T(8,128)(2,1)S(1)} %get-tuple-element.43), channel_id=1, source_target_pairs={{0,24},{8,0},{16,8},{24,16},{1,25},{9,1},{17,9},{25,17},{2,26},{10... | collective-permute-start | bytes 983048 | tf_op jit(solution)/shard_map/ppermute | solution.py:364
  98.2 5.2 %collective-permute-start.15 = (bf16[80,512]{1,0:T(8,128)(2,1)S(1)}, bf16[80,512]{1,0:T(8,128)(2,1)S(1)}, u32[]{:S(2)}, u32[]{:S(2)}) collective-permute-start(bf16[80,512]{1,0:T(8,128)(2,1)S(1)} %get-tuple-element.47), channel_id=1, source_target_pairs={{0,8},{8,16},{16,24},{24,0},{1,9},{9,17},{17,25},{25,1},{2,10},{10... | collective-permute-start | bytes 245768 | tf_op jit(solution)/shard_map/ppermute | solution.py:364
  99.1 6.4 %collective-permute-start.16 = (bf16[80,512]{1,0:T(8,128)(2,1)S(1)}, bf16[80,512]{1,0:T(8,128)(2,1)S(1)}, u32[]{:S(2)}, u32[]{:S(2)}) collective-permute-start(bf16[80,512]{1,0:T(8,128)(2,1)S(1)} %get-tuple-element.48), channel_id=1, source_target_pairs={{0,16},{8,24},{16,0},{24,8},{1,17},{9,25},{17,1},{25,9},{2,18},{10... | collective-permute-start | bytes 245768 | tf_op jit(solution)/shard_map/ppermute | solution.py:364
  102.8 3.9 %collective-permute-start.17 = (bf16[80,512]{1,0:T(8,128)(2,1)S(1)}, bf16[80,512]{1,0:T(8,128)(2,1)S(1)}, u32[]{:S(2)}, u32[]{:S(2)}) collective-permute-start(bf16[80,512]{1,0:T(8,128)(2,1)S(1)} %get-tuple-element.49), channel_id=1, source_target_pairs={{0,24},{8,0},{16,8},{24,16},{1,25},{9,1},{17,9},{25,17},{2,26},{10... | collective-permute-start | bytes 245768 | tf_op jit(solution)/shard_map/ppermute | solution.py:364
  102.8 5.4 %collective-permute-start.18 = (bf16[80,512]{1,0:T(8,128)(2,1)S(1)}, bf16[80,512]{1,0:T(8,128)(2,1)S(1)}, u32[]{:S(2)}, u32[]{:S(2)}) collective-permute-start(bf16[80,512]{1,0:T(8,128)(2,1)S(1)} %get-tuple-element.51), channel_id=1, source_target_pairs={{0,1},{1,2},{2,3},{3,0},{4,5},{5,6},{6,7},{7,4},{8,9},{9,10},{10,1... | collective-permute-start | bytes 245768 | tf_op jit(solution)/shard_map/ppermute | solution.py:364
  102.8 5.6 %collective-permute-start.19 = (bf16[80,512]{1,0:T(8,128)(2,1)S(1)}, bf16[80,512]{1,0:T(8,128)(2,1)S(1)}, u32[]{:S(2)}, u32[]{:S(2)}) collective-permute-start(bf16[80,512]{1,0:T(8,128)(2,1)S(1)} %get-tuple-element.52), channel_id=1, source_target_pairs={{0,2},{1,3},{2,0},{3,1},{4,6},{5,7},{6,4},{7,5},{8,10},{9,11},{10,... | collective-permute-start | bytes 245768 | tf_op jit(solution)/shard_map/ppermute | solution.py:364
  103.4 5.6 %collective-permute-start.20 = (bf16[80,512]{1,0:T(8,128)(2,1)S(1)}, bf16[80,512]{1,0:T(8,128)(2,1)S(1)}, u32[]{:S(2)}, u32[]{:S(2)}) collective-permute-start(bf16[80,512]{1,0:T(8,128)(2,1)S(1)} %get-tuple-element.53), channel_id=1, source_target_pairs={{0,3},{1,0},{2,1},{3,2},{4,7},{5,4},{6,5},{7,6},{8,11},{9,8},{10,9... | collective-permute-start | bytes 245768 | tf_op jit(solution)/shard_map/ppermute | solution.py:364
  134.4 10.5 %collective-permute-start.23 = (bf16[8,80,128]{2,1,0:T(8,128)(2,1)S(1)}, bf16[8,80,128]{2,1,0:T(8,128)(2,1)S(1)}, u32[]{:S(2)}, u32[]{:S(2)}) collective-permute-start(bf16[8,80,128]{2,1,0:T(8,128)(2,1)S(1)} %all_to_all.21.o0), channel_id=1, source_target_pairs={{0,24},{8,0},{16,8},{24,16},{1,25},{9,1},{17,9},{25,17},{2,26},{10... | collective-permute-start | bytes 491528 | tf_op jit(solution)/shard_map/ppermute | solution.py:364
  134.7 11.7 %collective-permute-start.22 = (bf16[8,80,128]{2,1,0:T(8,128)(2,1)S(1)}, bf16[8,80,128]{2,1,0:T(8,128)(2,1)S(1)}, u32[]{:S(2)}, u32[]{:S(2)}) collective-permute-start(bf16[8,80,128]{2,1,0:T(8,128)(2,1)S(1)} %all_to_all.21.o0), channel_id=1, source_target_pairs={{0,16},{8,24},{16,0},{24,8},{1,17},{9,25},{17,1},{25,9},{2,18},{10... | collective-permute-start | bytes 491528 | tf_op jit(solution)/shard_map/ppermute | solution.py:364
  137.3 10.8 %collective-permute-start.21 = (bf16[8,80,128]{2,1,0:T(8,128)(2,1)S(1)}, bf16[8,80,128]{2,1,0:T(8,128)(2,1)S(1)}, u32[]{:S(2)}, u32[]{:S(2)}) collective-permute-start(bf16[8,80,128]{2,1,0:T(8,128)(2,1)S(1)} %all_to_all.21.o0), channel_id=1, source_target_pairs={{0,8},{8,16},{16,24},{24,0},{1,9},{9,17},{17,25},{25,1},{2,10},{10... | collective-permute-start | bytes 491528 | tf_op jit(solution)/shard_map/ppermute | solution.py:364
  137.3 14.1 %collective-permute-start.24 = (bf16[8,80,128]{2,1,0:T(8,128)(2,1)S(1)}, bf16[8,80,128]{2,1,0:T(8,128)(2,1)S(1)}, u32[]{:S(2)}, u32[]{:S(2)}) collective-permute-start(bf16[8,80,128]{2,1,0:T(8,128)(2,1)S(1)} %all_to_all.21.o0), channel_id=1, source_target_pairs={{0,4},{4,0},{1,5},{5,1},{2,6},{6,2},{3,7},{7,3},{8,12},{12,8},{9,1... | collective-permute-start | bytes 491528 | tf_op jit(solution)/shard_map/ppermute | solution.py:364
  144.9 6.5 %collective-permute-start.27 = (bf16[8,80,128]{2,1,0:T(8,128)(2,1)S(1)}, bf16[8,80,128]{2,1,0:T(8,128)(2,1)S(1)}, u32[]{:S(2)}, u32[]{:S(2)}) collective-permute-start(bf16[8,80,128]{2,1,0:T(8,128)(2,1)S(1)} %collective-permute-done.23.o3), channel_id=1, source_target_pairs={{0,4},{4,0},{1,5},{5,1},{2,6},{6,2},{3,7},{7,3},{8,12},{12,8},{9,1... | collective-permute-start | bytes 491528 | tf_op jit(solution)/shard_map/ppermute | solution.py:364
  146.3 5.1 %collective-permute-start.26 = (bf16[8,80,128]{2,1,0:T(8,128)(2,1)S(1)}, bf16[8,80,128]{2,1,0:T(8,128)(2,1)S(1)}, u32[]{:S(2)}, u32[]{:S(2)}) collective-permute-start(bf16[8,80,128]{2,1,0:T(8,128)(2,1)S(1)} %collective-permute-done.22.o2), channel_id=1, source_target_pairs={{0,4},{4,0},{1,5},{5,1},{2,6},{6,2},{3,7},{7,3},{8,12},{12,8},{9,1... | collective-permute-start | bytes 491528 | tf_op jit(solution)/shard_map/ppermute | solution.py:364
  148.2 4.3 %collective-permute-start.25 = (bf16[8,80,128]{2,1,0:T(8,128)(2,1)S(1)}, bf16[8,80,128]{2,1,0:T(8,128)(2,1)S(1)}, u32[]{:S(2)}, u32[]{:S(2)}) collective-permute-start(bf16[8,80,128]{2,1,0:T(8,128)(2,1)S(1)} %collective-permute-done.21.o1), channel_id=1, source_target_pairs={{0,4},{4,0},{1,5},{5,1},{2,6},{6,2},{3,7},{7,3},{8,12},{12,8},{9,1... | collective-permute-start | bytes 491528 | tf_op jit(solution)/shard_map/ppermute | solution.py:364
  (9 other events, 94.5 us)

commit v3 on v2

--- a/solution.py
+++ b/solution.py
@@ -61,23 +61,37 @@
     return (code + b[:1]).astype(jnp.int32)
 
 
-def pack_body(w_in_ref, w_out_ref, pack_ref):
+def entry_body(blocks_hbm, owners_hbm, x_hbm, w_in, w_out, out_ref, pack, blocks, owners, rows, sems):
     half = lax.axis_index("c")
-    pack_ref[:256, :] = w_in_ref[:, pl.ds(pl.multiple_of(half * 1024, 1024), 1024)]
-    wo = w_out_ref[:, pl.ds(pl.multiple_of(half * 512, 512), 512)]
-    pack_ref[256:, :512] = wo[:64]
-    pack_ref[256:, 512:] = wo[64:]
-
-
-def rows_out_body(blocks_ref, owners_ref, x_ref, out_ref):
-    code = slots_of_rows(blocks_ref, owners_ref, 128)
+    wide = pl.ds(pl.multiple_of(half * 1024, 1024), 1024)
+    left = pl.ds(pl.multiple_of(half * 1024 // 2, 512), 512)
+    copies = [
+        pltpu.make_async_copy(a, b, sems.at[i])
+        for i, (a, b) in enumerate(
+            (
+                (blocks_hbm, blocks),
+                (owners_hbm, owners),
+                (x_hbm, rows),
+                (w_in.at[:, wide], pack.at[pl.ds(0, 256), :]),
+                (w_out.at[pl.ds(0, 64), left], pack.at[pl.ds(256, 64), pl.ds(0, 512)]),
+                (w_out.at[pl.ds(64, 64), left], pack.at[pl.ds(256, 64), pl.ds(512, 512)]),
+            )
+        )
+    ]
+    for copy in copies:
+        copy.start()
+    for copy in copies[:3]:
+        copy.wait()
+    code = slots_of_rows(blocks, owners, 128)
     row = iota((1024, 128), 0)
     total = None
     for j in range(4):
         pick = (row == code * 4 + j).astype(F32).astype(BF16)
-        part = dot(pick, x_ref[:, j * 256 : (j + 1) * 256])
+        part = dot(pick, rows[:, j * 256 : (j + 1) * 256])
         total = part if total is None else total + part
     out_ref[...] = total.astype(BF16)
+    for copy in copies[3:]:
+        copy.wait()
 
 
 def rows_back(blocks_ref, owners_ref, returned_ref, out_ref):
@@ -129,6 +143,10 @@
             put(sx, (m + 4 - y) % 4, rows)
 
 
+def order_of(half, sx, sy):
+    return jnp.where(half == 0, sx, sy), jnp.where(half == 0, sy, sx)
+
+
 CHUNK = 32
 
 
@@ -260,15 +278,15 @@
         dpre[1, :, 512 + lo : 512 + hi] = (dk * pre[1, :, 512 + lo : 512 + hi]).astype(BF16)
 
     def put(sx, sy, rows):
-        gother[0, sx, sy] = rows[:, :512]
-        gother[1, sy, sx] = rows[:, 512:]
+        first, second = order_of(1 - c, sx, sy)
+        gother[first, second] = rows
 
     grad_chunks(x, y, 1 - c, nrm, dpre, mix, cot, put)
 
 
 def rest_body(
     nrm, dpre, rstd, cot, w_in, w_out, a1, a2, a3, a4, b1, b2, b3, b4,
-    downed, dnorm,
+    outgoing, dnorm, downed,
 ):
     x, c = lax.axis_index("x"), lax.axis_index("c")
     proj, _ = weights_of(x, c, (w_in, w_out, (a1, a2, a3, a4), (b1, b2, b3, b4)))
@@ -290,19 +308,6 @@
         return 0
 
     lax.fori_loop(0, 256 // CHUNK, unnorm_rows, 0)
-
-def sum_pair_body(nrm, dpre, mix, cot, downed, gfrom, *refs):
-    outs, outgoing, held = refs[:8], refs[8], refs[9]
-    x, y, c = lax.axis_index("x"), lax.axis_index("y"), lax.axis_index("c")
-
-    def put(sx, sy, rows):
-        rows = rows.astype(F32)
-        outs[sx][sy] = (rows[:, :512] + gfrom[0, sx, sy].astype(F32)).astype(BF16)
-        held[sy, sx] = (rows[:, 512:] + gfrom[1, sy, sx].astype(F32)).astype(BF16)
-
-    grad_chunks(x, y, c, nrm, dpre, mix, cot, put)
-    for sy in range(4):
-        outs[4 + sy][...] = held[sy]
     t = iota((1024, 256), 1)
     wanted = (t & 63) * 16 + (t >> 6) * 4
     row = iota((1024, 256), 0)
@@ -313,25 +318,42 @@
         total = part if total is None else total + part
     outgoing[...] = total.astype(BF16)
 
-
-def add_four_body(a0, a1, a2, a3, b0, b1, b2, b3, blocks, owners, returned, rows, *outs):
-    rows_back(blocks, owners, returned, rows)
-    for color, refs in enumerate(((a0, a1, a2, a3), (b0, b1, b2, b3))):
-        for s in range(4):
-            total = refs[0][s].astype(F32)
-            for ref in refs[1:]:
-                total = total + ref[s].astype(F32)
-            outs[color * 4 + s][...] = total.astype(BF16)
-
-
-def add_last_body(a0, a1, a2, a3, b0, b1, b2, b3, out):
-    for color, refs in enumerate(((a0, a1, a2, a3), (b0, b1, b2, b3))):
-        total = refs[0][...].astype(F32)
-        for ref in refs[1:]:
-            total = total + ref[...].astype(F32)
-        total = total.astype(BF16)
-        for j in range(4):
-            out[color * 4 + j] = total[:, j * 128 : (j + 1) * 128]
+def sum_pair_body(nrm, dpre, mix, cot, gfrom, backward, ahead, behind, kept, held):
+    x, y, c = lax.axis_index("x"), lax.axis_index("y"), lax.axis_index("c")
+
+    def put(sx, sy, rows):
+        first, second = order_of(c, sx, sy)
+        held[first, second] = (rows.astype(F32) + gfrom[first, second].astype(F32)).astype(BF16)
+
+    grad_chunks(x, y, c, nrm, dpre, mix, cot, put)
+    ahead[0] = held[2, :2]
+    ahead[1] = held[1, 2:]
+    behind[0] = held[2, 2:]
+    behind[1] = held[3, :2]
+    kept[:4] = held[0]
+    kept[4:6] = held[1, :2]
+    kept[6:] = held[3, 2:]
+
+
+def add_relayed_body(kept, ahead, behind, forth, back):
+    forth[...] = (kept[4:6].astype(F32) + ahead[0].astype(F32)).astype(BF16)
+    back[...] = (kept[6:].astype(F32) + behind[0].astype(F32)).astype(BF16)
+
+
+def add_four_body(kept, ahead, behind, forth, back, *outs):
+    for s in range(4):
+        if s < 2:
+            total = kept[s].astype(F32) + behind[1, s].astype(F32) + forth[s].astype(F32)
+        else:
+            total = kept[s].astype(F32) + ahead[1, s - 2].astype(F32) + back[s - 2].astype(F32)
+        outs[s][...] = total.astype(BF16)
+
+
+def add_last_body(a0, a1, a2, a3, out):
+    total = a0[...].astype(F32) + a1[...].astype(F32) + a2[...].astype(F32) + a3[...].astype(F32)
+    total = total.astype(BF16)
+    for j in range(8):
+        out[j] = total[:, j * 128 : (j + 1) * 128]
 
 
 def add_eight_body(parts, out):
@@ -364,13 +386,40 @@
     return lax.ppermute(a, axis, [(i, (i + s) % n) for i in range(n)])
 
 
+def crossed(a, s, first):
+    pairs = []
+    for z in range(8):
+        for y in range(4):
+            for c in range(2):
+                for x in range(4):
+                    over_x = (c == 0) == first
+                    ty, tx = (y, (x + s) % 4) if over_x else ((y + s) % 4, x)
+                    at = lambda v, w: ((z * 4 + v) * 2 + c) * 4 + w
+                    pairs.append((at(y, x), at(ty, tx)))
+    return lax.ppermute(a, ("z", "y", "c", "x"), pairs)
+
+
 def on_device(x_rows, cotangent, w_in, w_out, hist_blocks, owner):
     cot = cotangent[0]
-    (pack,) = call(pack_body, [((320, 1024), BF16)], (w_in, w_out), "pack")
+    hbm = pl.BlockSpec(memory_space=pltpu.HBM)
+    outgoing, pack = pl.pallas_call(
+        entry_body,
+        out_shape=[
+            jax.ShapeDtypeStruct((1024, 256), BF16),
+            jax.ShapeDtypeStruct((320, 1024), BF16),
+        ],
+        in_specs=[hbm] * 5,
+        out_specs=[pl.BlockSpec(memory_space=pltpu.VMEM)] * 2,
+        scratch_shapes=[
+            pltpu.VMEM((1, 64), jnp.int32),
+            pltpu.VMEM((1, 64), jnp.int32),
+            pltpu.VMEM((128, 1024), BF16),
+            pltpu.SemaphoreType.DMA((6,)),
+        ],
+        compiler_params=pltpu.CompilerParams(vmem_limit_bytes=60 * 1024 * 1024),
+        name="entry",
+    )(hist_blocks, owner, x_rows[0], w_in, w_out)
     left, right = shift(pack, "x", 4, 1), shift(pack, "x", 4, 3)
-    (outgoing,) = call(
-        rows_out_body, [((1024, 256), BF16)], (hist_blocks, owner, x_rows[0]), "rows_out"
-    )
     arrived = lax.all_to_all(
         outgoing.reshape(64, 16, 256), DP, split_axis=0, concat_axis=0, tiled=True
     ).reshape(1024, 256)
@@ -380,7 +429,7 @@
         layer_body,
         [
             ((256, 1024), BF16),
-            ((2, 4, 4, 80, 512), BF16),
+            ((4, 4, 80, 1024), BF16),
             ((4, 256, 256), BF16),
             ((2, 256, 1024), BF16),
             ((4, 256, 128), BF16),
@@ -401,34 +450,38 @@
         ],
     )
     gfrom = shift(gother, "c", 2, 1)
-    (downed,) = call(
+    (backward,) = call(
         rest_body,
-        [((256, 1024), BF16)],
+        [((1024, 256), BF16)],
         (nrm, dpre, rstd, cot) + weights,
         "rest",
-        scratch=[((4, 256, 256), BF16)],
-    )
-    *big, backward = call(
+        scratch=[((4, 256, 256), BF16), ((256, 1024), BF16)],
+    )
+    ahead, behind, kept = call(
         sum_pair_body,
-        [((4, 80, 512), BF16)] * 8 + [((1024, 256), BF16)],
-        (nrm, dpre, mix, cot, downed, gfrom),
+        [((2, 2, 80, 1024), BF16), ((2, 2, 80, 1024), BF16), ((8, 80, 1024), BF16)],
+        (nrm, dpre, mix, cot, gfrom, backward),
         "sum_pair",
-        scratch=[((4, 4, 80, 512), BF16)],
-    )
-    first = [big[0]] + [shift(big[s], "x", 4, s) for s in (1, 2, 3)]
-    second = [big[4]] + [shift(big[4 + s], "y", 4, s) for s in (1, 2, 3)]
+        scratch=[((4, 4, 80, 1024), BF16)],
+    )
+    backward, kept = lax.optimization_barrier((backward, kept))
+    ahead, behind = crossed(ahead, 1, True), crossed(behind, 3, True)
     returned = lax.all_to_all(
         backward.reshape(64, 16, 256), DP, split_axis=0, concat_axis=0, tiled=True
     ).reshape(1024, 256)
-    grad_rows, *mid = call(
-        add_four_body,
-        [((128, 1024), BF16)] + [((80, 512), BF16)] * 8,
-        (*first, *second, hist_blocks, owner, returned),
-        "add_four",
-    )
-    first = [mid[0]] + [shift(mid[s], "y", 4, s) for s in (1, 2, 3)]
-    second = [mid[4]] + [shift(mid[4 + s], "x", 4, s) for s in (1, 2, 3)]
-    (columns,) = call(add_last_body, [((8, 80, 128), BF16)], (*first, *second), "add_last")
+    forth, back = call(
+        add_relayed_body, [((2, 80, 1024), BF16)] * 2, (kept, ahead, behind), "add_relayed"
+    )
+    forth, back = crossed(forth, 1, True), crossed(back, 3, True)
+    mid = call(
+        add_four_body, [((80, 1024), BF16)] * 4, (kept, ahead, behind, forth, back), "add_four"
+    )
+    second = [mid[0]] + [crossed(mid[s], s, False) for s in (1, 2, 3)]
+    returned, second[1] = lax.optimization_barrier((returned, second[1]))
+    (columns,) = call(add_last_body, [((8, 80, 128), BF16)], second, "add_last")
+    (grad_rows,) = call(
+        rows_back, [((128, 1024), BF16)], (hist_blocks, owner, returned), "rows_back"
+    )
     parts = lax.all_to_all(columns, "z", split_axis=0, concat_axis=0, tiled=True)
     (summed,) = call(add_eight_body, [((8, 80, 128), BF16)], (parts,), "add_eight")
     mine = lax.all_to_all(summed, "z", split_axis=0, concat_axis=0, tiled=True)

time: 155 us -> 140 us (0.903)
  waiting for transfers between devices: 32.7 us -> 20.1 us
  starting transfers between devices: 65.5 us -> 59.1 us
  local copies, waits for them, and re-layouts: 5.44 us -> 0.07 us
  Pallas kernels: 24.7 us -> 29.3 us
  blocking collectives: 25.2 us -> 29.7 us
    ppermute x28 -> x16, waiting for transfers between devices: 29.7 us -> 5.51 us  [shift(): return lax.ppermute(a, axis, [(i, (i + s) % n) for i in range(n)])]
    ppermute x28 -> x16, starting transfers between devices: 43.9 us -> 25.8 us  [shift(): return lax.ppermute(a, axis, [(i, (i + s) % n) for i in range(n)])]
    ppermute x0 -> x7, waiting for transfers between devices: none -> 9 us  [crossed(): return lax.ppermute(a, ('z', 'y', 'c', 'x'), pairs)]
    ppermute x0 -> x7, starting transfers between devices: none -> 8.34 us  [crossed(): return lax.ppermute(a, ('z', 'y', 'c', 'x'), pairs)]
    unnamed x22 -> x10, local copies, waits for them, and re-layouts: 5.39 us -> 0.02 us
    all_to_all x1, waiting for transfers between devices: 0.01 us -> 3.84 us  [on_device(): lax.all_to_all(backward.reshape(64, 16, 256), DP, split_axis=0, concat_ax...]
    all_to_all x1, starting transfers between devices: 8.84 us -> 12.2 us  [on_device(): lax.all_to_all(backward.reshape(64, 16, 256), DP, split_axis=0, concat_ax...]
    pallas_call x0 -> x1, Pallas kernels: none -> 3.04 us  [on_device(): pl.pallas_call(entry_body, out_shape=[jax.ShapeDtypeStruct((1024, 256), B...]
  transfers between devices with their start and end apart: 30 -> 25, of which waited for: 14 -> 10; matrix products, arithmetic and copies ran while one was open for 0% -> 0% of each run, Pallas kernels for 4% -> 6%
where the time goes in v3:
time: 140 us; the launch traced here: 139 us
  starting transfers between devices  59.1 us (42%)
  blocking collectives  29.7 us (21%)
  Pallas kernels  29.3 us (21%)
  waiting for transfers between devices  20.1 us (14%)
    pallas_call x9, Pallas kernels, call(): pl.pallas_call(body, out_shape=[jax.ShapeDtypeStruct(s, d) for s, d in ou...  26.3 us
    ppermute x16, starting transfers between devices, shift(): return lax.ppermute(a, axis, [(i, (i + s) % n) for i in range(n)])  25.8 us
    all_to_all x1, blocking collectives, on_device(): lax.all_to_all(columns, 'z', split_axis=0, concat_axis=0, tiled=True)  17 us
    all_to_all x1, starting transfers between devices, on_device(): lax.all_to_all(outgoing.reshape(64, 16, 256), DP, split_axis=0, concat_ax...  12.8 us
    all_to_all x1, blocking collectives, on_device(): mine = lax.all_to_all(summed, 'z', split_axis=0, concat_axis=0, tiled=True)  12.7 us
    all_to_all x1, starting transfers between devices, on_device(): lax.all_to_all(backward.reshape(64, 16, 256), DP, split_axis=0, concat_ax...  12.2 us
    ppermute x7, waiting for transfers between devices, crossed(): return lax.ppermute(a, ('z', 'y', 'c', 'x'), pairs)  9 us
    ppermute x7, starting transfers between devices, crossed(): return lax.ppermute(a, ('z', 'y', 'c', 'x'), pairs)  8.34 us
  transfers between devices with their start and end apart: 25, of which 10 were waited for; matrix products, arithmetic and copies ran while one was open for 0% of the time, Pallas kernels for 6%

profile of v3, /device:TPU:1, one launch (start us, length us, event | category | flops | bytes accessed | tf_op | source)
XLA Modules:
  0.0 139.1 jit_solution(2332288645412044196)
XLA Ops:
  0.7 3.0 %entry.1 = (bf16[1024,256]{1,0:T(8,128)(2,1)}, bf16[320,1024]{1,0:T(8,128)(2,1)}) custom-call(s32[1,64]{1,0:T(1,128)} %blocks_ref.3, s32[1,64]{1,0:T(1,128)} %owners_ref.3, bf16[128,1024]{1,0:T(8,128)(2,1)} %bitcast.14, bf16[256,2048]{1,0:T(8,128)(2,1)} %w_in.5, bf16[128,1024]{1,0:T(8,128)(2,1)} %w_out.5), custom_call_target="tpu_custom_call" | custom-call | tf_op jit(solution)/shard_map/entry/pallas_call | solution.py:405
  3.7 3.4 %collective-permute-start.1 = (bf16[320,1024]{1,0:T(8,128)(2,1)}, bf16[320,1024]{1,0:T(8,128)(2,1)S(1)}, u32[]{:S(2)}, u32[]{:S(2)}) collective-permute-start(bf16[320,1024]{1,0:T(8,128)(2,1)} %get-tuple-element.28), channel_id=1, source_target_pairs={{0,3},{1,0},{2,1},{3,2},{4,7},{5,4},{6,5},{7,6},{8,11},{9,8},{10,9... | collective-permute-start | bytes 1966088 | tf_op jit(solution)/shard_map/ppermute | solution.py:386
  7.1 12.8 %all-to-all-start = ((bf16[64,16,256]{2,1,0:T(8,128)(2,1)}), bf16[64,16,256]{2,1,0:T(8,128)(2,1)}, u32[]{:S(2)}, u32[]{:S(2)}) async-start(bf16[64,16,256]{2,1,0:T(8,128)(2,1)} %bitcast.12), calls=%async_computation | async-start | bytes 1048576 | tf_op jit(solution)/shard_map/all_to_all | solution.py:423
  19.9 0.9 collective-permute-done.1.a2
  20.9 3.4 %collective-permute-start.3 = (bf16[160,1024]{1,0:T(8,128)(2,1)S(1)}, bf16[160,1024]{1,0:T(8,128)(2,1)S(1)}, u32[]{:S(2)}, u32[]{:S(2)}) collective-permute-start(bf16[160,1024]{1,0:T(8,128)(2,1)S(1)} %slice.9), channel_id=1, source_target_pairs={{0,3},{1,0},{2,1},{3,2},{4,7},{5,4},{6,5},{7,6},{8,11},{9,8},{10,9... | collective-permute-start | bytes 983048 | tf_op jit(solution)/shard_map/ppermute | solution.py:386
  24.4 1.9 %collective-permute-start.5 = (bf16[320,1024]{1,0:T(8,128)(2,1)S(1)}, bf16[320,1024]{1,0:T(8,128)(2,1)}, u32[]{:S(2)}, u32[]{:S(2)}) collective-permute-start(bf16[320,1024]{1,0:T(8,128)(2,1)S(1)} %collective-permute-done.1.a2), channel_id=1, source_target_pairs={{0,4},{4,0},{1,5},{5,1},{2,6},{6,2},{3,7},{7,3},{8,12},{12,8},{9,1... | collective-permute-start | bytes 1966088 | tf_op jit(solution)/shard_map/ppermute | solution.py:386
  26.4 3.3 %collective-permute-done.3.a4 = bf16[160,1024]{1,0:T(8,128)(2,1)S(1)} collective-permute-done((bf16[160,1024]{1,0:T(8,128)(2,1)S(1)}, bf16[160,1024]{1,0:T(8,128)(2,1)S(1)}, u32[]{:S(2)}, u32[]{:S(2)}) %collective-permute-start.3) | collective-permute-done | bytes 327712 | tf_op jit(solution)/shard_map/ppermute | solution.py:386
  29.7 2.5 %collective-permute-start.7 = (bf16[160,1024]{1,0:T(8,128)(2,1)S(1)}, bf16[160,1024]{1,0:T(8,128)(2,1)}, u32[]{:S(2)}, u32[]{:S(2)}) collective-permute-start(bf16[160,1024]{1,0:T(8,128)(2,1)S(1)} %collective-permute-done.3.a4), channel_id=1, source_target_pairs={{0,4},{4,0},{1,5},{5,1},{2,6},{6,2},{3,7},{7,3},{8,12},{12,8},{9,1... | collective-permute-start | bytes 983048 | tf_op jit(solution)/shard_map/ppermute | solution.py:386
  33.0 2.7 %collective-permute-start.6 = (bf16[160,1024]{1,0:T(8,128)(2,1)}, bf16[160,1024]{1,0:T(8,128)(2,1)}, u32[]{:S(2)}, u32[]{:S(2)}) collective-permute-start(bf16[160,1024]{1,0:T(8,128)(2,1)} %collective-permute-done.2.a3), channel_id=1, source_target_pairs={{0,4},{4,0},{1,5},{5,1},{2,6},{6,2},{3,7},{7,3},{8,12},{12,8},{9,1... | collective-permute-start | bytes 983048 | tf_op jit(solution)/shard_map/ppermute | solution.py:386
  35.8 1.8 %all-to-all-done = bf16[64,16,256]{2,1,0:T(8,128)(2,1)} async-done(((bf16[64,16,256]{2,1,0:T(8,128)(2,1)}), bf16[64,16,256]{2,1,0:T(8,128)(2,1)}, u32[]{:S(2)}, u32[]{:S(2)}) %all-to-all-start) | async-done | bytes 524320 | tf_op jit(solution)/shard_map/all_to_all | solution.py:423
  37.6 13.0 %layer.1 = (bf16[256,1024]{1,0:T(8,128)(2,1)}, bf16[4,4,80,1024]{3,2,1,0:T(8,128)(2,1)S(1)}, bf16[4,256,256]{2,1,0:T(8,128)(2,1)S(1)}, bf16[2,256,1024]{2,1,0:T(...) custom-call(s32[1,64]{1,0:T(1,128)S(1)} %copy-done.3, s32[1,64]{1,0:T(1,128)S(1)} %copy-done.4, ...), custom_call_target="tpu_custom_call" | custom-call | tf_op jit(solution)/shard_map/layer/pallas_call | solution.py:30
  51.0 5.5 %rest.1.backward = bf16[1024,256]{1,0:T(8,128)(2,1)} custom-call(bf16[4,256,256]{2,1,0:T(8,128)(2,1)S(1)} %get-tuple-element.30.nrm, bf16[2,256,1024]{2,1,0:T(8,128)(2,1)S(1)} %get-tuple-element.31.dpre, f32[256,128]{1,0:T(8,128)S(1)} %get-tuple-element.32.rstd, bf16[256,1024]{1,0:T(8,128)(2,1)S(1)} %bitcast.9, bf16[256,2048]{1,0:T(8,128)(2,1)S(1)} %copy-done, ...), custom_call_target="tpu_custom_call" | custom-call | tf_op jit(solution)/shard_map/rest/pallas_call | solution.py:30
  56.5 3.2 %sum_pair.1 = (bf16[2,2,80,1024]{3,2,1,0:T(8,128)(2,1)}, bf16[2,2,80,1024]{3,2,1,0:T(8,128)(2,1)}, bf16[8,80,1024]{2,1,0:T(8,128)(2,1)S(1)}) custom-call(bf16[4,256,256]{2,1,0:T(8,128)(2,1)S(1)} %get-tuple-element.30.nrm, bf16[2,256,1024]{2,1,0:T(8,128)(2,1)S(1)} %get-tuple-element.31.dpre, bf16[4,256,128]{2,1,0:T(8,128)(2,1)S(1)} %get-tuple-element.33.mix, ...), custom_call_target="tpu_custom_call" | custom-call | tf_op jit(solution)/shard_map/sum_pair/pallas_call | solution.py:30
  59.7 1.2 collective-permute-start.9
  60.9 1.5 %collective-permute-start.10 = (bf16[2,2,80,1024]{3,2,1,0:T(8,128)(2,1)}, bf16[2,2,80,1024]{3,2,1,0:T(8,128)(2,1)S(1)}, u32[]{:S(2)}, u32[]{:S(2)}) collective-permute-start(bf16[2,2,80,1024]{3,2,1,0:T(8,128)(2,1)} %get-tuple-element.39), channel_id=1, source_target_pairs={{0,3},{1,0},{2,1},{3,2},{4,28},{5,29},{6,30},{7,31},{8,11},{9,8},{... | collective-permute-start | bytes 1966088 | tf_op jit(solution)/shard_map/ppermute | solution.py:399
  62.4 12.2 %all-to-all-start.1 = ((bf16[64,16,256]{2,1,0:T(8,128)(2,1)}), bf16[64,16,256]{2,1,0:T(8,128)(2,1)S(1)}, u32[]{:S(2)}, u32[]{:S(2)}) async-start(bf16[64,16,256]{2,1,0:T(8,128)(2,1)} %bitcast.5), calls=%async_computation.1 | async-start | bytes 1048576 | tf_op jit(solution)/shard_map/all_to_all | solution.py:469
  74.8 1.5 %collective-permute-start.11 = (bf16[2,80,1024]{2,1,0:T(8,128)(2,1)S(1)}, bf16[2,80,1024]{2,1,0:T(8,128)(2,1)S(1)}, u32[]{:S(2)}, u32[]{:S(2)}) collective-permute-start(bf16[2,80,1024]{2,1,0:T(8,128)(2,1)S(1)} %get-tuple-element.40), channel_id=1, source_target_pairs={{0,1},{1,2},{2,3},{3,0},{4,12},{5,13},{6,14},{7,15},{8,9},{9,10},{... | collective-permute-start | bytes 983048 | tf_op jit(solution)/shard_map/ppermute | solution.py:399
  76.2 1.5 %collective-permute-start.12 = (bf16[2,80,1024]{2,1,0:T(8,128)(2,1)S(1)}, bf16[2,80,1024]{2,1,0:T(8,128)(2,1)S(1)}, u32[]{:S(2)}, u32[]{:S(2)}) collective-permute-start(bf16[2,80,1024]{2,1,0:T(8,128)(2,1)S(1)} %get-tuple-element.41), channel_id=1, source_target_pairs={{0,3},{1,0},{2,1},{3,2},{4,28},{5,29},{6,30},{7,31},{8,11},{9,8},{... | collective-permute-start | bytes 983048 | tf_op jit(solution)/shard_map/ppermute | solution.py:399
  77.8 6.7 %collective-permute-done.11.forth = bf16[2,80,1024]{2,1,0:T(8,128)(2,1)S(1)} collective-permute-done((bf16[2,80,1024]{2,1,0:T(8,128)(2,1)S(1)}, bf16[2,80,1024]{2,1,0:T(8,128)(2,1)S(1)}, u32[]{:S(2)}, u32[]{:S(2)}) %collective-permute-start.11) | collective-permute-done | bytes 327712 | tf_op jit(solution)/shard_map/ppermute | solution.py:399
  85.9 0.9 collective-permute-start.14
  86.8 1.8 %collective-permute-start.15 = (bf16[80,1024]{1,0:T(8,128)(2,1)S(1)}, bf16[80,1024]{1,0:T(8,128)(2,1)S(1)}, u32[]{:S(2)}, u32[]{:S(2)}) collective-permute-start(bf16[80,1024]{1,0:T(8,128)(2,1)S(1)} %get-tuple-element.47), channel_id=1, source_target_pairs={{0,24},{1,25},{2,26},{3,27},{4,7},{5,4},{6,5},{7,6},{8,0},{9,1},{1... | collective-permute-start | bytes 491528 | tf_op jit(solution)/shard_map/ppermute | solution.py:399
  88.6 3.8 %all-to-all-done.1 = bf16[64,16,256]{2,1,0:T(8,128)(2,1)S(1)} async-done(((bf16[64,16,256]{2,1,0:T(8,128)(2,1)}), bf16[64,16,256]{2,1,0:T(8,128)(2,1)S(1)}, u32[]{:S(2)}, u32[]{:S(2)}) %all-to-all-start.1) | async-done | bytes 524320 | tf_op jit(solution)/shard_map/all_to_all | solution.py:469
  92.4 1.1 collective-permute-done.13.a1
  94.3 17.0 %all_to_all.20.parts = bf16[8,80,128]{2,1,0:T(8,128)(2,1)S(1)} all-to-all(bf16[8,80,128]{2,1,0:T(8,128)(2,1)S(1)} %add_last.1), channel_id=1, replica_groups=mesh['z'=8,'y'=4,'c'=2,'x'=4] {'z'}, dimensions={0} | all-to-all | bytes 327680 | tf_op jit(solution)/shard_map/all_to_all | solution.py:485
  111.3 12.7 %all_to_all.21.o0 = bf16[8,80,128]{2,1,0:T(8,128)(2,1)S(1)} all-to-all(bf16[8,80,128]{2,1,0:T(8,128)(2,1)S(1)} %add_eight.1), channel_id=1, replica_groups=mesh['z'=8,'y'=4,'c'=2,'x'=4] {'z'}, dimensions={0} | all-to-all | bytes 327680 | tf_op jit(solution)/shard_map/all_to_all | solution.py:487
  123.9 1.9 %collective-permute-start.17 = (bf16[8,80,128]{2,1,0:T(8,128)(2,1)S(1)}, bf16[8,80,128]{2,1,0:T(8,128)(2,1)S(1)}, u32[]{:S(2)}, u32[]{:S(2)}) collective-permute-start(bf16[8,80,128]{2,1,0:T(8,128)(2,1)S(1)} %all_to_all.21.o0), channel_id=1, source_target_pairs={{0,16},{8,24},{16,0},{24,8},{1,17},{9,25},{17,1},{25,9},{2,18},{10... | collective-permute-start | bytes 491528 | tf_op jit(solution)/shard_map/ppermute | solution.py:386
  126.4 2.5 %collective-permute-start.19 = (bf16[8,80,128]{2,1,0:T(8,128)(2,1)S(1)}, bf16[8,80,128]{2,1,0:T(8,128)(2,1)S(1)}, u32[]{:S(2)}, u32[]{:S(2)}) collective-permute-start(bf16[8,80,128]{2,1,0:T(8,128)(2,1)S(1)} %all_to_all.21.o0), channel_id=1, source_target_pairs={{0,4},{4,0},{1,5},{5,1},{2,6},{6,2},{3,7},{7,3},{8,12},{12,8},{9,1... | collective-permute-start | bytes 491528 | tf_op jit(solution)/shard_map/ppermute | solution.py:386
  129.3 2.1 %collective-permute-start.22 = (bf16[8,80,128]{2,1,0:T(8,128)(2,1)S(1)}, bf16[8,80,128]{2,1,0:T(8,128)(2,1)S(1)}, u32[]{:S(2)}, u32[]{:S(2)}) collective-permute-start(bf16[8,80,128]{2,1,0:T(8,128)(2,1)S(1)} %collective-permute-done.18.o3), channel_id=1, source_target_pairs={{0,4},{4,0},{1,5},{5,1},{2,6},{6,2},{3,7},{7,3},{8,12},{12,8},{9,1... | collective-permute-start | bytes 491528 | tf_op jit(solution)/shard_map/ppermute | solution.py:386
  131.4 2.7 %collective-permute-start.21 = (bf16[8,80,128]{2,1,0:T(8,128)(2,1)S(1)}, bf16[8,80,128]{2,1,0:T(8,128)(2,1)S(1)}, u32[]{:S(2)}, u32[]{:S(2)}) collective-permute-start(bf16[8,80,128]{2,1,0:T(8,128)(2,1)S(1)} %collective-permute-done.17.o2), channel_id=1, source_target_pairs={{0,4},{4,0},{1,5},{5,1},{2,6},{6,2},{3,7},{7,3},{8,12},{12,8},{9,1... | collective-permute-start | bytes 491528 | tf_op jit(solution)/shard_map/ppermute | solution.py:386
  134.2 1.4 %collective-permute-start.20 = (bf16[8,80,128]{2,1,0:T(8,128)(2,1)S(1)}, bf16[8,80,128]{2,1,0:T(8,128)(2,1)S(1)}, u32[]{:S(2)}, u32[]{:S(2)}) collective-permute-start(bf16[8,80,128]{2,1,0:T(8,128)(2,1)S(1)} %collective-permute-done.16.o1), channel_id=1, source_target_pairs={{0,4},{4,0},{1,5},{5,1},{2,6},{6,2},{3,7},{7,3},{8,12},{12,8},{9,1... | collective-permute-start | bytes 491528 | tf_op jit(solution)/shard_map/ppermute | solution.py:386
  135.6 1.5 %rows_back.1 = bf16[128,1024]{1,0:T(8,128)(2,1)} custom-call(s32[1,64]{1,0:T(1,128)S(1)} %copy-done.3, s32[1,64]{1,0:T(1,128)S(1)} %copy-done.4, bf16[1024,256]{1,0:T(8,128)(2,1)S(1)} %bitcast.11), custom_call_target="tpu_custom_call" | custom-call | tf_op jit(solution)/shard_map/rows_back/pallas_call | solution.py:30
  137.1 2.0 %place.1 = (f32[256,2048]{1,0:T(8,128)}, f32[128,1024]{1,0:T(8,128)}) custom-call(bf16[8,80,128]{2,1,0:T(8,128)(2,1)S(1)} %all_to_all.21.o0, bf16[8,80,128]{2,1,0:T(8,128)(2,1)S(1)} %collective-permute-done.16.o1, bf16[8,80,128]{2,1,0:T(8,128)(2,1)S(1)} %collective-permute-done.17.o2, bf16[8,80,128]{2,1,0:T(8,128)(2,1)S(1)} %collective-permute-done.18.o3, ...), custom_call_target="tpu_custom_call" | custom-call | tf_op jit(solution)/shard_map/place/pallas_call | solution.py:30
  (42 shorter events, 4.9 us)
Async XLA Ops:
  0.6 36.9 %copy-start.4 = (s32[1,64]{1,0:T(1,128)S(1)}, s32[1,64]{1,0:T(1,128)}, u32[]{:S(2)}) copy-start(s32[1,64]{1,0:T(1,128)} %owners_ref.3) | copy-start | bytes 772
  0.6 36.9 %copy-start.3 = (s32[1,64]{1,0:T(1,128)S(1)}, s32[1,64]{1,0:T(1,128)}, u32[]{:S(2)}) copy-start(s32[1,64]{1,0:T(1,128)} %blocks_ref.3) | copy-start | bytes 772
  0.7 36.9 %copy-start.2 = (bf16[128,1024]{1,0:T(8,128)(2,1)S(1)}, bf16[128,1024]{1,0:T(8,128)(2,1)}, u32[]{:S(2)}) copy-start(bf16[128,1024]{1,0:T(8,128)(2,1)} %w_out.5) | copy-start | bytes 786436
  0.7 36.9 %copy-start = (bf16[256,2048]{1,0:T(8,128)(2,1)S(1)}, bf16[256,2048]{1,0:T(8,128)(2,1)}, u32[]{:S(2)}) copy-start(bf16[256,2048]{1,0:T(8,128)(2,1)} %w_in.5) | copy-start | bytes 3145732
  0.7 36.9 %copy-start.1 = (bf16[1,256,1024]{2,1,0:T(8,128)(2,1)S(1)}, bf16[1,256,1024]{2,1,0:T(8,128)(2,1)}, u32[]{:S(2)}) copy-start(bf16[1,256,1024]{2,1,0:T(8,128)(2,1)} %param.7) | copy-start | bytes 1572868
  3.7 17.1 %collective-permute-start.1 = (bf16[320,1024]{1,0:T(8,128)(2,1)}, bf16[320,1024]{1,0:T(8,128)(2,1)S(1)}, u32[]{:S(2)}, u32[]{:S(2)}) collective-permute-start(bf16[320,1024]{1,0:T(8,128)(2,1)} %get-tuple-element.28), channel_id=1, source_target_pairs={{0,3},{1,0},{2,1},{3,2},{4,7},{5,4},{6,5},{7,6},{8,11},{9,8},{10,9... | collective-permute-start | bytes 1966088 | tf_op jit(solution)/shard_map/ppermute | solution.py:386
  7.1 17.1 %collective-permute-start = (bf16[320,1024]{1,0:T(8,128)(2,1)}, bf16[320,1024]{1,0:T(8,128)(2,1)S(1)}, u32[]{:S(2)}, u32[]{:S(2)}) collective-permute-start(bf16[320,1024]{1,0:T(8,128)(2,1)} %get-tuple-element.28), channel_id=1, source_target_pairs={{0,1},{1,2},{2,3},{3,0},{4,5},{5,6},{6,7},{7,4},{8,9},{9,10},{10,1... | collective-permute-start | bytes 1966088 | tf_op jit(solution)/shard_map/ppermute | solution.py:386
  7.1 30.4 %all-to-all-start = ((bf16[64,16,256]{2,1,0:T(8,128)(2,1)}), bf16[64,16,256]{2,1,0:T(8,128)(2,1)}, u32[]{:S(2)}, u32[]{:S(2)}) async-start(bf16[64,16,256]{2,1,0:T(8,128)(2,1)} %bitcast.12), calls=%async_computation | async-start | bytes 1048576 | tf_op jit(solution)/shard_map/all_to_all | solution.py:423
  20.9 8.8 %collective-permute-start.3 = (bf16[160,1024]{1,0:T(8,128)(2,1)S(1)}, bf16[160,1024]{1,0:T(8,128)(2,1)S(1)}, u32[]{:S(2)}, u32[]{:S(2)}) collective-permute-start(bf16[160,1024]{1,0:T(8,128)(2,1)S(1)} %slice.9), channel_id=1, source_target_pairs={{0,3},{1,0},{2,1},{3,2},{4,7},{5,4},{6,5},{7,6},{8,11},{9,8},{10,9... | collective-permute-start | bytes 983048 | tf_op jit(solution)/shard_map/ppermute | solution.py:386
  24.3 8.8 %collective-permute-start.2 = (bf16[160,1024]{1,0:T(8,128)(2,1)S(1)}, bf16[160,1024]{1,0:T(8,128)(2,1)}, u32[]{:S(2)}, u32[]{:S(2)}) collective-permute-start(bf16[160,1024]{1,0:T(8,128)(2,1)S(1)} %slice.8), channel_id=1, source_target_pairs={{0,1},{1,2},{2,3},{3,0},{4,5},{5,6},{6,7},{7,4},{8,9},{9,10},{10,1... | collective-permute-start | bytes 983048 | tf_op jit(solution)/shard_map/ppermute | solution.py:386
  24.4 13.2 %collective-permute-start.5 = (bf16[320,1024]{1,0:T(8,128)(2,1)S(1)}, bf16[320,1024]{1,0:T(8,128)(2,1)}, u32[]{:S(2)}, u32[]{:S(2)}) collective-permute-start(bf16[320,1024]{1,0:T(8,128)(2,1)S(1)} %collective-permute-done.1.a2), channel_id=1, source_target_pairs={{0,4},{4,0},{1,5},{5,1},{2,6},{6,2},{3,7},{7,3},{8,12},{12,8},{9,1... | collective-permute-start | bytes 1966088 | tf_op jit(solution)/shard_map/ppermute | solution.py:386
  26.3 11.3 %collective-permute-start.4 = (bf16[320,1024]{1,0:T(8,128)(2,1)S(1)}, bf16[320,1024]{1,0:T(8,128)(2,1)}, u32[]{:S(2)}, u32[]{:S(2)}) collective-permute-start(bf16[320,1024]{1,0:T(8,128)(2,1)S(1)} %collective-permute-done.a1), channel_id=1, source_target_pairs={{0,4},{4,0},{1,5},{5,1},{2,6},{6,2},{3,7},{7,3},{8,12},{12,8},{9,1... | collective-permute-start | bytes 1966088 | tf_op jit(solution)/shard_map/ppermute | solution.py:386
  29.7 7.9 %collective-permute-start.7 = (bf16[160,1024]{1,0:T(8,128)(2,1)S(1)}, bf16[160,1024]{1,0:T(8,128)(2,1)}, u32[]{:S(2)}, u32[]{:S(2)}) collective-permute-start(bf16[160,1024]{1,0:T(8,128)(2,1)S(1)} %collective-permute-done.3.a4), channel_id=1, source_target_pairs={{0,4},{4,0},{1,5},{5,1},{2,6},{6,2},{3,7},{7,3},{8,12},{12,8},{9,1... | collective-permute-start | bytes 983048 | tf_op jit(solution)/shard_map/ppermute | solution.py:386
  33.0 4.5 %collective-permute-start.6 = (bf16[160,1024]{1,0:T(8,128)(2,1)}, bf16[160,1024]{1,0:T(8,128)(2,1)}, u32[]{:S(2)}, u32[]{:S(2)}) collective-permute-start(bf16[160,1024]{1,0:T(8,128)(2,1)} %collective-permute-done.2.a3), channel_id=1, source_target_pairs={{0,4},{4,0},{1,5},{5,1},{2,6},{6,2},{3,7},{7,3},{8,12},{12,8},{9,1... | collective-permute-start | bytes 983048 | tf_op jit(solution)/shard_map/ppermute | solution.py:386
  50.6 5.9 %collective-permute-start.8 = (bf16[4,4,80,1024]{3,2,1,0:T(8,128)(2,1)S(1)}, bf16[4,4,80,1024]{3,2,1,0:T(8,128)(2,1)S(1)}, u32[]{:S(2)}, u32[]{:S(2)}) collective-permute-start(bf16[4,4,80,1024]{3,2,1,0:T(8,128)(2,1)S(1)} %get-tuple-element.34), channel_id=1, source_target_pairs={{0,4},{4,0},{1,5},{5,1},{2,6},{6,2},{3,7},{7,3},{8,12},{12,8},{9,1... | collective-permute-start | bytes 7864328 | tf_op jit(solution)/shard_map/ppermute | solution.py:386
  59.7 14.9 %collective-permute-start.9 = (bf16[2,2,80,1024]{3,2,1,0:T(8,128)(2,1)}, bf16[2,2,80,1024]{3,2,1,0:T(8,128)(2,1)S(1)}, u32[]{:S(2)}, u32[]{:S(2)}) collective-permute-start(bf16[2,2,80,1024]{3,2,1,0:T(8,128)(2,1)} %get-tuple-element.38), channel_id=1, source_target_pairs={{0,1},{1,2},{2,3},{3,0},{4,12},{5,13},{6,14},{7,15},{8,9},{9,10},{... | collective-permute-start | bytes 1966088 | tf_op jit(solution)/shard_map/ppermute | solution.py:399
  60.9 13.7 %collective-permute-start.10 = (bf16[2,2,80,1024]{3,2,1,0:T(8,128)(2,1)}, bf16[2,2,80,1024]{3,2,1,0:T(8,128)(2,1)S(1)}, u32[]{:S(2)}, u32[]{:S(2)}) collective-permute-start(bf16[2,2,80,1024]{3,2,1,0:T(8,128)(2,1)} %get-tuple-element.39), channel_id=1, source_target_pairs={{0,3},{1,0},{2,1},{3,2},{4,28},{5,29},{6,30},{7,31},{8,11},{9,8},{... | collective-permute-start | bytes 1966088 | tf_op jit(solution)/shard_map/ppermute | solution.py:399
  62.4 30.0 %all-to-all-start.1 = ((bf16[64,16,256]{2,1,0:T(8,128)(2,1)}), bf16[64,16,256]{2,1,0:T(8,128)(2,1)S(1)}, u32[]{:S(2)}, u32[]{:S(2)}) async-start(bf16[64,16,256]{2,1,0:T(8,128)(2,1)} %bitcast.5), calls=%async_computation.1 | async-start | bytes 1048576 | tf_op jit(solution)/shard_map/all_to_all | solution.py:469
  74.8 9.7 %collective-permute-start.11 = (bf16[2,80,1024]{2,1,0:T(8,128)(2,1)S(1)}, bf16[2,80,1024]{2,1,0:T(8,128)(2,1)S(1)}, u32[]{:S(2)}, u32[]{:S(2)}) collective-permute-start(bf16[2,80,1024]{2,1,0:T(8,128)(2,1)S(1)} %get-tuple-element.40), channel_id=1, source_target_pairs={{0,1},{1,2},{2,3},{3,0},{4,12},{5,13},{6,14},{7,15},{8,9},{9,10},{... | collective-permute-start | bytes 983048 | tf_op jit(solution)/shard_map/ppermute | solution.py:399
  76.2 8.8 %collective-permute-start.12 = (bf16[2,80,1024]{2,1,0:T(8,128)(2,1)S(1)}, bf16[2,80,1024]{2,1,0:T(8,128)(2,1)S(1)}, u32[]{:S(2)}, u32[]{:S(2)}) collective-permute-start(bf16[2,80,1024]{2,1,0:T(8,128)(2,1)S(1)} %get-tuple-element.41), channel_id=1, source_target_pairs={{0,3},{1,0},{2,1},{3,2},{4,28},{5,29},{6,30},{7,31},{8,11},{9,8},{... | collective-permute-start | bytes 983048 | tf_op jit(solution)/shard_map/ppermute | solution.py:399
  85.9 7.6 %collective-permute-start.13 = (bf16[80,1024]{1,0:T(8,128)(2,1)}, bf16[80,1024]{1,0:T(8,128)(2,1)S(1)}, u32[]{:S(2)}, u32[]{:S(2)}) collective-permute-start(bf16[80,1024]{1,0:T(8,128)(2,1)} %get-tuple-element.42), channel_id=1, source_target_pairs={{0,8},{1,9},{2,10},{3,11},{4,5},{5,6},{6,7},{7,4},{8,16},{9,17},{1... | collective-permute-start | bytes 491528 | tf_op jit(solution)/shard_map/ppermute | solution.py:399
  85.9 7.6 %collective-permute-start.14 = (bf16[80,1024]{1,0:T(8,128)(2,1)}, bf16[80,1024]{1,0:T(8,128)(2,1)S(1)}, u32[]{:S(2)}, u32[]{:S(2)}) collective-permute-start(bf16[80,1024]{1,0:T(8,128)(2,1)} %get-tuple-element.46), channel_id=1, source_target_pairs={{0,16},{1,17},{2,18},{3,19},{4,6},{5,7},{6,4},{7,5},{8,24},{9,25},... | collective-permute-start | bytes 491528 | tf_op jit(solution)/shard_map/ppermute | solution.py:399
  86.8 7.4 %collective-permute-start.15 = (bf16[80,1024]{1,0:T(8,128)(2,1)S(1)}, bf16[80,1024]{1,0:T(8,128)(2,1)S(1)}, u32[]{:S(2)}, u32[]{:S(2)}) collective-permute-start(bf16[80,1024]{1,0:T(8,128)(2,1)S(1)} %get-tuple-element.47), channel_id=1, source_target_pairs={{0,24},{1,25},{2,26},{3,27},{4,7},{5,4},{6,5},{7,6},{8,0},{9,1},{1... | collective-permute-start | bytes 491528 | tf_op jit(solution)/shard_map/ppermute | solution.py:399
  123.9 5.3 %collective-permute-start.18 = (bf16[8,80,128]{2,1,0:T(8,128)(2,1)S(1)}, bf16[8,80,128]{2,1,0:T(8,128)(2,1)S(1)}, u32[]{:S(2)}, u32[]{:S(2)}) collective-permute-start(bf16[8,80,128]{2,1,0:T(8,128)(2,1)S(1)} %all_to_all.21.o0), channel_id=1, source_target_pairs={{0,24},{8,0},{16,8},{24,16},{1,25},{9,1},{17,9},{25,17},{2,26},{10... | collective-permute-start | bytes 491528 | tf_op jit(solution)/shard_map/ppermute | solution.py:386
  123.9 7.5 %collective-permute-start.17 = (bf16[8,80,128]{2,1,0:T(8,128)(2,1)S(1)}, bf16[8,80,128]{2,1,0:T(8,128)(2,1)S(1)}, u32[]{:S(2)}, u32[]{:S(2)}) collective-permute-start(bf16[8,80,128]{2,1,0:T(8,128)(2,1)S(1)} %all_to_all.21.o0), channel_id=1, source_target_pairs={{0,16},{8,24},{16,0},{24,8},{1,17},{9,25},{17,1},{25,9},{2,18},{10... | collective-permute-start | bytes 491528 | tf_op jit(solution)/shard_map/ppermute | solution.py:386
  125.9 8.3 %collective-permute-start.16 = (bf16[8,80,128]{2,1,0:T(8,128)(2,1)S(1)}, bf16[8,80,128]{2,1,0:T(8,128)(2,1)S(1)}, u32[]{:S(2)}, u32[]{:S(2)}) collective-permute-start(bf16[8,80,128]{2,1,0:T(8,128)(2,1)S(1)} %all_to_all.21.o0), channel_id=1, source_target_pairs={{0,8},{8,16},{16,24},{24,0},{1,9},{9,17},{17,25},{25,1},{2,10},{10... | collective-permute-start | bytes 491528 | tf_op jit(solution)/shard_map/ppermute | solution.py:386
  126.4 10.7 %collective-permute-start.19 = (bf16[8,80,128]{2,1,0:T(8,128)(2,1)S(1)}, bf16[8,80,128]{2,1,0:T(8,128)(2,1)S(1)}, u32[]{:S(2)}, u32[]{:S(2)}) collective-permute-start(bf16[8,80,128]{2,1,0:T(8,128)(2,1)S(1)} %all_to_all.21.o0), channel_id=1, source_target_pairs={{0,4},{4,0},{1,5},{5,1},{2,6},{6,2},{3,7},{7,3},{8,12},{12,8},{9,1... | collective-permute-start | bytes 491528 | tf_op jit(solution)/shard_map/ppermute | solution.py:386
  129.3 7.8 %collective-permute-start.22 = (bf16[8,80,128]{2,1,0:T(8,128)(2,1)S(1)}, bf16[8,80,128]{2,1,0:T(8,128)(2,1)S(1)}, u32[]{:S(2)}, u32[]{:S(2)}) collective-permute-start(bf16[8,80,128]{2,1,0:T(8,128)(2,1)S(1)} %collective-permute-done.18.o3), channel_id=1, source_target_pairs={{0,4},{4,0},{1,5},{5,1},{2,6},{6,2},{3,7},{7,3},{8,12},{12,8},{9,1... | collective-permute-start | bytes 491528 | tf_op jit(solution)/shard_map/ppermute | solution.py:386
  131.4 5.7 %collective-permute-start.21 = (bf16[8,80,128]{2,1,0:T(8,128)(2,1)S(1)}, bf16[8,80,128]{2,1,0:T(8,128)(2,1)S(1)}, u32[]{:S(2)}, u32[]{:S(2)}) collective-permute-start(bf16[8,80,128]{2,1,0:T(8,128)(2,1)S(1)} %collective-permute-done.17.o2), channel_id=1, source_target_pairs={{0,4},{4,0},{1,5},{5,1},{2,6},{6,2},{3,7},{7,3},{8,12},{12,8},{9,1... | collective-permute-start | bytes 491528 | tf_op jit(solution)/shard_map/ppermute | solution.py:386
  134.2 2.9 %collective-permute-start.20 = (bf16[8,80,128]{2,1,0:T(8,128)(2,1)S(1)}, bf16[8,80,128]{2,1,0:T(8,128)(2,1)S(1)}, u32[]{:S(2)}, u32[]{:S(2)}) collective-permute-start(bf16[8,80,128]{2,1,0:T(8,128)(2,1)S(1)} %collective-permute-done.16.o1), channel_id=1, source_target_pairs={{0,4},{4,0},{1,5},{5,1},{2,6},{6,2},{3,7},{7,3},{8,12},{12,8},{9,1... | collective-permute-start | bytes 491528 | tf_op jit(solution)/shard_map/ppermute | solution.py:386

commit v4 on v3

--- a/solution.py
+++ b/solution.py
@@ -15,7 +15,7 @@
 NN = (((1,), (0,)), ((), ()))
 NT = (((1,), (1,)), ((), ()))
 TN = (((0,), (0,)), ((), ()))
-VMEM_LIMIT = 24 * 1024 * 1024
+MIB = 1024 * 1024
 
 
 def dot(a, b, dims=NN):
@@ -26,14 +26,14 @@
     return lax.broadcasted_iota(jnp.int32, shape, dim)
 
 
-def call(body, outs, args, name, scratch=(), smem=0):
+def call(body, outs, args, name, scratch=(), mib=12):
     return pl.pallas_call(
         body,
         out_shape=[jax.ShapeDtypeStruct(s, d) for s, d in outs],
         in_specs=[pl.BlockSpec(memory_space=pltpu.VMEM) for _ in args],
         out_specs=[pl.BlockSpec(memory_space=pltpu.VMEM) for _ in outs],
         scratch_shapes=[pltpu.VMEM(s, d) for s, d in scratch],
-        compiler_params=pltpu.CompilerParams(vmem_limit_bytes=VMEM_LIMIT),
+        compiler_params=pltpu.CompilerParams(vmem_limit_bytes=mib * MIB),
         name=name,
     )(*args)
 
@@ -128,75 +128,66 @@
     return proj, back
 
 
-def grad_chunks(x, y, half, nrm, dpre, mix, cot, put):
-    right = cot[:, pl.ds(pl.multiple_of(half * 512, 512), 512)]
-    for sx in range(4):
-        block = (x + sx) % 4
-        d_in = dot(nrm[block], dpre[half], TN).astype(BF16)
-        d_out = dot(mix[block], right, TN).astype(BF16)
-        tail = jnp.concatenate([d_out[:64], d_out[64:]], axis=1)
-        for m in range(4):
-            if m < 3:
-                rows = d_in[80 * m : 80 * m + 80]
-            else:
-                rows = jnp.concatenate([d_in[240:], tail], axis=0)
-            put(sx, (m + 4 - y) % 4, rows)
-
-
 def order_of(half, sx, sy):
     return jnp.where(half == 0, sx, sy), jnp.where(half == 0, sy, sx)
 
 
-CHUNK = 32
-
-
-def layer_body(
+ROWS = 256
+
+
+def half_columns(half, width):
+    return pl.ds(pl.multiple_of(half * width, width), width)
+
+
+def forward_body(
     blocks_ref, owners_ref, arrived, cot, w_in, w_out, a1, a2, a3, a4, b1, b2, b3, b4,
-    layer_out, gother, nrm, dpre, mix, rstd,
-    owned, pre, act, att, att_rstd, weights, dscore, dmixed, datt,
+    shared, owned, rstd, act, dsilu, hat, att_rstd, weights, dscore, w_full,
+    wide, pre,
 ):
     x, y, c = lax.axis_index("x"), lax.axis_index("y"), lax.axis_index("c")
     me = (lax.axis_index("z") * 4 + y) * 2 + c
     proj, back = weights_of(x, c, (w_in, w_out, (a1, a2, a3, a4), (b1, b2, b3, b4)))
     halves = ((True, c), (False, 1 - c))
 
-    t = iota((256, 1024), 0)
-    wanted = (t & 63) * 16 + (t >> 6) * 4
-    lane = iota((256, 1024), 1)
-    for j in range(4):
-        pick = (lane == wanted + j).astype(F32).astype(BF16)
-        owned[:, j * 256 : (j + 1) * 256] = dot(pick, arrived[...])
-
-    def norm_rows(r, _):
-        rows = pl.ds(pl.multiple_of(r * CHUNK, CHUNK), CHUNK)
-        v = owned[rows, :]
+    for i in range(2):
+        wide[i] = arrived[:, i * 128 : (i + 1) * 128].astype(F32)
+    for s in range(4):
+        for j in range(8):
+            rows = wide.at[j % 2][pl.ds(s * 4 + j // 2, 64, stride=16), :]
+            owned[s * 64 : (s + 1) * 64, j * 128 : (j + 1) * 128] = rows.astype(BF16)
+
+    def norm_rows(rows):
+        v = owned[rows, :].astype(F32)
         cen = v - jnp.sum(v, axis=1, keepdims=True) * (1.0 / 1024)
         rs = lax.rsqrt(jnp.sum(cen * cen, axis=1, keepdims=True) * (1.0 / 1024) + EPS)
         n = (cen * rs).astype(BF16)
         for j in range(4):
-            nrm[j, rows, :] = n[:, j * 256 : (j + 1) * 256]
-        rstd[rows, :] = jnp.broadcast_to(rs, (CHUNK, 128))
-        return 0
-
-    lax.fori_loop(0, 256 // CHUNK, norm_rows, 0)
+            shared[j, rows, :256] = n[:, j * 256 : (j + 1) * 256]
+        rstd[rows, :] = jnp.broadcast_to(rs, (ROWS, 128))
+
+    norm_rows(pl.ds(0, ROWS))
+    right = cot[:, half_columns(1 - c, 512)]
+    for j in range(4):
+        shared[j, :, 384:] = right[:, j * 128 : (j + 1) * 128]
+    for k in range(4):
+        for is_own, h in halves:
+            w_full[(x + 4 - k) % 4, :, half_columns(h, 512)] = back(k, is_own)
 
     for is_own, h in halves:
         total = None
         for k in range(4):
-            part = dot(nrm[(x + 4 - k) % 4], proj(k, is_own))
+            part = dot(shared[(x + 4 - k) % 4, :, :256], proj(k, is_own))
             total = part if total is None else total + part
         pre[h] = total
 
-    def activate(r, _):
-        rows = pl.ds(pl.multiple_of(r * CHUNK, CHUNK), CHUNK)
+    def activate(rows):
         for h in range(2):
             v = pre[h, rows, :]
             sig = jax.nn.sigmoid(v)
             act[h, rows, :] = (v * sig).astype(BF16)
-            pre[h, rows, :] = sig * (1.0 + v * (1.0 - sig))
-        return 0
-
-    lax.fori_loop(0, 256 // CHUNK, activate, 0)
+            dsilu[h, rows, :] = sig * (1.0 + v * (1.0 - sig))
+
+    activate(pl.ds(0, ROWS))
 
     n_row, o_row, n_col, o_col, _, before_col, before_row = histories(blocks_ref, owners_ref)
     mine = me.astype(F32)
@@ -218,52 +209,44 @@
         sig = jax.nn.sigmoid(s)
         w = (s * sig * mask).astype(BF16)
         weights[h] = w
-        dscore[h] = mask * (sig * (1.0 + s * (1.0 - sig))) * scale
-        att[:, lo:hi] = dot(w, act[0, :, 512 + lo : 512 + hi])
-
-    def mix_rows(r, _):
-        rows = pl.ds(pl.multiple_of(r * CHUNK, CHUNK), CHUNK)
-        v = att[rows, :]
+        dscore[h] = (mask * scale) * (sig * (1.0 + s * (1.0 - sig)))
+        hat[:, lo:hi] = dot(w, act[0, :, 512 + lo : 512 + hi])
+
+    def mix_rows(rows):
+        v = hat[rows, :]
         cen = v - jnp.sum(v, axis=1, keepdims=True) * (1.0 / 512)
         rs = lax.rsqrt(jnp.sum(cen * cen, axis=1, keepdims=True) * (1.0 / 512) + EPS)
-        hat = cen * rs
-        mixed = (act[0, rows, :512].astype(F32) * hat).astype(BF16)
+        cen = cen * rs
+        mixed = (act[0, rows, :512].astype(F32) * cen).astype(BF16)
         for h in range(4):
-            mix[h, rows, :] = mixed[:, h * HEAD : (h + 1) * HEAD]
-        att[rows, :] = hat
-        att_rstd[rows, :] = jnp.broadcast_to(rs, (CHUNK, 128))
-        return 0
-
-    lax.fori_loop(0, 256 // CHUNK, mix_rows, 0)
-
-    for is_own, h in halves:
-        columns = pl.ds(pl.multiple_of(h * 512, 512), 512)
-        total = owned[:, columns]
-        for k in range(4):
-            total = total + dot(mix[(x + 4 - k) % 4], back(k, is_own))
-        layer_out[:, columns] = total.astype(BF16)
-
-    for k in range(4):
-        total = None
-        for is_own, h in halves:
-            columns = pl.ds(pl.multiple_of(h * 512, 512), 512)
-            part = dot(cot[:, columns], back(k, is_own), NT)
-            total = part if total is None else total + part
-        dmixed[(x + 4 - k) % 4] = total.astype(BF16)
-
-    def unmix_rows(r, _):
-        rows = pl.ds(pl.multiple_of(r * CHUNK, CHUNK), CHUNK)
-        dm = jnp.concatenate([dmixed[h, rows, :] for h in range(4)], axis=1).astype(F32)
-        hat = att[rows, :]
-        du = (dm * hat).astype(BF16).astype(F32)
-        dpre[0, rows, :512] = (du * pre[0, rows, :512]).astype(BF16)
+            shared[h, rows, 256:384] = mixed[:, h * HEAD : (h + 1) * HEAD]
+        hat[rows, :] = cen
+        att_rstd[rows, :] = jnp.broadcast_to(rs, (ROWS, 128))
+
+    mix_rows(pl.ds(0, ROWS))
+
+
+def backward_body(
+    shared, owned, cot, act, dsilu, hat, att_rstd, weights, dscore, w_full,
+    out, kept, sent, dpre, dmixed, datt,
+):
+    c = lax.axis_index("c")
+    w_out = w_full[...].reshape(512, 1024)
+    mixed = jnp.concatenate([shared[h, :, 256:384] for h in range(4)], axis=1)
+    out[...] = (dot(mixed, w_out) + owned[...].astype(F32)).astype(BF16)
+    dmixed[...] = dot(cot[...], w_out, NT).astype(BF16)
+
+    def unmix_rows(rows):
+        dm = dmixed[rows, :].astype(F32)
+        n = hat[rows, :]
+        du = (dm * n).astype(BF16).astype(F32)
+        dpre[0, rows, :512] = (du * dsilu[0, rows, :512]).astype(BF16)
         dh = dm * act[0, rows, :512].astype(F32)
         m1 = jnp.sum(dh, axis=1, keepdims=True) * (1.0 / 512)
-        m2 = jnp.sum(dh * hat, axis=1, keepdims=True) * (1.0 / 512)
-        datt[rows, :] = (att_rstd[rows, :1] * (dh - m1 - hat * m2)).astype(BF16)
-        return 0
-
-    lax.fori_loop(0, 256 // CHUNK, unmix_rows, 0)
+        m2 = jnp.sum(dh * n, axis=1, keepdims=True) * (1.0 / 512)
+        datt[rows, :] = (att_rstd[rows, :1] * (dh - m1 - n * m2)).astype(BF16)
+
+    unmix_rows(pl.ds(0, ROWS))
 
     for h in range(4):
         lo, hi = h * HEAD, (h + 1) * HEAD
@@ -273,66 +256,60 @@
         dv = dot(weights[h], d_h, TN).astype(BF16).astype(F32)
         dq = dot(ds, act[1, :, 512 + lo : 512 + hi]).astype(BF16).astype(F32)
         dk = dot(ds, act[1, :, lo:hi], TN).astype(BF16).astype(F32)
-        dpre[0, :, 512 + lo : 512 + hi] = (dv * pre[0, :, 512 + lo : 512 + hi]).astype(BF16)
-        dpre[1, :, lo:hi] = (dq * pre[1, :, lo:hi]).astype(BF16)
-        dpre[1, :, 512 + lo : 512 + hi] = (dk * pre[1, :, 512 + lo : 512 + hi]).astype(BF16)
-
-    def put(sx, sy, rows):
-        first, second = order_of(1 - c, sx, sy)
-        gother[first, second] = rows
-
-    grad_chunks(x, y, 1 - c, nrm, dpre, mix, cot, put)
+        dpre[0, :, 512 + lo : 512 + hi] = (dv * dsilu[0, :, 512 + lo : 512 + hi]).astype(BF16)
+        dpre[1, :, lo:hi] = (dq * dsilu[1, :, lo:hi]).astype(BF16)
+        dpre[1, :, 512 + lo : 512 + hi] = (dk * dsilu[1, :, 512 + lo : 512 + hi]).astype(BF16)
+    kept[...] = dpre[c]
+    sent[...] = dpre[1 - c]
 
 
 def rest_body(
-    nrm, dpre, rstd, cot, w_in, w_out, a1, a2, a3, a4, b1, b2, b3, b4,
-    outgoing, dnorm, downed,
+    shared, rstd, cot, kept, sent, w_in, a1, a2, a3, a4, b1, b2, b3, b4,
+    outgoing, dnorm, wide,
 ):
     x, c = lax.axis_index("x"), lax.axis_index("c")
-    proj, _ = weights_of(x, c, (w_in, w_out, (a1, a2, a3, a4), (b1, b2, b3, b4)))
+    proj, _ = weights_of(x, c, (w_in, None, (a1, a2, a3, a4), (b1, b2, b3, b4)))
     for k in range(4):
-        total = None
-        for is_own, h in ((True, c), (False, 1 - c)):
-            part = dot(dpre[h], proj(k, is_own), NT)
-            total = part if total is None else total + part
+        total = dot(kept[...], proj(k, True), NT) + dot(sent[...], proj(k, False), NT)
         dnorm[(x + 4 - k) % 4] = total.astype(BF16)
 
-    def unnorm_rows(r, _):
-        rows = pl.ds(pl.multiple_of(r * CHUNK, CHUNK), CHUNK)
-        dn = jnp.concatenate([dnorm[j, rows, :] for j in range(4)], axis=1).astype(F32)
-        hat = jnp.concatenate([nrm[j, rows, :] for j in range(4)], axis=1).astype(F32)
-        m1 = jnp.sum(dn, axis=1, keepdims=True) * (1.0 / 1024)
-        m2 = jnp.sum(dn * hat, axis=1, keepdims=True) * (1.0 / 1024)
-        d = rstd[rows, :1] * (dn - m1 - hat * m2) + cot[rows, :].astype(F32)
-        downed[rows, :] = d.astype(BF16)
-        return 0
-
-    lax.fori_loop(0, 256 // CHUNK, unnorm_rows, 0)
-    t = iota((1024, 256), 1)
-    wanted = (t & 63) * 16 + (t >> 6) * 4
-    row = iota((1024, 256), 0)
-    total = None
-    for j in range(4):
-        pick = (row == wanted + j).astype(F32).astype(BF16)
-        part = dot(pick, downed[:, j * 256 : (j + 1) * 256])
-        total = part if total is None else total + part
-    outgoing[...] = total.astype(BF16)
-
-def sum_pair_body(nrm, dpre, mix, cot, gfrom, backward, ahead, behind, kept, held):
+    dn = jnp.concatenate([dnorm[j] for j in range(4)], axis=1).astype(F32)
+    n = jnp.concatenate([shared[j, :, :256] for j in range(4)], axis=1).astype(F32)
+    m1 = jnp.sum(dn, axis=1, keepdims=True) * (1.0 / 1024)
+    m2 = jnp.sum(dn * n, axis=1, keepdims=True) * (1.0 / 1024)
+    d = rstd[:, :1] * (dn - m1 - n * m2) + cot[...].astype(F32)
+    for s in range(4):
+        for j in range(8):
+            part = d[s * 64 : (s + 1) * 64, j * 128 : (j + 1) * 128]
+            wide.at[j % 2][pl.ds(s * 4 + j // 2, 64, stride=16), :] = part
+    for i in range(2):
+        outgoing[:, i * 128 : (i + 1) * 128] = wide[i].astype(BF16)
+
+
+def sum_pair_body(shared, other, kept, received, cot, backward, ahead, behind, held_own, held):
     x, y, c = lax.axis_index("x"), lax.axis_index("y"), lax.axis_index("c")
-
-    def put(sx, sy, rows):
-        first, second = order_of(c, sx, sy)
-        held[first, second] = (rows.astype(F32) + gfrom[first, second].astype(F32)).astype(BF16)
-
-    grad_chunks(x, y, c, nrm, dpre, mix, cot, put)
+    right = cot[:, half_columns(c, 512)]
+    other_right = jnp.concatenate([other[j, :, 384:] for j in range(4)], axis=1)
+    for sx in range(4):
+        block = (x + sx) % 4
+        d_in = dot(shared[block, :, :256], kept[...], TN) + dot(other[block, :, :256], received[...], TN)
+        d_out = dot(shared[block, :, 256:384], right, TN) + dot(other[block, :, 256:384], other_right, TN)
+        d_in, d_out = d_in.astype(BF16), d_out.astype(BF16)
+        tail = jnp.concatenate([d_out[:64], d_out[64:]], axis=1)
+        for m in range(4):
+            if m < 3:
+                rows = d_in[80 * m : 80 * m + 80]
+            else:
+                rows = jnp.concatenate([d_in[240:], tail], axis=0)
+            first, second = order_of(c, sx, (m + 4 - y) % 4)
+            held[first, second] = rows
     ahead[0] = held[2, :2]
     ahead[1] = held[1, 2:]
     behind[0] = held[2, 2:]
     behind[1] = held[3, :2]
-    kept[:4] = held[0]
-    kept[4:6] = held[1, :2]
-    kept[6:] = held[3, 2:]
+    held_own[:4] = held[0]
+    held_own[4:6] = held[1, :2]
+    held_own[6:] = held[3, 2:]
 
 
 def add_relayed_body(kept, ahead, behind, forth, back):
@@ -416,7 +393,7 @@
             pltpu.VMEM((128, 1024), BF16),
             pltpu.SemaphoreType.DMA((6,)),
         ],
-        compiler_params=pltpu.CompilerParams(vmem_limit_bytes=60 * 1024 * 1024),
+        compiler_params=pltpu.CompilerParams(vmem_limit_bytes=60 * MIB),
         name="entry",
     )(hist_blocks, owner, x_rows[0], w_in, w_out)
     left, right = shift(pack, "x", 4, 1), shift(pack, "x", 4, 3)
@@ -425,44 +402,50 @@
     ).reshape(1024, 256)
     own = [left, right, shift(left[:160], "x", 4, 1), shift(right[160:], "x", 4, 3)]
     weights = (w_in, w_out, *own, *[shift(a, "c", 2, 1) for a in own])
-    layer_out, gother, nrm, dpre, mix, rstd = call(
-        layer_body,
+    shared, owned, rstd, act, dsilu, hat, att_rstd, scores, dscore, w_full = call(
+        forward_body,
         [
+            ((4, 256, 512), BF16),
             ((256, 1024), BF16),
-            ((4, 4, 80, 1024), BF16),
-            ((4, 256, 256), BF16),
+            ((256, 128), F32),
             ((2, 256, 1024), BF16),
-            ((4, 256, 128), BF16),
-            ((256, 128), F32),
-        ],
-        (hist_blocks, owner, arrived, cot) + weights,
-        "layer",
-        scratch=[
-            ((256, 1024), F32),
             ((2, 256, 1024), F32),
-            ((2, 256, 1024), BF16),
             ((256, 512), F32),
             ((256, 128), F32),
             ((4, 256, 256), BF16),
             ((4, 256, 256), F32),
-            ((4, 256, 128), BF16),
-            ((256, 512), BF16),
+            ((4, 128, 1024), BF16),
         ],
-    )
-    gfrom = shift(gother, "c", 2, 1)
+        (hist_blocks, owner, arrived, cot) + weights,
+        "forward",
+        scratch=[((2, 1024, 128), F32), ((2, 256, 1024), F32)],
+        mib=20,
+    )
+    other = shift(shared, "c", 2, 1)
+    layer_out, kept, sent = call(
+        backward_body,
+        [((256, 1024), BF16)] * 3,
+        (shared, owned, cot, act, dsilu, hat, att_rstd, scores, dscore, w_full),
+        "backward",
+        scratch=[((2, 256, 1024), BF16), ((256, 512), BF16), ((256, 512), BF16)],
+        mib=12,
+    )
+    received = shift(sent, "c", 2, 1)
     (backward,) = call(
         rest_body,
         [((1024, 256), BF16)],
-        (nrm, dpre, rstd, cot) + weights,
+        (shared, rstd, cot, kept, sent, w_in) + weights[2:],
         "rest",
-        scratch=[((4, 256, 256), BF16), ((256, 1024), BF16)],
+        scratch=[((4, 256, 256), BF16), ((2, 1024, 128), F32)],
+        mib=12,
     )
     ahead, behind, kept = call(
         sum_pair_body,
         [((2, 2, 80, 1024), BF16), ((2, 2, 80, 1024), BF16), ((8, 80, 1024), BF16)],
-        (nrm, dpre, mix, cot, gfrom, backward),
+        (shared, other, kept, received, cot, backward),
         "sum_pair",
         scratch=[((4, 4, 80, 1024), BF16)],
+        mib=12,
     )
     backward, kept = lax.optimization_barrier((backward, kept))
     ahead, behind = crossed(ahead, 1, True), crossed(behind, 3, True)
@@ -477,11 +460,11 @@
         add_four_body, [((80, 1024), BF16)] * 4, (kept, ahead, behind, forth, back), "add_four"
     )
     second = [mid[0]] + [crossed(mid[s], s, False) for s in (1, 2, 3)]
-    returned, second[1] = lax.optimization_barrier((returned, second[1]))
-    (columns,) = call(add_last_body, [((8, 80, 128), BF16)], second, "add_last")
     (grad_rows,) = call(
         rows_back, [((128, 1024), BF16)], (hist_blocks, owner, returned), "rows_back"
     )
+    grad_rows, second[1] = lax.optimization_barrier((grad_rows, second[1]))
+    (columns,) = call(add_last_body, [((8, 80, 128), BF16)], second, "add_last")
     parts = lax.all_to_all(columns, "z", split_axis=0, concat_axis=0, tiled=True)
     (summed,) = call(add_eight_body, [((8, 80, 128), BF16)], (parts,), "add_eight")
     mine = lax.all_to_all(summed, "z", split_axis=0, concat_axis=0, tiled=True)

time: 140 us -> 135 us (0.964)
  Pallas kernels: 29.3 us -> 23.7 us
    pallas_call x9 -> x10, Pallas kernels: 26.3 us -> 20.6 us  [call(): pl.pallas_call(body, out_shape=[jax.ShapeDtypeStruct(s, d) for s, d in ou...]
    ppermute x16 -> x17, starting transfers between devices: 25.8 us -> 26.8 us  [shift(): return lax.ppermute(a, axis, [(i, (i + s) % n) for i in range(n)])]
    ppermute x16 -> x17, waiting for transfers between devices: 5.51 us -> 6.16 us  [shift(): return lax.ppermute(a, axis, [(i, (i + s) % n) for i in range(n)])]
  transfers between devices with their start and end apart: 25 -> 26, of which waited for: 10 -> 9; matrix products, arithmetic and copies ran while one was open for 0% -> 0% of each run, Pallas kernels for 6% -> 7%
where the time goes in v4:
time: 135 us; the launch traced here: 134 us
  starting transfers between devices  60.2 us (45%)
  blocking collectives  29.1 us (22%)
  Pallas kernels  23.7 us (18%)
  waiting for transfers between devices  19.5 us (14%)
    ppermute x17, starting transfers between devices, shift(): return lax.ppermute(a, axis, [(i, (i + s) % n) for i in range(n)])  26.8 us
    pallas_call x10, Pallas kernels, call(): pl.pallas_call(body, out_shape=[jax.ShapeDtypeStruct(s, d) for s, d in ou...  20.6 us
    all_to_all x1, blocking collectives, on_device(): lax.all_to_all(columns, 'z', split_axis=0, concat_axis=0, tiled=True)  17.2 us
    all_to_all x1, starting transfers between devices, on_device(): lax.all_to_all(outgoing.reshape(64, 16, 256), DP, split_axis=0, concat_ax...  12.8 us
    all_to_all x1, starting transfers between devices, on_device(): lax.all_to_all(backward.reshape(64, 16, 256), DP, split_axis=0, concat_ax...  12.5 us
    all_to_all x1, blocking collectives, on_device(): mine = lax.all_to_all(summed, 'z', split_axis=0, concat_axis=0, tiled=True)  11.9 us
    ppermute x7, starting transfers between devices, crossed(): return lax.ppermute(a, ('z', 'y', 'c', 'x'), pairs)  8.12 us
    ppermute x7, waiting for transfers between devices, crossed(): return lax.ppermute(a, ('z', 'y', 'c', 'x'), pairs)  7.7 us
  transfers between devices with their start and end apart: 26, of which 9 were waited for; matrix products, arithmetic and copies ran while one was open for 0% of the time, Pallas kernels for 7%

profile of v4, /device:TPU:1, one launch (start us, length us, event | category | flops | bytes accessed | tf_op | source)
XLA Modules:
  0.0 134.2 jit_solution(13345684427004627082)
XLA Ops:
  0.7 3.0 %entry.1 = (bf16[1024,256]{1,0:T(8,128)(2,1)}, bf16[320,1024]{1,0:T(8,128)(2,1)}) custom-call(s32[1,64]{1,0:T(1,128)} %blocks_ref.3, s32[1,64]{1,0:T(1,128)} %owners_ref.3, bf16[128,1024]{1,0:T(8,128)(2,1)} %bitcast.15, bf16[256,2048]{1,0:T(8,128)(2,1)} %w_in.5, bf16[128,1024]{1,0:T(8,128)(2,1)} %w_out.3), custom_call_target="tpu_custom_call" | custom-call | tf_op jit(solution)/shard_map/entry/pallas_call | solution.py:382
  3.7 3.4 %collective-permute-start.1 = (bf16[320,1024]{1,0:T(8,128)(2,1)}, bf16[320,1024]{1,0:T(8,128)(2,1)S(1)}, u32[]{:S(2)}, u32[]{:S(2)}) collective-permute-start(bf16[320,1024]{1,0:T(8,128)(2,1)} %get-tuple-element.35), channel_id=1, source_target_pairs={{0,3},{1,0},{2,1},{3,2},{4,7},{5,4},{6,5},{7,6},{8,11},{9,8},{10,9... | collective-permute-start | bytes 1966088 | tf_op jit(solution)/shard_map/ppermute | solution.py:363
  7.1 12.8 %all-to-all-start = ((bf16[64,16,256]{2,1,0:T(8,128)(2,1)}), bf16[64,16,256]{2,1,0:T(8,128)(2,1)}, u32[]{:S(2)}, u32[]{:S(2)}) async-start(bf16[64,16,256]{2,1,0:T(8,128)(2,1)} %bitcast.13), calls=%async_computation | async-start | bytes 1048576 | tf_op jit(solution)/shard_map/all_to_all | solution.py:400
  20.8 3.4 %collective-permute-start.3 = (bf16[160,1024]{1,0:T(8,128)(2,1)S(1)}, bf16[160,1024]{1,0:T(8,128)(2,1)}, u32[]{:S(2)}, u32[]{:S(2)}) collective-permute-start(bf16[160,1024]{1,0:T(8,128)(2,1)S(1)} %slice.9), channel_id=1, source_target_pairs={{0,3},{1,0},{2,1},{3,2},{4,7},{5,4},{6,5},{7,6},{8,11},{9,8},{10,9... | collective-permute-start | bytes 983048 | tf_op jit(solution)/shard_map/ppermute | solution.py:363
  24.3 1.9 %collective-permute-start.5 = (bf16[320,1024]{1,0:T(8,128)(2,1)S(1)}, bf16[320,1024]{1,0:T(8,128)(2,1)S(1)}, u32[]{:S(2)}, u32[]{:S(2)}) collective-permute-start(bf16[320,1024]{1,0:T(8,128)(2,1)S(1)} %collective-permute-done.1.a2), channel_id=1, source_target_pairs={{0,4},{4,0},{1,5},{5,1},{2,6},{6,2},{3,7},{7,3},{8,12},{12,8},{9,1... | collective-permute-start | bytes 1966088 | tf_op jit(solution)/shard_map/ppermute | solution.py:363
  26.4 3.3 %collective-permute-done.3.a4 = bf16[160,1024]{1,0:T(8,128)(2,1)} collective-permute-done((bf16[160,1024]{1,0:T(8,128)(2,1)S(1)}, bf16[160,1024]{1,0:T(8,128)(2,1)}, u32[]{:S(2)}, u32[]{:S(2)}) %collective-permute-start.3) | collective-permute-done | bytes 327712 | tf_op jit(solution)/shard_map/ppermute | solution.py:363
  29.7 2.5 %collective-permute-start.7 = (bf16[160,1024]{1,0:T(8,128)(2,1)}, bf16[160,1024]{1,0:T(8,128)(2,1)}, u32[]{:S(2)}, u32[]{:S(2)}) collective-permute-start(bf16[160,1024]{1,0:T(8,128)(2,1)} %collective-permute-done.3.a4), channel_id=1, source_target_pairs={{0,4},{4,0},{1,5},{5,1},{2,6},{6,2},{3,7},{7,3},{8,12},{12,8},{9,1... | collective-permute-start | bytes 983048 | tf_op jit(solution)/shard_map/ppermute | solution.py:363
  33.0 2.7 %collective-permute-start.6 = (bf16[160,1024]{1,0:T(8,128)(2,1)}, bf16[160,1024]{1,0:T(8,128)(2,1)}, u32[]{:S(2)}, u32[]{:S(2)}) collective-permute-start(bf16[160,1024]{1,0:T(8,128)(2,1)} %collective-permute-done.2.a3), channel_id=1, source_target_pairs={{0,4},{4,0},{1,5},{5,1},{2,6},{6,2},{3,7},{7,3},{8,12},{12,8},{9,1... | collective-permute-start | bytes 983048 | tf_op jit(solution)/shard_map/ppermute | solution.py:363
  35.8 1.8 %all-to-all-done = bf16[64,16,256]{2,1,0:T(8,128)(2,1)} async-done(((bf16[64,16,256]{2,1,0:T(8,128)(2,1)}), bf16[64,16,256]{2,1,0:T(8,128)(2,1)}, u32[]{:S(2)}, u32[]{:S(2)}) %all-to-all-start) | async-done | bytes 524320 | tf_op jit(solution)/shard_map/all_to_all | solution.py:400
  37.6 0.9 copy-done.2
  38.5 5.4 %forward.1 = (bf16[4,256,512]{2,1,0:T(8,128)(2,1)S(1)}, bf16[256,1024]{1,0:T(8,128)(2,1)S(1)}, f32[256,128]{1,0:T(8,128)S(1)}, bf16[2,256,1024]{2,1,0:T(8,128)(2...) custom-call(s32[1,64]{1,0:T(1,128)S(1)} %copy-done.3, ...), custom_call_target="tpu_custom_call" | custom-call | tf_op jit(solution)/shard_map/forward/pallas_call | solution.py:30
  44.6 2.5 %backward.1 = (bf16[256,1024]{1,0:T(8,128)(2,1)}, bf16[256,1024]{1,0:T(8,128)(2,1)S(1)}, bf16[256,1024]{1,0:T(8,128)(2,1)S(1)}) custom-call(bf16[4,256,512]{2,1,0:T(8,128)(2,1)S(1)} %get-tuple-element.36.shared, bf16[256,1024]{1,0:T(8,128)(2,1)S(1)} %get-tuple-element.37.owned, bf16[256,1024]{1,0:T(8,128)(2,1)S(1)} %bitcast.9, ...), custom_call_target="tpu_custom_call" | custom-call | tf_op jit(solution)/shard_map/backward/pallas_call | solution.py:30
  47.3 4.3 %rest.1.backward = bf16[1024,256]{1,0:T(8,128)(2,1)} custom-call(bf16[4,256,512]{2,1,0:T(8,128)(2,1)S(1)} %get-tuple-element.36.shared, f32[256,128]{1,0:T(8,128)S(1)} %get-tuple-element.46.rstd, bf16[256,1024]{1,0:T(8,128)(2,1)S(1)} %bitcast.10, bf16[256,1024]{1,0:T(8,128)(2,1)S(1)} %get-tuple-element.47.kept, ...), custom_call_target="tpu_custom_call" | custom-call | tf_op jit(solution)/shard_map/rest/pallas_call | solution.py:30
  51.6 3.7 %sum_pair.1 = (bf16[2,2,80,1024]{3,2,1,0:T(8,128)(2,1)}, bf16[2,2,80,1024]{3,2,1,0:T(8,128)(2,1)}, bf16[8,80,1024]{2,1,0:T(8,128)(2,1)S(1)}) custom-call(bf16[4,256,512]{2,1,0:T(8,128)(2,1)S(1)} %get-tuple-element.36.shared, bf16[4,256,512]{2,1,0:T(8,128)(2,1)S(1)} %collective-permute-done.8.other, bf16[256,1024]{1,0:T(8,128)(2,1)S(1)} %get-tuple-element.47.kept, ...), custom_call_target="tpu_custom_call" | custom-call | tf_op jit(solution)/shard_map/sum_pair/pallas_call | solution.py:30
  55.3 1.1 collective-permute-start.10
  56.4 1.6 %collective-permute-start.11 = (bf16[2,2,80,1024]{3,2,1,0:T(8,128)(2,1)}, bf16[2,2,80,1024]{3,2,1,0:T(8,128)(2,1)S(1)}, u32[]{:S(2)}, u32[]{:S(2)}) collective-permute-start(bf16[2,2,80,1024]{3,2,1,0:T(8,128)(2,1)} %get-tuple-element.53), channel_id=1, source_target_pairs={{0,3},{1,0},{2,1},{3,2},{4,28},{5,29},{6,30},{7,31},{8,11},{9,8},{... | collective-permute-start | bytes 1966088 | tf_op jit(solution)/shard_map/ppermute | solution.py:376
  58.0 12.5 %all-to-all-start.1 = ((bf16[64,16,256]{2,1,0:T(8,128)(2,1)}), bf16[64,16,256]{2,1,0:T(8,128)(2,1)S(1)}, u32[]{:S(2)}, u32[]{:S(2)}) async-start(bf16[64,16,256]{2,1,0:T(8,128)(2,1)} %bitcast.5), calls=%async_computation.1 | async-start | bytes 1048576 | tf_op jit(solution)/shard_map/all_to_all | solution.py:452
  70.7 1.5 %collective-permute-start.12 = (bf16[2,80,1024]{2,1,0:T(8,128)(2,1)S(1)}, bf16[2,80,1024]{2,1,0:T(8,128)(2,1)S(1)}, u32[]{:S(2)}, u32[]{:S(2)}) collective-permute-start(bf16[2,80,1024]{2,1,0:T(8,128)(2,1)S(1)} %get-tuple-element.54), channel_id=1, source_target_pairs={{0,1},{1,2},{2,3},{3,0},{4,12},{5,13},{6,14},{7,15},{8,9},{9,10},{... | collective-permute-start | bytes 983048 | tf_op jit(solution)/shard_map/ppermute | solution.py:376
  72.2 1.3 collective-permute-start.13
  73.5 6.9 %collective-permute-done.12.forth = bf16[2,80,1024]{2,1,0:T(8,128)(2,1)S(1)} collective-permute-done((bf16[2,80,1024]{2,1,0:T(8,128)(2,1)S(1)}, bf16[2,80,1024]{2,1,0:T(8,128)(2,1)S(1)}, u32[]{:S(2)}, u32[]{:S(2)}) %collective-permute-start.12) | collective-permute-done | bytes 327712 | tf_op jit(solution)/shard_map/ppermute | solution.py:376
  82.7 1.8 %collective-permute-start.16 = (bf16[80,1024]{1,0:T(8,128)(2,1)}, bf16[80,1024]{1,0:T(8,128)(2,1)S(1)}, u32[]{:S(2)}, u32[]{:S(2)}) collective-permute-start(bf16[80,1024]{1,0:T(8,128)(2,1)} %get-tuple-element.61), channel_id=1, source_target_pairs={{0,24},{1,25},{2,26},{3,27},{4,7},{5,4},{6,5},{7,6},{8,0},{9,1},{1... | collective-permute-start | bytes 491528 | tf_op jit(solution)/shard_map/ppermute | solution.py:376
  84.5 3.8 %all-to-all-done.1 = bf16[64,16,256]{2,1,0:T(8,128)(2,1)S(1)} async-done(((bf16[64,16,256]{2,1,0:T(8,128)(2,1)}), bf16[64,16,256]{2,1,0:T(8,128)(2,1)S(1)}, u32[]{:S(2)}, u32[]{:S(2)}) %all-to-all-start.1) | async-done | bytes 524320 | tf_op jit(solution)/shard_map/all_to_all | solution.py:452
  88.3 1.5 %rows_back.1 = bf16[128,1024]{1,0:T(8,128)(2,1)} custom-call(s32[1,64]{1,0:T(1,128)S(1)} %copy-done.3, s32[1,64]{1,0:T(1,128)S(1)} %copy-done.4, bf16[1024,256]{1,0:T(8,128)(2,1)S(1)} %bitcast.12), custom_call_target="tpu_custom_call" | custom-call | tf_op jit(solution)/shard_map/rows_back/pallas_call | solution.py:30
  90.2 17.2 %all_to_all.20.parts = bf16[8,80,128]{2,1,0:T(8,128)(2,1)S(1)} all-to-all(bf16[8,80,128]{2,1,0:T(8,128)(2,1)S(1)} %add_last.1), channel_id=1, replica_groups=mesh['z'=8,'y'=4,'c'=2,'x'=4] {'z'}, dimensions={0} | all-to-all | bytes 327680 | tf_op jit(solution)/shard_map/all_to_all | solution.py:468
  107.4 11.9 %all_to_all.21.o0 = bf16[8,80,128]{2,1,0:T(8,128)(2,1)S(1)} all-to-all(bf16[8,80,128]{2,1,0:T(8,128)(2,1)S(1)} %add_eight.1), channel_id=1, replica_groups=mesh['z'=8,'y'=4,'c'=2,'x'=4] {'z'}, dimensions={0} | all-to-all | bytes 327680 | tf_op jit(solution)/shard_map/all_to_all | solution.py:470
  119.3 2.3 %collective-permute-start.18 = (bf16[8,80,128]{2,1,0:T(8,128)(2,1)S(1)}, bf16[8,80,128]{2,1,0:T(8,128)(2,1)S(1)}, u32[]{:S(2)}, u32[]{:S(2)}) collective-permute-start(bf16[8,80,128]{2,1,0:T(8,128)(2,1)S(1)} %all_to_all.21.o0), channel_id=1, source_target_pairs={{0,16},{8,24},{16,0},{24,8},{1,17},{9,25},{17,1},{25,9},{2,18},{10... | collective-permute-start | bytes 491528 | tf_op jit(solution)/shard_map/ppermute | solution.py:363
  122.3 2.5 %collective-permute-start.20 = (bf16[8,80,128]{2,1,0:T(8,128)(2,1)S(1)}, bf16[8,80,128]{2,1,0:T(8,128)(2,1)S(1)}, u32[]{:S(2)}, u32[]{:S(2)}) collective-permute-start(bf16[8,80,128]{2,1,0:T(8,128)(2,1)S(1)} %all_to_all.21.o0), channel_id=1, source_target_pairs={{0,4},{4,0},{1,5},{5,1},{2,6},{6,2},{3,7},{7,3},{8,12},{12,8},{9,1... | collective-permute-start | bytes 491528 | tf_op jit(solution)/shard_map/ppermute | solution.py:363
  124.8 2.8 %collective-permute-start.23 = (bf16[8,80,128]{2,1,0:T(8,128)(2,1)S(1)}, bf16[8,80,128]{2,1,0:T(8,128)(2,1)S(1)}, u32[]{:S(2)}, u32[]{:S(2)}) collective-permute-start(bf16[8,80,128]{2,1,0:T(8,128)(2,1)S(1)} %collective-permute-done.19.o3), channel_id=1, source_target_pairs={{0,4},{4,0},{1,5},{5,1},{2,6},{6,2},{3,7},{7,3},{8,12},{12,8},{9,1... | collective-permute-start | bytes 491528 | tf_op jit(solution)/shard_map/ppermute | solution.py:363
  127.6 1.9 %collective-permute-start.22 = (bf16[8,80,128]{2,1,0:T(8,128)(2,1)S(1)}, bf16[8,80,128]{2,1,0:T(8,128)(2,1)S(1)}, u32[]{:S(2)}, u32[]{:S(2)}) collective-permute-start(bf16[8,80,128]{2,1,0:T(8,128)(2,1)S(1)} %collective-permute-done.18.o2), channel_id=1, source_target_pairs={{0,4},{4,0},{1,5},{5,1},{2,6},{6,2},{3,7},{7,3},{8,12},{12,8},{9,1... | collective-permute-start | bytes 491528 | tf_op jit(solution)/shard_map/ppermute | solution.py:363
  129.5 1.7 %collective-permute-start.21 = (bf16[8,80,128]{2,1,0:T(8,128)(2,1)S(1)}, bf16[8,80,128]{2,1,0:T(8,128)(2,1)S(1)}, u32[]{:S(2)}, u32[]{:S(2)}) collective-permute-start(bf16[8,80,128]{2,1,0:T(8,128)(2,1)S(1)} %collective-permute-done.17.o1), channel_id=1, source_target_pairs={{0,4},{4,0},{1,5},{5,1},{2,6},{6,2},{3,7},{7,3},{8,12},{12,8},{9,1... | collective-permute-start | bytes 491528 | tf_op jit(solution)/shard_map/ppermute | solution.py:363
  131.2 1.0 collective-permute-done.21.t1
  132.2 2.0 %place.1 = (f32[256,2048]{1,0:T(8,128)}, f32[128,1024]{1,0:T(8,128)}) custom-call(bf16[8,80,128]{2,1,0:T(8,128)(2,1)S(1)} %all_to_all.21.o0, bf16[8,80,128]{2,1,0:T(8,128)(2,1)S(1)} %collective-permute-done.17.o1, bf16[8,80,128]{2,1,0:T(8,128)(2,1)S(1)} %collective-permute-done.18.o2, bf16[8,80,128]{2,1,0:T(8,128)(2,1)S(1)} %collective-permute-done.19.o3, ...), custom_call_target="tpu_custom_call" | custom-call | tf_op jit(solution)/shard_map/place/pallas_call | solution.py:30
  (45 shorter events, 6.4 us)
Async XLA Ops:
  0.6 36.9 %copy-start.4 = (s32[1,64]{1,0:T(1,128)S(1)}, s32[1,64]{1,0:T(1,128)}, u32[]{:S(2)}) copy-start(s32[1,64]{1,0:T(1,128)} %owners_ref.3) | copy-start | bytes 772
  0.6 36.9 %copy-start.3 = (s32[1,64]{1,0:T(1,128)S(1)}, s32[1,64]{1,0:T(1,128)}, u32[]{:S(2)}) copy-start(s32[1,64]{1,0:T(1,128)} %blocks_ref.3) | copy-start | bytes 772
  0.7 36.9 %copy-start = (bf16[256,2048]{1,0:T(8,128)(2,1)S(1)}, bf16[256,2048]{1,0:T(8,128)(2,1)}, u32[]{:S(2)}) copy-start(bf16[256,2048]{1,0:T(8,128)(2,1)} %w_in.5) | copy-start | bytes 3145732
  0.7 36.9 %copy-start.1 = (bf16[1,256,1024]{2,1,0:T(8,128)(2,1)S(1)}, bf16[1,256,1024]{2,1,0:T(8,128)(2,1)}, u32[]{:S(2)}) copy-start(bf16[1,256,1024]{2,1,0:T(8,128)(2,1)} %param.7) | copy-start | bytes 1572868
  3.7 17.1 %collective-permute-start.1 = (bf16[320,1024]{1,0:T(8,128)(2,1)}, bf16[320,1024]{1,0:T(8,128)(2,1)S(1)}, u32[]{:S(2)}, u32[]{:S(2)}) collective-permute-start(bf16[320,1024]{1,0:T(8,128)(2,1)} %get-tuple-element.35), channel_id=1, source_target_pairs={{0,3},{1,0},{2,1},{3,2},{4,7},{5,4},{6,5},{7,6},{8,11},{9,8},{10,9... | collective-permute-start | bytes 1966088 | tf_op jit(solution)/shard_map/ppermute | solution.py:363
  7.1 17.1 %collective-permute-start = (bf16[320,1024]{1,0:T(8,128)(2,1)}, bf16[320,1024]{1,0:T(8,128)(2,1)S(1)}, u32[]{:S(2)}, u32[]{:S(2)}) collective-permute-start(bf16[320,1024]{1,0:T(8,128)(2,1)} %get-tuple-element.35), channel_id=1, source_target_pairs={{0,1},{1,2},{2,3},{3,0},{4,5},{5,6},{6,7},{7,4},{8,9},{9,10},{10,1... | collective-permute-start | bytes 1966088 | tf_op jit(solution)/shard_map/ppermute | solution.py:363
  7.1 30.4 %all-to-all-start = ((bf16[64,16,256]{2,1,0:T(8,128)(2,1)}), bf16[64,16,256]{2,1,0:T(8,128)(2,1)}, u32[]{:S(2)}, u32[]{:S(2)}) async-start(bf16[64,16,256]{2,1,0:T(8,128)(2,1)} %bitcast.13), calls=%async_computation | async-start | bytes 1048576 | tf_op jit(solution)/shard_map/all_to_all | solution.py:400
  20.8 8.8 %collective-permute-start.3 = (bf16[160,1024]{1,0:T(8,128)(2,1)S(1)}, bf16[160,1024]{1,0:T(8,128)(2,1)}, u32[]{:S(2)}, u32[]{:S(2)}) collective-permute-start(bf16[160,1024]{1,0:T(8,128)(2,1)S(1)} %slice.9), channel_id=1, source_target_pairs={{0,3},{1,0},{2,1},{3,2},{4,7},{5,4},{6,5},{7,6},{8,11},{9,8},{10,9... | collective-permute-start | bytes 983048 | tf_op jit(solution)/shard_map/ppermute | solution.py:363
  24.2 8.8 %collective-permute-start.2 = (bf16[160,1024]{1,0:T(8,128)(2,1)S(1)}, bf16[160,1024]{1,0:T(8,128)(2,1)}, u32[]{:S(2)}, u32[]{:S(2)}) collective-permute-start(bf16[160,1024]{1,0:T(8,128)(2,1)S(1)} %slice.8), channel_id=1, source_target_pairs={{0,1},{1,2},{2,3},{3,0},{4,5},{5,6},{6,7},{7,4},{8,9},{9,10},{10,1... | collective-permute-start | bytes 983048 | tf_op jit(solution)/shard_map/ppermute | solution.py:363
  24.3 13.2 %collective-permute-start.5 = (bf16[320,1024]{1,0:T(8,128)(2,1)S(1)}, bf16[320,1024]{1,0:T(8,128)(2,1)S(1)}, u32[]{:S(2)}, u32[]{:S(2)}) collective-permute-start(bf16[320,1024]{1,0:T(8,128)(2,1)S(1)} %collective-permute-done.1.a2), channel_id=1, source_target_pairs={{0,4},{4,0},{1,5},{5,1},{2,6},{6,2},{3,7},{7,3},{8,12},{12,8},{9,1... | collective-permute-start | bytes 1966088 | tf_op jit(solution)/shard_map/ppermute | solution.py:363
  26.3 11.3 %collective-permute-start.4 = (bf16[320,1024]{1,0:T(8,128)(2,1)S(1)}, bf16[320,1024]{1,0:T(8,128)(2,1)}, u32[]{:S(2)}, u32[]{:S(2)}) collective-permute-start(bf16[320,1024]{1,0:T(8,128)(2,1)S(1)} %collective-permute-done.a1), channel_id=1, source_target_pairs={{0,4},{4,0},{1,5},{5,1},{2,6},{6,2},{3,7},{7,3},{8,12},{12,8},{9,1... | collective-permute-start | bytes 1966088 | tf_op jit(solution)/shard_map/ppermute | solution.py:363
  29.7 7.9 %collective-permute-start.7 = (bf16[160,1024]{1,0:T(8,128)(2,1)}, bf16[160,1024]{1,0:T(8,128)(2,1)}, u32[]{:S(2)}, u32[]{:S(2)}) collective-permute-start(bf16[160,1024]{1,0:T(8,128)(2,1)} %collective-permute-done.3.a4), channel_id=1, source_target_pairs={{0,4},{4,0},{1,5},{5,1},{2,6},{6,2},{3,7},{7,3},{8,12},{12,8},{9,1... | collective-permute-start | bytes 983048 | tf_op jit(solution)/shard_map/ppermute | solution.py:363
  33.0 4.5 %collective-permute-start.6 = (bf16[160,1024]{1,0:T(8,128)(2,1)}, bf16[160,1024]{1,0:T(8,128)(2,1)}, u32[]{:S(2)}, u32[]{:S(2)}) collective-permute-start(bf16[160,1024]{1,0:T(8,128)(2,1)} %collective-permute-done.2.a3), channel_id=1, source_target_pairs={{0,4},{4,0},{1,5},{5,1},{2,6},{6,2},{3,7},{7,3},{8,12},{12,8},{9,1... | collective-permute-start | bytes 983048 | tf_op jit(solution)/shard_map/ppermute | solution.py:363
  37.6 1.0 copy-start.2
  44.0 7.6 %collective-permute-start.8 = (bf16[4,256,512]{2,1,0:T(8,128)(2,1)S(1)}, bf16[4,256,512]{2,1,0:T(8,128)(2,1)S(1)}, u32[]{:S(2)}, u32[]{:S(2)}) collective-permute-start(bf16[4,256,512]{2,1,0:T(8,128)(2,1)S(1)} %get-tuple-element.36.shared), channel_id=1, source_target_pairs={{0,4},{4,0},{1,5},{5,1},{2,6},{6,2},{3,7},{7,3},{8,12},{12,8},{9,1... | collective-permute-start | bytes 3145736 | tf_op jit(solution)/shard_map/ppermute | solution.py:363
  47.2 4.4 %collective-permute-start.9 = (bf16[256,1024]{1,0:T(8,128)(2,1)S(1)}, bf16[256,1024]{1,0:T(8,128)(2,1)S(1)}, u32[]{:S(2)}, u32[]{:S(2)}) collective-permute-start(bf16[256,1024]{1,0:T(8,128)(2,1)S(1)} %get-tuple-element.48.sent), channel_id=1, source_target_pairs={{0,4},{4,0},{1,5},{5,1},{2,6},{6,2},{3,7},{7,3},{8,12},{12,8},{9,1... | collective-permute-start | bytes 1572872 | tf_op jit(solution)/shard_map/ppermute | solution.py:363
  55.3 15.2 %collective-permute-start.10 = (bf16[2,2,80,1024]{3,2,1,0:T(8,128)(2,1)}, bf16[2,2,80,1024]{3,2,1,0:T(8,128)(2,1)S(1)}, u32[]{:S(2)}, u32[]{:S(2)}) collective-permute-start(bf16[2,2,80,1024]{3,2,1,0:T(8,128)(2,1)} %get-tuple-element.52), channel_id=1, source_target_pairs={{0,1},{1,2},{2,3},{3,0},{4,12},{5,13},{6,14},{7,15},{8,9},{9,10},{... | collective-permute-start | bytes 1966088 | tf_op jit(solution)/shard_map/ppermute | solution.py:376
  56.4 14.1 %collective-permute-start.11 = (bf16[2,2,80,1024]{3,2,1,0:T(8,128)(2,1)}, bf16[2,2,80,1024]{3,2,1,0:T(8,128)(2,1)S(1)}, u32[]{:S(2)}, u32[]{:S(2)}) collective-permute-start(bf16[2,2,80,1024]{3,2,1,0:T(8,128)(2,1)} %get-tuple-element.53), channel_id=1, source_target_pairs={{0,3},{1,0},{2,1},{3,2},{4,28},{5,29},{6,30},{7,31},{8,11},{9,8},{... | collective-permute-start | bytes 1966088 | tf_op jit(solution)/shard_map/ppermute | solution.py:376
  58.0 30.3 %all-to-all-start.1 = ((bf16[64,16,256]{2,1,0:T(8,128)(2,1)}), bf16[64,16,256]{2,1,0:T(8,128)(2,1)S(1)}, u32[]{:S(2)}, u32[]{:S(2)}) async-start(bf16[64,16,256]{2,1,0:T(8,128)(2,1)} %bitcast.5), calls=%async_computation.1 | async-start | bytes 1048576 | tf_op jit(solution)/shard_map/all_to_all | solution.py:452
  70.7 9.7 %collective-permute-start.12 = (bf16[2,80,1024]{2,1,0:T(8,128)(2,1)S(1)}, bf16[2,80,1024]{2,1,0:T(8,128)(2,1)S(1)}, u32[]{:S(2)}, u32[]{:S(2)}) collective-permute-start(bf16[2,80,1024]{2,1,0:T(8,128)(2,1)S(1)} %get-tuple-element.54), channel_id=1, source_target_pairs={{0,1},{1,2},{2,3},{3,0},{4,12},{5,13},{6,14},{7,15},{8,9},{9,10},{... | collective-permute-start | bytes 983048 | tf_op jit(solution)/shard_map/ppermute | solution.py:376
  72.2 8.8 %collective-permute-start.13 = (bf16[2,80,1024]{2,1,0:T(8,128)(2,1)S(1)}, bf16[2,80,1024]{2,1,0:T(8,128)(2,1)S(1)}, u32[]{:S(2)}, u32[]{:S(2)}) collective-permute-start(bf16[2,80,1024]{2,1,0:T(8,128)(2,1)S(1)} %get-tuple-element.55), channel_id=1, source_target_pairs={{0,3},{1,0},{2,1},{3,2},{4,28},{5,29},{6,30},{7,31},{8,11},{9,8},{... | collective-permute-start | bytes 983048 | tf_op jit(solution)/shard_map/ppermute | solution.py:376
  81.8 8.0 %collective-permute-start.14 = (bf16[80,1024]{1,0:T(8,128)(2,1)}, bf16[80,1024]{1,0:T(8,128)(2,1)S(1)}, u32[]{:S(2)}, u32[]{:S(2)}) collective-permute-start(bf16[80,1024]{1,0:T(8,128)(2,1)} %get-tuple-element.56), channel_id=1, source_target_pairs={{0,8},{1,9},{2,10},{3,11},{4,5},{5,6},{6,7},{7,4},{8,16},{9,17},{1... | collective-permute-start | bytes 491528 | tf_op jit(solution)/shard_map/ppermute | solution.py:376
  81.8 8.0 %collective-permute-start.15 = (bf16[80,1024]{1,0:T(8,128)(2,1)}, bf16[80,1024]{1,0:T(8,128)(2,1)S(1)}, u32[]{:S(2)}, u32[]{:S(2)}) collective-permute-start(bf16[80,1024]{1,0:T(8,128)(2,1)} %get-tuple-element.60), channel_id=1, source_target_pairs={{0,16},{1,17},{2,18},{3,19},{4,6},{5,7},{6,4},{7,5},{8,24},{9,25},... | collective-permute-start | bytes 491528 | tf_op jit(solution)/shard_map/ppermute | solution.py:376
  82.7 7.4 %collective-permute-start.16 = (bf16[80,1024]{1,0:T(8,128)(2,1)}, bf16[80,1024]{1,0:T(8,128)(2,1)S(1)}, u32[]{:S(2)}, u32[]{:S(2)}) collective-permute-start(bf16[80,1024]{1,0:T(8,128)(2,1)} %get-tuple-element.61), channel_id=1, source_target_pairs={{0,24},{1,25},{2,26},{3,27},{4,7},{5,4},{6,5},{7,6},{8,0},{9,1},{1... | collective-permute-start | bytes 491528 | tf_op jit(solution)/shard_map/ppermute | solution.py:376
  119.3 5.5 %collective-permute-start.19 = (bf16[8,80,128]{2,1,0:T(8,128)(2,1)S(1)}, bf16[8,80,128]{2,1,0:T(8,128)(2,1)S(1)}, u32[]{:S(2)}, u32[]{:S(2)}) collective-permute-start(bf16[8,80,128]{2,1,0:T(8,128)(2,1)S(1)} %all_to_all.21.o0), channel_id=1, source_target_pairs={{0,24},{8,0},{16,8},{24,16},{1,25},{9,1},{17,9},{25,17},{2,26},{10... | collective-permute-start | bytes 491528 | tf_op jit(solution)/shard_map/ppermute | solution.py:363
  119.3 8.3 %collective-permute-start.18 = (bf16[8,80,128]{2,1,0:T(8,128)(2,1)S(1)}, bf16[8,80,128]{2,1,0:T(8,128)(2,1)S(1)}, u32[]{:S(2)}, u32[]{:S(2)}) collective-permute-start(bf16[8,80,128]{2,1,0:T(8,128)(2,1)S(1)} %all_to_all.21.o0), channel_id=1, source_target_pairs={{0,16},{8,24},{16,0},{24,8},{1,17},{9,25},{17,1},{25,9},{2,18},{10... | collective-permute-start | bytes 491528 | tf_op jit(solution)/shard_map/ppermute | solution.py:363
  121.6 7.9 %collective-permute-start.17 = (bf16[8,80,128]{2,1,0:T(8,128)(2,1)S(1)}, bf16[8,80,128]{2,1,0:T(8,128)(2,1)S(1)}, u32[]{:S(2)}, u32[]{:S(2)}) collective-permute-start(bf16[8,80,128]{2,1,0:T(8,128)(2,1)S(1)} %all_to_all.21.o0), channel_id=1, source_target_pairs={{0,8},{8,16},{16,24},{24,0},{1,9},{9,17},{17,25},{25,1},{2,10},{10... | collective-permute-start | bytes 491528 | tf_op jit(solution)/shard_map/ppermute | solution.py:363
  122.3 8.9 %collective-permute-start.20 = (bf16[8,80,128]{2,1,0:T(8,128)(2,1)S(1)}, bf16[8,80,128]{2,1,0:T(8,128)(2,1)S(1)}, u32[]{:S(2)}, u32[]{:S(2)}) collective-permute-start(bf16[8,80,128]{2,1,0:T(8,128)(2,1)S(1)} %all_to_all.21.o0), channel_id=1, source_target_pairs={{0,4},{4,0},{1,5},{5,1},{2,6},{6,2},{3,7},{7,3},{8,12},{12,8},{9,1... | collective-permute-start | bytes 491528 | tf_op jit(solution)/shard_map/ppermute | solution.py:363
  124.8 6.4 %collective-permute-start.23 = (bf16[8,80,128]{2,1,0:T(8,128)(2,1)S(1)}, bf16[8,80,128]{2,1,0:T(8,128)(2,1)S(1)}, u32[]{:S(2)}, u32[]{:S(2)}) collective-permute-start(bf16[8,80,128]{2,1,0:T(8,128)(2,1)S(1)} %collective-permute-done.19.o3), channel_id=1, source_target_pairs={{0,4},{4,0},{1,5},{5,1},{2,6},{6,2},{3,7},{7,3},{8,12},{12,8},{9,1... | collective-permute-start | bytes 491528 | tf_op jit(solution)/shard_map/ppermute | solution.py:363
  127.6 3.6 %collective-permute-start.22 = (bf16[8,80,128]{2,1,0:T(8,128)(2,1)S(1)}, bf16[8,80,128]{2,1,0:T(8,128)(2,1)S(1)}, u32[]{:S(2)}, u32[]{:S(2)}) collective-permute-start(bf16[8,80,128]{2,1,0:T(8,128)(2,1)S(1)} %collective-permute-done.18.o2), channel_id=1, source_target_pairs={{0,4},{4,0},{1,5},{5,1},{2,6},{6,2},{3,7},{7,3},{8,12},{12,8},{9,1... | collective-permute-start | bytes 491528 | tf_op jit(solution)/shard_map/ppermute | solution.py:363
  129.5 2.7 %collective-permute-start.21 = (bf16[8,80,128]{2,1,0:T(8,128)(2,1)S(1)}, bf16[8,80,128]{2,1,0:T(8,128)(2,1)S(1)}, u32[]{:S(2)}, u32[]{:S(2)}) collective-permute-start(bf16[8,80,128]{2,1,0:T(8,128)(2,1)S(1)} %collective-permute-done.17.o1), channel_id=1, source_target_pairs={{0,4},{4,0},{1,5},{5,1},{2,6},{6,2},{3,7},{7,3},{8,12},{12,8},{9,1... | collective-permute-start | bytes 491528 | tf_op jit(solution)/shard_map/ppermute | solution.py:363

commit v5 on v4

--- a/solution.py
+++ b/solution.py
@@ -11,7 +11,8 @@
 BF16 = jnp.bfloat16
 EPS = 1e-06
 HEAD = 128
-DP = ("z", "y", "c")
+Z = ("zh", "zl")
+DP = ("zh", "zl", "y", "c")
 NN = (((1,), (0,)), ((), ()))
 NT = (((1,), (1,)), ((), ()))
 TN = (((0,), (0,)), ((), ()))
@@ -36,6 +37,10 @@
         compiler_params=pltpu.CompilerParams(vmem_limit_bytes=mib * MIB),
         name=name,
     )(*args)
+
+
+def half_columns(half, width):
+    return pl.ds(pl.multiple_of(half * width, width), width)
 
 
 def histories(blocks_ref, owners_ref):
@@ -53,35 +58,35 @@
     return n_row, o_row, n_col, o_col, start, before_col, before_row
 
 
-def slots_of_rows(blocks_ref, owners_ref, count):
+def slots_of_rows(blocks_ref, owners_ref, count, core=0):
     _, _, n_col, o_col, start, before, _ = histories(blocks_ref, owners_ref)
+    o_col = (o_col.astype(jnp.int32) ^ core).astype(F32)
     b = iota((n_col.shape[0], count), 1).astype(F32)
     inside = (start <= b) & (b < start + n_col)
     code = jnp.sum(jnp.where(inside, o_col * 4.0 + before - start, 0.0), axis=0, keepdims=True)
     return (code + b[:1]).astype(jnp.int32)
 
 
-def entry_body(blocks_hbm, owners_hbm, x_hbm, w_in, w_out, out_ref, pack, blocks, owners, rows, sems):
+def pack_body(w_in, w_out, pack, sems):
     half = lax.axis_index("c")
-    wide = pl.ds(pl.multiple_of(half * 1024, 1024), 1024)
-    left = pl.ds(pl.multiple_of(half * 1024 // 2, 512), 512)
+    wide, narrow = half_columns(half, 1024), half_columns(half, 512)
     copies = [
         pltpu.make_async_copy(a, b, sems.at[i])
         for i, (a, b) in enumerate(
             (
-                (blocks_hbm, blocks),
-                (owners_hbm, owners),
-                (x_hbm, rows),
                 (w_in.at[:, wide], pack.at[pl.ds(0, 256), :]),
-                (w_out.at[pl.ds(0, 64), left], pack.at[pl.ds(256, 64), pl.ds(0, 512)]),
-                (w_out.at[pl.ds(64, 64), left], pack.at[pl.ds(256, 64), pl.ds(512, 512)]),
+                (w_out.at[pl.ds(0, 64), narrow], pack.at[pl.ds(256, 64), pl.ds(0, 512)]),
+                (w_out.at[pl.ds(64, 64), narrow], pack.at[pl.ds(256, 64), pl.ds(512, 512)]),
             )
         )
     ]
     for copy in copies:
         copy.start()
-    for copy in copies[:3]:
+    for copy in copies:
         copy.wait()
+
+
+def rows_out_body(blocks, owners, rows, out_ref):
     code = slots_of_rows(blocks, owners, 128)
     row = iota((1024, 128), 0)
     total = None
@@ -90,12 +95,10 @@
         part = dot(pick, rows[:, j * 256 : (j + 1) * 256])
         total = part if total is None else total + part
     out_ref[...] = total.astype(BF16)
-    for copy in copies[3:]:
-        copy.wait()
 
 
 def rows_back(blocks_ref, owners_ref, returned_ref, out_ref):
-    code = slots_of_rows(blocks_ref, owners_ref, 128)
+    code = slots_of_rows(blocks_ref, owners_ref, 128, lax.axis_index("c"))
     eye = iota((128, 128), 0) == iota((128, 128), 1)
     column = jnp.sum(jnp.where(eye, code.astype(F32), 0.0), axis=1, keepdims=True).astype(jnp.int32)
     lane = iota((128, 1024), 1)
@@ -135,17 +138,13 @@
 ROWS = 256
 
 
-def half_columns(half, width):
-    return pl.ds(pl.multiple_of(half * width, width), width)
-
-
 def forward_body(
     blocks_ref, owners_ref, arrived, cot, w_in, w_out, a1, a2, a3, a4, b1, b2, b3, b4,
     shared, owned, rstd, act, dsilu, hat, att_rstd, weights, dscore, w_full,
     wide, pre,
 ):
     x, y, c = lax.axis_index("x"), lax.axis_index("y"), lax.axis_index("c")
-    me = (lax.axis_index("z") * 4 + y) * 2 + c
+    me = ((lax.axis_index("zh") * 4 + lax.axis_index("zl")) * 4 + y) * 2 + c
     proj, back = weights_of(x, c, (w_in, w_out, (a1, a2, a3, a4), (b1, b2, b3, b4)))
     halves = ((True, c), (False, 1 - c))
 
@@ -265,7 +264,7 @@
 
 def rest_body(
     shared, rstd, cot, kept, sent, w_in, a1, a2, a3, a4, b1, b2, b3, b4,
-    outgoing, dnorm, wide,
+    same, across, dnorm, wide,
 ):
     x, c = lax.axis_index("x"), lax.axis_index("c")
     proj, _ = weights_of(x, c, (w_in, None, (a1, a2, a3, a4), (b1, b2, b3, b4)))
@@ -282,11 +281,19 @@
         for j in range(8):
             part = d[s * 64 : (s + 1) * 64, j * 128 : (j + 1) * 128]
             wide.at[j % 2][pl.ds(s * 4 + j // 2, 64, stride=16), :] = part
-    for i in range(2):
-        outgoing[:, i * 128 : (i + 1) * 128] = wide[i].astype(BF16)
-
-
-def sum_pair_body(shared, other, kept, received, cot, backward, ahead, behind, held_own, held):
+    for out, side in ((same, c), (across, 1 - c)):
+        for chip in range(32):
+            rows = pl.ds(pl.multiple_of((chip * 2 + side) * 16, 16), 16)
+            for i in range(2):
+                out[chip, :, i * 128 : (i + 1) * 128] = wide.at[i][rows, :].astype(BF16)
+
+
+def both_sides_body(same, across, out):
+    out[:, :16, :] = same[...]
+    out[:, 16:, :] = across[...]
+
+
+def sum_pair_body(shared, other, kept, received, cot, same, ahead, behind, held_own, held):
     x, y, c = lax.axis_index("x"), lax.axis_index("y"), lax.axis_index("c")
     right = cot[:, half_columns(c, 512)]
     other_right = jnp.concatenate([other[j, :, 384:] for j in range(4)], axis=1)
@@ -326,29 +333,35 @@
         outs[s][...] = total.astype(BF16)
 
 
-def add_last_body(a0, a1, a2, a3, out):
+def add_last_body(a0, a1, a2, a3, *refs):
+    outs, held = refs[:4], refs[4]
+    zl = lax.axis_index("zl")
     total = a0[...].astype(F32) + a1[...].astype(F32) + a2[...].astype(F32) + a3[...].astype(F32)
     total = total.astype(BF16)
-    for j in range(8):
-        out[j] = total[:, j * 128 : (j + 1) * 128]
-
-
-def add_eight_body(parts, out):
-    total = parts[0].astype(F32)
-    for i in range(1, 8):
-        total = total + parts[i].astype(F32)
+    for j in range(4):
+        held[(j + 4 - zl) % 4] = total[:, j * 256 : (j + 1) * 256]
+    for s in range(4):
+        outs[s][...] = held[s]
+
+
+def add_near_body(a0, a1, a2, a3, out):
+    total = a0[...].astype(F32) + a1[...].astype(F32) + a2[...].astype(F32) + a3[...].astype(F32)
     total = total.astype(BF16)
     for i in range(8):
         out[i] = total
+
+
+def join_body(parts, out):
+    for j in range(4):
+        total = parts[j].astype(F32) + parts[4 + j].astype(F32)
+        out[:, j * 256 : (j + 1) * 256] = total.astype(BF16)
 
 
 def place_body(o0, o1, o2, o3, t0, t1, t2, t3, g_in, g_out, rows):
     y, c = lax.axis_index("y"), lax.axis_index("c")
     for refs, h in (((o0, o1, o2, o3), c), ((t0, t1, t2, t3), 1 - c)):
         for s in range(4):
-            m = (y + 4 - s) % 4
-            for j in range(8):
-                rows[h, m, :, j * 128 : (j + 1) * 128] = refs[s][j]
+            rows[h, (y + 4 - s) % 4] = refs[s][...]
     factor = 1.0 / 256.0
     for h in range(2):
         for m in range(3):
@@ -373,30 +386,28 @@
                     ty, tx = (y, (x + s) % 4) if over_x else ((y + s) % 4, x)
                     at = lambda v, w: ((z * 4 + v) * 2 + c) * 4 + w
                     pairs.append((at(y, x), at(ty, tx)))
-    return lax.ppermute(a, ("z", "y", "c", "x"), pairs)
+    return lax.ppermute(a, ("zh", "zl", "y", "c", "x"), pairs)
 
 
 def on_device(x_rows, cotangent, w_in, w_out, hist_blocks, owner):
     cot = cotangent[0]
-    hbm = pl.BlockSpec(memory_space=pltpu.HBM)
-    outgoing, pack = pl.pallas_call(
-        entry_body,
-        out_shape=[
-            jax.ShapeDtypeStruct((1024, 256), BF16),
-            jax.ShapeDtypeStruct((320, 1024), BF16),
-        ],
-        in_specs=[hbm] * 5,
-        out_specs=[pl.BlockSpec(memory_space=pltpu.VMEM)] * 2,
-        scratch_shapes=[
-            pltpu.VMEM((1, 64), jnp.int32),
-            pltpu.VMEM((1, 64), jnp.int32),
-            pltpu.VMEM((128, 1024), BF16),
-            pltpu.SemaphoreType.DMA((6,)),
-        ],
+    pack = pl.pallas_call(
+        pack_body,
+        out_shape=jax.ShapeDtypeStruct((320, 1024), BF16),
+        in_specs=[pl.BlockSpec(memory_space=pltpu.HBM)] * 2,
+        out_specs=pl.BlockSpec(memory_space=pltpu.VMEM),
+        scratch_shapes=[pltpu.SemaphoreType.DMA((3,))],
         compiler_params=pltpu.CompilerParams(vmem_limit_bytes=60 * MIB),
-        name="entry",
-    )(hist_blocks, owner, x_rows[0], w_in, w_out)
+        name="pack",
+    )(w_in, w_out)
     left, right = shift(pack, "x", 4, 1), shift(pack, "x", 4, 3)
+    (outgoing,) = call(
+        rows_out_body,
+        [((1024, 256), BF16)],
+        (hist_blocks, owner, x_rows[0]),
+        "rows_out",
+        mib=60,
+    )
     arrived = lax.all_to_all(
         outgoing.reshape(64, 16, 256), DP, split_axis=0, concat_axis=0, tiled=True
     ).reshape(1024, 256)
@@ -431,9 +442,9 @@
         mib=12,
     )
     received = shift(sent, "c", 2, 1)
-    (backward,) = call(
+    same, across = call(
         rest_body,
-        [((1024, 256), BF16)],
+        [((32, 16, 256), BF16)] * 2,
         (shared, rstd, cot, kept, sent, w_in) + weights[2:],
         "rest",
         scratch=[((4, 256, 256), BF16), ((2, 1024, 128), F32)],
@@ -442,15 +453,17 @@
     ahead, behind, kept = call(
         sum_pair_body,
         [((2, 2, 80, 1024), BF16), ((2, 2, 80, 1024), BF16), ((8, 80, 1024), BF16)],
-        (shared, other, kept, received, cot, backward),
+        (shared, other, kept, received, cot, same),
         "sum_pair",
         scratch=[((4, 4, 80, 1024), BF16)],
         mib=12,
     )
-    backward, kept = lax.optimization_barrier((backward, kept))
+    across = shift(across, "c", 2, 1)
+    across, kept = lax.optimization_barrier((across, kept))
+    (backward,) = call(both_sides_body, [((32, 32, 256), BF16)], (same, across), "both_sides")
     ahead, behind = crossed(ahead, 1, True), crossed(behind, 3, True)
     returned = lax.all_to_all(
-        backward.reshape(64, 16, 256), DP, split_axis=0, concat_axis=0, tiled=True
+        backward, ("zh", "zl", "y"), split_axis=0, concat_axis=0, tiled=True
     ).reshape(1024, 256)
     forth, back = call(
         add_relayed_body, [((2, 80, 1024), BF16)] * 2, (kept, ahead, behind), "add_relayed"
@@ -464,10 +477,17 @@
         rows_back, [((128, 1024), BF16)], (hist_blocks, owner, returned), "rows_back"
     )
     grad_rows, second[1] = lax.optimization_barrier((grad_rows, second[1]))
-    (columns,) = call(add_last_body, [((8, 80, 128), BF16)], second, "add_last")
-    parts = lax.all_to_all(columns, "z", split_axis=0, concat_axis=0, tiled=True)
-    (summed,) = call(add_eight_body, [((8, 80, 128), BF16)], (parts,), "add_eight")
-    mine = lax.all_to_all(summed, "z", split_axis=0, concat_axis=0, tiled=True)
+    quarters = call(
+        add_last_body,
+        [((80, 256), BF16)] * 4,
+        second,
+        "add_last",
+        scratch=[((4, 80, 256), BF16)],
+    )
+    near = [quarters[0]] + [shift(quarters[s], "zl", 4, s) for s in (1, 2, 3)]
+    (summed,) = call(add_near_body, [((8, 80, 256), BF16)], near, "add_near")
+    parts = lax.all_to_all(summed, Z, split_axis=0, concat_axis=0, tiled=True)
+    (mine,) = call(join_body, [((80, 1024), BF16)], (parts,), "join")
     lines = [mine] + [shift(mine, "y", 4, s) for s in (1, 2, 3)]
     paired = [shift(a, "c", 2, 1) for a in lines]
     g_in, g_out = call(
@@ -481,7 +501,7 @@
 
 
 def solution(mesh):
-    fine = Mesh(mesh.devices.reshape(8, 4, 2, 4), ("z", "y", "c", "x"))
+    fine = Mesh(mesh.devices.reshape(2, 4, 4, 2, 4), ("zh", "zl", "y", "c", "x"))
     placed = (
         P("x", DP, None),
         P("x", DP, None),

time: 135 us -> 129 us (0.956)
  blocking collectives: 29.1 us -> 16.1 us
  waiting for transfers between devices: 19.5 us -> 24.8 us
    all_to_all x2 -> x1, blocking collectives: 29.1 us -> 16.1 us  [on_device(): parts = lax.all_to_all(summed, Z, split_axis=0, concat_axis=0, tiled=True)]
    all_to_all x1, starting transfers between devices: 12.5 us -> 7.26 us  [on_device(): lax.all_to_all(backward, ('zh', 'zl', 'y'), split_axis=0, concat_axis=0,...]
    ppermute x17 -> x21, starting transfers between devices: 26.8 us -> 31.9 us  [shift(): return lax.ppermute(a, axis, [(i, (i + s) % n) for i in range(n)])]
    ppermute x7, waiting for transfers between devices: 7.7 us -> 11.8 us  [crossed(): return lax.ppermute(a, ('zh', 'zl', 'y', 'c', 'x'), pairs)]
    ppermute x17 -> x21, waiting for transfers between devices: 6.16 us -> 10 us  [shift(): return lax.ppermute(a, axis, [(i, (i + s) % n) for i in range(n)])]
    all_to_all x1, waiting for transfers between devices: 3.84 us -> 0.01 us  [on_device(): lax.all_to_all(backward, ('zh', 'zl', 'y'), split_axis=0, concat_axis=0,...]
    pallas_call x10 -> x13, Pallas kernels: 20.6 us -> 21.4 us  [call(): pl.pallas_call(body, out_shape=[jax.ShapeDtypeStruct(s, d) for s, d in ou...]
  transfers between devices with their start and end apart: 26 -> 30, of which waited for: 9 -> 11; matrix products, arithmetic and copies ran while one was open for 0% -> 0% of each run, Pallas kernels for 7% -> 11%
where the time goes in v5:
time: 129 us; the launch traced here: 128 us
  starting transfers between devices  61.2 us (47%)
  waiting for transfers between devices  24.8 us (19%)
  Pallas kernels  23.4 us (18%)
  blocking collectives  16.1 us (12%)
  local copies, waits for them, and re-layouts  1.8 us (1%)
    ppermute x21, starting transfers between devices, shift(): return lax.ppermute(a, axis, [(i, (i + s) % n) for i in range(n)])  31.9 us
    pallas_call x13, Pallas kernels, call(): pl.pallas_call(body, out_shape=[jax.ShapeDtypeStruct(s, d) for s, d in ou...  21.4 us
    all_to_all x1, blocking collectives, on_device(): parts = lax.all_to_all(summed, Z, split_axis=0, concat_axis=0, tiled=True)  16.1 us
    all_to_all x1, starting transfers between devices, on_device(): lax.all_to_all(outgoing.reshape(64, 16, 256), DP, split_axis=0, concat_ax...  12.8 us
    ppermute x7, waiting for transfers between devices, crossed(): return lax.ppermute(a, ('zh', 'zl', 'y', 'c', 'x'), pairs)  11.8 us
    ppermute x21, waiting for transfers between devices, shift(): return lax.ppermute(a, axis, [(i, (i + s) % n) for i in range(n)])  10 us
    ppermute x7, starting transfers between devices, crossed(): return lax.ppermute(a, ('zh', 'zl', 'y', 'c', 'x'), pairs)  9.23 us
    all_to_all x1, starting transfers between devices, on_device(): lax.all_to_all(backward, ('zh', 'zl', 'y'), split_axis=0, concat_axis=0,...  7.26 us
  transfers between devices with their start and end apart: 30, of which 11 were waited for; matrix products, arithmetic and copies ran while one was open for 0% of the time, Pallas kernels for 11%

profile of v5, /device:TPU:1, one launch (start us, length us, event | category | flops | bytes accessed | tf_op | source)
XLA Modules:
  0.0 128.2 jit_solution(3833406118266953310)
XLA Ops:
  0.7 2.0 %pack.1 = bf16[320,1024]{1,0:T(8,128)(2,1)} custom-call(bf16[256,2048]{1,0:T(8,128)(2,1)} %w_in.5, bf16[128,1024]{1,0:T(8,128)(2,1)} %w_out.3), custom_call_target="tpu_custom_call" | custom-call | tf_op jit(solution)/shard_map/pack/pallas_call | solution.py:394
  2.7 3.4 %collective-permute-start.1 = (bf16[320,1024]{1,0:T(8,128)(2,1)}, bf16[320,1024]{1,0:T(8,128)(2,1)S(1)}, u32[]{:S(2)}, u32[]{:S(2)}) collective-permute-start(bf16[320,1024]{1,0:T(8,128)(2,1)} %pack.1), channel_id=1, source_target_pairs={{0,3},{1,0},{2,1},{3,2},{4,7},{5,4},{6,5},{7,6},{8,11},{9,8},{10,9... | collective-permute-start | bytes 1966088 | tf_op jit(solution)/shard_map/ppermute | solution.py:376
  6.1 2.6 %rows_out.1 = bf16[1024,256]{1,0:T(8,128)(2,1)} custom-call(s32[1,64]{1,0:T(1,128)} %blocks_ref.3, s32[1,64]{1,0:T(1,128)} %owners_ref.3, bf16[128,1024]{1,0:T(8,128)(2,1)} %bitcast.13), custom_call_target="tpu_custom_call" | custom-call | tf_op jit(solution)/shard_map/rows_out/pallas_call | solution.py:31
  8.7 12.8 %all-to-all-start = ((bf16[64,16,256]{2,1,0:T(8,128)(2,1)}), bf16[64,16,256]{2,1,0:T(8,128)(2,1)}, u32[]{:S(2)}, u32[]{:S(2)}) async-start(bf16[64,16,256]{2,1,0:T(8,128)(2,1)} %bitcast.12), calls=%async_computation | async-start | bytes 1048576 | tf_op jit(solution)/shard_map/all_to_all | solution.py:411
  21.6 3.0 %collective-permute-start.3 = (bf16[160,1024]{1,0:T(8,128)(2,1)S(1)}, bf16[160,1024]{1,0:T(8,128)(2,1)}, u32[]{:S(2)}, u32[]{:S(2)}) collective-permute-start(bf16[160,1024]{1,0:T(8,128)(2,1)S(1)} %slice.9), channel_id=1, source_target_pairs={{0,3},{1,0},{2,1},{3,2},{4,7},{5,4},{6,5},{7,6},{8,11},{9,8},{10,9... | collective-permute-start | bytes 983048 | tf_op jit(solution)/shard_map/ppermute | solution.py:376
  25.7 5.4 %collective-permute-done.3.a4 = bf16[160,1024]{1,0:T(8,128)(2,1)} collective-permute-done((bf16[160,1024]{1,0:T(8,128)(2,1)S(1)}, bf16[160,1024]{1,0:T(8,128)(2,1)}, u32[]{:S(2)}, u32[]{:S(2)}) %collective-permute-start.3) | collective-permute-done | bytes 327712 | tf_op jit(solution)/shard_map/ppermute | solution.py:376
  31.1 1.4 %collective-permute-start.7 = (bf16[160,1024]{1,0:T(8,128)(2,1)}, bf16[160,1024]{1,0:T(8,128)(2,1)}, u32[]{:S(2)}, u32[]{:S(2)}) collective-permute-start(bf16[160,1024]{1,0:T(8,128)(2,1)} %collective-permute-done.3.a4), channel_id=1, source_target_pairs={{0,4},{4,0},{1,5},{5,1},{2,6},{6,2},{3,7},{7,3},{8,12},{12,8},{9,1... | collective-permute-start | bytes 983048 | tf_op jit(solution)/shard_map/ppermute | solution.py:376
  32.5 1.9 %collective-permute-done.2.a3 = bf16[160,1024]{1,0:T(8,128)(2,1)} collective-permute-done((bf16[160,1024]{1,0:T(8,128)(2,1)S(1)}, bf16[160,1024]{1,0:T(8,128)(2,1)}, u32[]{:S(2)}, u32[]{:S(2)}) %collective-permute-start.2) | collective-permute-done | bytes 327712 | tf_op jit(solution)/shard_map/ppermute | solution.py:376
  34.5 1.7 %collective-permute-start.6 = (bf16[160,1024]{1,0:T(8,128)(2,1)}, bf16[160,1024]{1,0:T(8,128)(2,1)}, u32[]{:S(2)}, u32[]{:S(2)}) collective-permute-start(bf16[160,1024]{1,0:T(8,128)(2,1)} %collective-permute-done.2.a3), channel_id=1, source_target_pairs={{0,4},{4,0},{1,5},{5,1},{2,6},{6,2},{3,7},{7,3},{8,12},{12,8},{9,1... | collective-permute-start | bytes 983048 | tf_op jit(solution)/shard_map/ppermute | solution.py:376
  36.2 3.0 %all-to-all-done = bf16[64,16,256]{2,1,0:T(8,128)(2,1)} async-done(((bf16[64,16,256]{2,1,0:T(8,128)(2,1)}), bf16[64,16,256]{2,1,0:T(8,128)(2,1)}, u32[]{:S(2)}, u32[]{:S(2)}) %all-to-all-start) | async-done | bytes 524320 | tf_op jit(solution)/shard_map/all_to_all | solution.py:411
  40.2 5.4 %forward.1 = (bf16[4,256,512]{2,1,0:T(8,128)(2,1)S(1)}, bf16[256,1024]{1,0:T(8,128)(2,1)S(1)}, f32[256,128]{1,0:T(8,128)S(1)}, bf16[2,256,1024]{2,1,0:T(8,128)(2...) custom-call(s32[1,64]{1,0:T(1,128)S(1)} %copy-done.4, ...), custom_call_target="tpu_custom_call" | custom-call | tf_op jit(solution)/shard_map/forward/pallas_call | solution.py:31
  46.3 2.5 %backward.1 = (bf16[256,1024]{1,0:T(8,128)(2,1)}, bf16[256,1024]{1,0:T(8,128)(2,1)S(1)}, bf16[256,1024]{1,0:T(8,128)(2,1)S(1)}) custom-call(bf16[4,256,512]{2,1,0:T(8,128)(2,1)S(1)} %get-tuple-element.38.shared, bf16[256,1024]{1,0:T(8,128)(2,1)S(1)} %get-tuple-element.39.owned, bf16[256,1024]{1,0:T(8,128)(2,1)S(1)} %bitcast.8, ...), custom_call_target="tpu_custom_call" | custom-call | tf_op jit(solution)/shard_map/backward/pallas_call | solution.py:31
  48.9 3.6 %rest.1 = (bf16[32,16,256]{2,1,0:T(8,128)(2,1)S(1)}, bf16[32,16,256]{2,1,0:T(8,128)(2,1)S(1)}) custom-call(bf16[4,256,512]{2,1,0:T(8,128)(2,1)S(1)} %get-tuple-element.38.shared, f32[256,128]{1,0:T(8,128)S(1)} %get-tuple-element.48.rstd, bf16[256,1024]{1,0:T(8,128)(2,1)S(1)} %bitcast.9, bf16[256,1024]{1,0:T(8,128)(2,1)S(1)} %get-tuple-element.49.kept, ...), custom_call_target="tpu_custom_call" | custom-call | tf_op jit(solution)/shard_map/rest/pallas_call | solution.py:31
  53.0 2.7 %sum_pair.1 = (bf16[2,2,80,1024]{3,2,1,0:T(8,128)(2,1)}, bf16[2,2,80,1024]{3,2,1,0:T(8,128)(2,1)}, bf16[8,80,1024]{2,1,0:T(8,128)(2,1)S(1)}) custom-call(bf16[4,256,512]{2,1,0:T(8,128)(2,1)S(1)} %get-tuple-element.38.shared, bf16[4,256,512]{2,1,0:T(8,128)(2,1)S(1)} %collective-permute-done.9.other, bf16[256,1024]{1,0:T(8,128)(2,1)S(1)} %get-tuple-element.49.kept, ...), custom_call_target="tpu_custom_call" | custom-call | tf_op jit(solution)/shard_map/sum_pair/pallas_call | solution.py:31
  56.9 1.5 %collective-permute-start.12 = (bf16[2,2,80,1024]{3,2,1,0:T(8,128)(2,1)}, bf16[2,2,80,1024]{3,2,1,0:T(8,128)(2,1)S(1)}, u32[]{:S(2)}, u32[]{:S(2)}) collective-permute-start(bf16[2,2,80,1024]{3,2,1,0:T(8,128)(2,1)} %get-tuple-element.57), channel_id=1, source_target_pairs={{0,3},{1,0},{2,1},{3,2},{4,28},{5,29},{6,30},{7,31},{8,11},{9,8},{... | collective-permute-start | bytes 1966088 | tf_op jit(solution)/shard_map/ppermute | solution.py:389
  59.2 7.3 %all-to-all-start.1 = ((bf16[32,32,256]{2,1,0:T(8,128)(2,1)}), bf16[32,32,256]{2,1,0:T(8,128)(2,1)S(1)}, u32[]{:S(2)}, u32[]{:S(2)}) async-start(bf16[32,32,256]{2,1,0:T(8,128)(2,1)} %copy-done.2), calls=%async_computation.1 | async-start | bytes 1048576 | tf_op jit(solution)/shard_map/all_to_all | solution.py:465
  67.0 1.3 collective-permute-start.13
  68.2 1.6 %collective-permute-start.14 = (bf16[2,80,1024]{2,1,0:T(8,128)(2,1)S(1)}, bf16[2,80,1024]{2,1,0:T(8,128)(2,1)S(1)}, u32[]{:S(2)}, u32[]{:S(2)}) collective-permute-start(bf16[2,80,1024]{2,1,0:T(8,128)(2,1)S(1)} %get-tuple-element.59), channel_id=1, source_target_pairs={{0,3},{1,0},{2,1},{3,2},{4,28},{5,29},{6,30},{7,31},{8,11},{9,8},{... | collective-permute-start | bytes 983048 | tf_op jit(solution)/shard_map/ppermute | solution.py:389
  69.8 6.6 %collective-permute-done.13.forth = bf16[2,80,1024]{2,1,0:T(8,128)(2,1)S(1)} collective-permute-done((bf16[2,80,1024]{2,1,0:T(8,128)(2,1)S(1)}, bf16[2,80,1024]{2,1,0:T(8,128)(2,1)S(1)}, u32[]{:S(2)}, u32[]{:S(2)}) %collective-permute-start.13) | collective-permute-done | bytes 327712 | tf_op jit(solution)/shard_map/ppermute | solution.py:389
  76.4 1.7 %collective-permute-done.14.back = bf16[2,80,1024]{2,1,0:T(8,128)(2,1)S(1)} collective-permute-done((bf16[2,80,1024]{2,1,0:T(8,128)(2,1)S(1)}, bf16[2,80,1024]{2,1,0:T(8,128)(2,1)S(1)}, u32[]{:S(2)}, u32[]{:S(2)}) %collective-permute-start.14) | collective-permute-done | bytes 327712 | tf_op jit(solution)/shard_map/ppermute | solution.py:389
  79.5 3.2 %collective-permute-start.16 = (bf16[80,1024]{1,0:T(8,128)(2,1)}, bf16[80,1024]{1,0:T(8,128)(2,1)S(1)}, u32[]{:S(2)}, u32[]{:S(2)}) collective-permute-start(bf16[80,1024]{1,0:T(8,128)(2,1)} %get-tuple-element.64), channel_id=1, source_target_pairs={{0,16},{1,17},{2,18},{3,19},{4,6},{5,7},{6,4},{7,5},{8,24},{9,25},... | collective-permute-start | bytes 491528 | tf_op jit(solution)/shard_map/ppermute | solution.py:389
  82.7 1.5 %rows_back.1 = bf16[128,1024]{1,0:T(8,128)(2,1)} custom-call(s32[1,64]{1,0:T(1,128)S(1)} %copy-done.4, s32[1,64]{1,0:T(1,128)S(1)} %copy-done.5, bf16[1024,256]{1,0:T(8,128)(2,1)S(1)} %bitcast.11), custom_call_target="tpu_custom_call" | custom-call | tf_op jit(solution)/shard_map/rows_back/pallas_call | solution.py:31
  84.8 2.5 %collective-permute-done.16.a2 = bf16[80,1024]{1,0:T(8,128)(2,1)S(1)} collective-permute-done((bf16[80,1024]{1,0:T(8,128)(2,1)}, bf16[80,1024]{1,0:T(8,128)(2,1)S(1)}, u32[]{:S(2)}, u32[]{:S(2)}) %collective-permute-start.16) | collective-permute-done | bytes 163872 | tf_op jit(solution)/shard_map/ppermute | solution.py:389
  88.6 2.7 %collective-permute-start.19 = (bf16[80,256]{1,0:T(8,128)(2,1)S(1)}, bf16[80,256]{1,0:T(8,128)(2,1)S(1)}, u32[]{:S(2)}, u32[]{:S(2)}) collective-permute-start(bf16[80,256]{1,0:T(8,128)(2,1)S(1)} %get-tuple-element.68), channel_id=1, source_target_pairs={{0,64},{32,96},{64,0},{96,32},{1,65},{33,97},{65,1},{97,33},{2,66}... | collective-permute-start | bytes 122888 | tf_op jit(solution)/shard_map/ppermute | solution.py:376
  91.2 1.7 %collective-permute-start.20 = (bf16[80,256]{1,0:T(8,128)(2,1)S(1)}, bf16[80,256]{1,0:T(8,128)(2,1)S(1)}, u32[]{:S(2)}, u32[]{:S(2)}) collective-permute-start(bf16[80,256]{1,0:T(8,128)(2,1)S(1)} %get-tuple-element.69), channel_id=1, source_target_pairs={{0,96},{32,0},{64,32},{96,64},{1,97},{33,1},{65,33},{97,65},{2,98}... | collective-permute-start | bytes 122888 | tf_op jit(solution)/shard_map/ppermute | solution.py:376
  94.6 16.1 %all_to_all.15.parts = bf16[8,80,256]{2,1,0:T(8,128)(2,1)S(1)} all-to-all(bf16[8,80,256]{2,1,0:T(8,128)(2,1)S(1)} %add_near.1), channel_id=1, replica_groups=mesh['zh'=2,'zl'=4,'y'=4,'c'=2,'x'=4] {'zh','zl'}, dimensions={0} | all-to-all | bytes 655360 | tf_op jit(solution)/shard_map/all_to_all | solution.py:489
  110.8 2.5 %collective-permute-start.23 = (bf16[80,1024]{1,0:T(8,128)(2,1)S(1)}, bf16[80,1024]{1,0:T(8,128)(2,1)S(1)}, u32[]{:S(2)}, u32[]{:S(2)}) collective-permute-start(bf16[80,1024]{1,0:T(8,128)(2,1)S(1)} %join.1.o0), channel_id=1, source_target_pairs={{0,24},{8,0},{16,8},{24,16},{1,25},{9,1},{17,9},{25,17},{2,26},{10... | collective-permute-start | bytes 491528 | tf_op jit(solution)/shard_map/ppermute | solution.py:376
  113.9 4.0 %collective-permute-start.24 = (bf16[80,1024]{1,0:T(8,128)(2,1)S(1)}, bf16[80,1024]{1,0:T(8,128)(2,1)S(1)}, u32[]{:S(2)}, u32[]{:S(2)}) collective-permute-start(bf16[80,1024]{1,0:T(8,128)(2,1)S(1)} %join.1.o0), channel_id=1, source_target_pairs={{0,4},{4,0},{1,5},{5,1},{2,6},{6,2},{3,7},{7,3},{8,12},{12,8},{9,1... | collective-permute-start | bytes 491528 | tf_op jit(solution)/shard_map/ppermute | solution.py:376
  117.9 3.6 %collective-permute-start.27 = (bf16[80,1024]{1,0:T(8,128)(2,1)S(1)}, bf16[80,1024]{1,0:T(8,128)(2,1)S(1)}, u32[]{:S(2)}, u32[]{:S(2)}) collective-permute-start(bf16[80,1024]{1,0:T(8,128)(2,1)S(1)} %collective-permute-done.23.o3), channel_id=1, source_target_pairs={{0,4},{4,0},{1,5},{5,1},{2,6},{6,2},{3,7},{7,3},{8,12},{12,8},{9,1... | collective-permute-start | bytes 491528 | tf_op jit(solution)/shard_map/ppermute | solution.py:376
  121.5 2.3 %collective-permute-start.26 = (bf16[80,1024]{1,0:T(8,128)(2,1)S(1)}, bf16[80,1024]{1,0:T(8,128)(2,1)S(1)}, u32[]{:S(2)}, u32[]{:S(2)}) collective-permute-start(bf16[80,1024]{1,0:T(8,128)(2,1)S(1)} %collective-permute-done.22.o2), channel_id=1, source_target_pairs={{0,4},{4,0},{1,5},{5,1},{2,6},{6,2},{3,7},{7,3},{8,12},{12,8},{9,1... | collective-permute-start | bytes 491528 | tf_op jit(solution)/shard_map/ppermute | solution.py:376
  123.8 1.6 %collective-permute-start.25 = (bf16[80,1024]{1,0:T(8,128)(2,1)S(1)}, bf16[80,1024]{1,0:T(8,128)(2,1)S(1)}, u32[]{:S(2)}, u32[]{:S(2)}) collective-permute-start(bf16[80,1024]{1,0:T(8,128)(2,1)S(1)} %collective-permute-done.21.o1), channel_id=1, source_target_pairs={{0,4},{4,0},{1,5},{5,1},{2,6},{6,2},{3,7},{7,3},{8,12},{12,8},{9,1... | collective-permute-start | bytes 491528 | tf_op jit(solution)/shard_map/ppermute | solution.py:376
  126.4 1.8 %place.1 = (f32[256,2048]{1,0:T(8,128)}, f32[128,1024]{1,0:T(8,128)}) custom-call(bf16[80,1024]{1,0:T(8,128)(2,1)S(1)} %join.1.o0, bf16[80,1024]{1,0:T(8,128)(2,1)S(1)} %collective-permute-done.21.o1, bf16[80,1024]{1,0:T(8,128)(2,1)S(1)} %collective-permute-done.22.o2, bf16[80,1024]{1,0:T(8,128)(2,1)S(1)} %collective-permute-done.23.o3, ...), custom_call_target="tpu_custom_call" | custom-call | tf_op jit(solution)/shard_map/place/pallas_call | solution.py:31
  (57 shorter events, 12.6 us)
Async XLA Ops:
  0.6 38.6 %copy-start = (bf16[256,2048]{1,0:T(8,128)(2,1)S(1)}, bf16[256,2048]{1,0:T(8,128)(2,1)}, u32[]{:S(2)}) copy-start(bf16[256,2048]{1,0:T(8,128)(2,1)} %w_in.5) | copy-start | bytes 3145732
  0.6 38.6 %copy-start.5 = (s32[1,64]{1,0:T(1,128)S(1)}, s32[1,64]{1,0:T(1,128)}, u32[]{:S(2)}) copy-start(s32[1,64]{1,0:T(1,128)} %owners_ref.3) | copy-start | bytes 772
  2.7 18.8 %collective-permute-start.1 = (bf16[320,1024]{1,0:T(8,128)(2,1)}, bf16[320,1024]{1,0:T(8,128)(2,1)S(1)}, u32[]{:S(2)}, u32[]{:S(2)}) collective-permute-start(bf16[320,1024]{1,0:T(8,128)(2,1)} %pack.1), channel_id=1, source_target_pairs={{0,3},{1,0},{2,1},{3,2},{4,7},{5,4},{6,5},{7,6},{8,11},{9,8},{10,9... | collective-permute-start | bytes 1966088 | tf_op jit(solution)/shard_map/ppermute | solution.py:376
  6.1 18.5 %collective-permute-start = (bf16[320,1024]{1,0:T(8,128)(2,1)}, bf16[320,1024]{1,0:T(8,128)(2,1)S(1)}, u32[]{:S(2)}, u32[]{:S(2)}) collective-permute-start(bf16[320,1024]{1,0:T(8,128)(2,1)} %pack.1), channel_id=1, source_target_pairs={{0,1},{1,2},{2,3},{3,0},{4,5},{5,6},{6,7},{7,4},{8,9},{9,10},{10,1... | collective-permute-start | bytes 1966088 | tf_op jit(solution)/shard_map/ppermute | solution.py:376
  8.7 30.4 %all-to-all-start = ((bf16[64,16,256]{2,1,0:T(8,128)(2,1)}), bf16[64,16,256]{2,1,0:T(8,128)(2,1)}, u32[]{:S(2)}, u32[]{:S(2)}) async-start(bf16[64,16,256]{2,1,0:T(8,128)(2,1)} %bitcast.12), calls=%async_computation | async-start | bytes 1048576 | tf_op jit(solution)/shard_map/all_to_all | solution.py:411
  21.6 9.6 %collective-permute-start.3 = (bf16[160,1024]{1,0:T(8,128)(2,1)S(1)}, bf16[160,1024]{1,0:T(8,128)(2,1)}, u32[]{:S(2)}, u32[]{:S(2)}) collective-permute-start(bf16[160,1024]{1,0:T(8,128)(2,1)S(1)} %slice.9), channel_id=1, source_target_pairs={{0,3},{1,0},{2,1},{3,2},{4,7},{5,4},{6,5},{7,6},{8,11},{9,8},{10,9... | collective-permute-start | bytes 983048 | tf_op jit(solution)/shard_map/ppermute | solution.py:376
  24.6 9.8 %collective-permute-start.2 = (bf16[160,1024]{1,0:T(8,128)(2,1)S(1)}, bf16[160,1024]{1,0:T(8,128)(2,1)}, u32[]{:S(2)}, u32[]{:S(2)}) collective-permute-start(bf16[160,1024]{1,0:T(8,128)(2,1)S(1)} %slice.8), channel_id=1, source_target_pairs={{0,1},{1,2},{2,3},{3,0},{4,5},{5,6},{6,7},{7,4},{8,9},{9,10},{10,1... | collective-permute-start | bytes 983048 | tf_op jit(solution)/shard_map/ppermute | solution.py:376
  24.7 14.4 %collective-permute-start.5 = (bf16[320,1024]{1,0:T(8,128)(2,1)S(1)}, bf16[320,1024]{1,0:T(8,128)(2,1)S(1)}, u32[]{:S(2)}, u32[]{:S(2)}) collective-permute-start(bf16[320,1024]{1,0:T(8,128)(2,1)S(1)} %collective-permute-done.1.a2), channel_id=1, source_target_pairs={{0,4},{4,0},{1,5},{5,1},{2,6},{6,2},{3,7},{7,3},{8,12},{12,8},{9,1... | collective-permute-start | bytes 1966088 | tf_op jit(solution)/shard_map/ppermute | solution.py:376
  25.6 13.6 %collective-permute-start.4 = (bf16[320,1024]{1,0:T(8,128)(2,1)S(1)}, bf16[320,1024]{1,0:T(8,128)(2,1)}, u32[]{:S(2)}, u32[]{:S(2)}) collective-permute-start(bf16[320,1024]{1,0:T(8,128)(2,1)S(1)} %collective-permute-done.a1), channel_id=1, source_target_pairs={{0,4},{4,0},{1,5},{5,1},{2,6},{6,2},{3,7},{7,3},{8,12},{12,8},{9,1... | collective-permute-start | bytes 1966088 | tf_op jit(solution)/shard_map/ppermute | solution.py:376
  31.1 8.0 %collective-permute-start.7 = (bf16[160,1024]{1,0:T(8,128)(2,1)}, bf16[160,1024]{1,0:T(8,128)(2,1)}, u32[]{:S(2)}, u32[]{:S(2)}) collective-permute-start(bf16[160,1024]{1,0:T(8,128)(2,1)} %collective-permute-done.3.a4), channel_id=1, source_target_pairs={{0,4},{4,0},{1,5},{5,1},{2,6},{6,2},{3,7},{7,3},{8,12},{12,8},{9,1... | collective-permute-start | bytes 983048 | tf_op jit(solution)/shard_map/ppermute | solution.py:376
  34.5 4.7 %collective-permute-start.6 = (bf16[160,1024]{1,0:T(8,128)(2,1)}, bf16[160,1024]{1,0:T(8,128)(2,1)}, u32[]{:S(2)}, u32[]{:S(2)}) collective-permute-start(bf16[160,1024]{1,0:T(8,128)(2,1)} %collective-permute-done.2.a3), channel_id=1, source_target_pairs={{0,4},{4,0},{1,5},{5,1},{2,6},{6,2},{3,7},{7,3},{8,12},{12,8},{9,1... | collective-permute-start | bytes 983048 | tf_op jit(solution)/shard_map/ppermute | solution.py:376
  45.6 7.4 %collective-permute-start.9 = (bf16[4,256,512]{2,1,0:T(8,128)(2,1)S(1)}, bf16[4,256,512]{2,1,0:T(8,128)(2,1)S(1)}, u32[]{:S(2)}, u32[]{:S(2)}) collective-permute-start(bf16[4,256,512]{2,1,0:T(8,128)(2,1)S(1)} %get-tuple-element.38.shared), channel_id=1, source_target_pairs={{0,4},{4,0},{1,5},{5,1},{2,6},{6,2},{3,7},{7,3},{8,12},{12,8},{9,1... | collective-permute-start | bytes 3145736 | tf_op jit(solution)/shard_map/ppermute | solution.py:376
  48.8 4.2 %collective-permute-start.10 = (bf16[256,1024]{1,0:T(8,128)(2,1)S(1)}, bf16[256,1024]{1,0:T(8,128)(2,1)S(1)}, u32[]{:S(2)}, u32[]{:S(2)}) collective-permute-start(bf16[256,1024]{1,0:T(8,128)(2,1)S(1)} %get-tuple-element.50.sent), channel_id=1, source_target_pairs={{0,4},{4,0},{1,5},{5,1},{2,6},{6,2},{3,7},{7,3},{8,12},{12,8},{9,1... | collective-permute-start | bytes 1572872 | tf_op jit(solution)/shard_map/ppermute | solution.py:376
  52.5 5.8 %collective-permute-start.8 = (bf16[32,16,256]{2,1,0:T(8,128)(2,1)S(1)}, bf16[32,16,256]{2,1,0:T(8,128)(2,1)S(1)}, u32[]{:S(2)}, u32[]{:S(2)}) collective-permute-start(bf16[32,16,256]{2,1,0:T(8,128)(2,1)S(1)} %get-tuple-element.52), channel_id=1, source_target_pairs={{0,4},{4,0},{1,5},{5,1},{2,6},{6,2},{3,7},{7,3},{8,12},{12,8},{9,1... | collective-permute-start | bytes 786440 | tf_op jit(solution)/shard_map/ppermute | solution.py:376
  55.7 11.2 %collective-permute-start.11 = (bf16[2,2,80,1024]{3,2,1,0:T(8,128)(2,1)}, bf16[2,2,80,1024]{3,2,1,0:T(8,128)(2,1)S(1)}, u32[]{:S(2)}, u32[]{:S(2)}) collective-permute-start(bf16[2,2,80,1024]{3,2,1,0:T(8,128)(2,1)} %get-tuple-element.56), channel_id=1, source_target_pairs={{0,1},{1,2},{2,3},{3,0},{4,12},{5,13},{6,14},{7,15},{8,9},{9,10},{... | collective-permute-start | bytes 1966088 | tf_op jit(solution)/shard_map/ppermute | solution.py:389
  56.9 10.0 %collective-permute-start.12 = (bf16[2,2,80,1024]{3,2,1,0:T(8,128)(2,1)}, bf16[2,2,80,1024]{3,2,1,0:T(8,128)(2,1)S(1)}, u32[]{:S(2)}, u32[]{:S(2)}) collective-permute-start(bf16[2,2,80,1024]{3,2,1,0:T(8,128)(2,1)} %get-tuple-element.57), channel_id=1, source_target_pairs={{0,3},{1,0},{2,1},{3,2},{4,28},{5,29},{6,30},{7,31},{8,11},{9,8},{... | collective-permute-start | bytes 1966088 | tf_op jit(solution)/shard_map/ppermute | solution.py:389
  59.2 23.5 %all-to-all-start.1 = ((bf16[32,32,256]{2,1,0:T(8,128)(2,1)}), bf16[32,32,256]{2,1,0:T(8,128)(2,1)S(1)}, u32[]{:S(2)}, u32[]{:S(2)}) async-start(bf16[32,32,256]{2,1,0:T(8,128)(2,1)} %copy-done.2), calls=%async_computation.1 | async-start | bytes 1048576 | tf_op jit(solution)/shard_map/all_to_all | solution.py:465
  67.0 9.4 %collective-permute-start.13 = (bf16[2,80,1024]{2,1,0:T(8,128)(2,1)S(1)}, bf16[2,80,1024]{2,1,0:T(8,128)(2,1)S(1)}, u32[]{:S(2)}, u32[]{:S(2)}) collective-permute-start(bf16[2,80,1024]{2,1,0:T(8,128)(2,1)S(1)} %get-tuple-element.58), channel_id=1, source_target_pairs={{0,1},{1,2},{2,3},{3,0},{4,12},{5,13},{6,14},{7,15},{8,9},{9,10},{... | collective-permute-start | bytes 983048 | tf_op jit(solution)/shard_map/ppermute | solution.py:389
  68.2 9.8 %collective-permute-start.14 = (bf16[2,80,1024]{2,1,0:T(8,128)(2,1)S(1)}, bf16[2,80,1024]{2,1,0:T(8,128)(2,1)S(1)}, u32[]{:S(2)}, u32[]{:S(2)}) collective-permute-start(bf16[2,80,1024]{2,1,0:T(8,128)(2,1)S(1)} %get-tuple-element.59), channel_id=1, source_target_pairs={{0,3},{1,0},{2,1},{3,2},{4,28},{5,29},{6,30},{7,31},{8,11},{9,8},{... | collective-permute-start | bytes 983048 | tf_op jit(solution)/shard_map/ppermute | solution.py:389
  79.0 5.9 %collective-permute-start.15 = (bf16[80,1024]{1,0:T(8,128)(2,1)}, bf16[80,1024]{1,0:T(8,128)(2,1)S(1)}, u32[]{:S(2)}, u32[]{:S(2)}) collective-permute-start(bf16[80,1024]{1,0:T(8,128)(2,1)} %get-tuple-element.60), channel_id=1, source_target_pairs={{0,8},{1,9},{2,10},{3,11},{4,5},{5,6},{6,7},{7,4},{8,16},{9,17},{1... | collective-permute-start | bytes 491528 | tf_op jit(solution)/shard_map/ppermute | solution.py:389
  79.5 7.9 %collective-permute-start.16 = (bf16[80,1024]{1,0:T(8,128)(2,1)}, bf16[80,1024]{1,0:T(8,128)(2,1)S(1)}, u32[]{:S(2)}, u32[]{:S(2)}) collective-permute-start(bf16[80,1024]{1,0:T(8,128)(2,1)} %get-tuple-element.64), channel_id=1, source_target_pairs={{0,16},{1,17},{2,18},{3,19},{4,6},{5,7},{6,4},{7,5},{8,24},{9,25},... | collective-permute-start | bytes 491528 | tf_op jit(solution)/shard_map/ppermute | solution.py:389
  82.7 4.7 %collective-permute-start.17 = (bf16[80,1024]{1,0:T(8,128)(2,1)S(1)}, bf16[80,1024]{1,0:T(8,128)(2,1)S(1)}, u32[]{:S(2)}, u32[]{:S(2)}) collective-permute-start(bf16[80,1024]{1,0:T(8,128)(2,1)S(1)} %get-tuple-element.65), channel_id=1, source_target_pairs={{0,24},{1,25},{2,26},{3,27},{4,7},{5,4},{6,5},{7,6},{8,0},{9,1},{1... | collective-permute-start | bytes 491528 | tf_op jit(solution)/shard_map/ppermute | solution.py:389
  87.5 5.4 %collective-permute-start.18 = (bf16[80,256]{1,0:T(8,128)(2,1)S(1)}, bf16[80,256]{1,0:T(8,128)(2,1)S(1)}, u32[]{:S(2)}, u32[]{:S(2)}) collective-permute-start(bf16[80,256]{1,0:T(8,128)(2,1)S(1)} %get-tuple-element.67), channel_id=1, source_target_pairs={{0,32},{32,64},{64,96},{96,0},{1,33},{33,65},{65,97},{97,1},{2,34}... | collective-permute-start | bytes 122888 | tf_op jit(solution)/shard_map/ppermute | solution.py:376
  88.6 4.9 %collective-permute-start.19 = (bf16[80,256]{1,0:T(8,128)(2,1)S(1)}, bf16[80,256]{1,0:T(8,128)(2,1)S(1)}, u32[]{:S(2)}, u32[]{:S(2)}) collective-permute-start(bf16[80,256]{1,0:T(8,128)(2,1)S(1)} %get-tuple-element.68), channel_id=1, source_target_pairs={{0,64},{32,96},{64,0},{96,32},{1,65},{33,97},{65,1},{97,33},{2,66}... | collective-permute-start | bytes 122888 | tf_op jit(solution)/shard_map/ppermute | solution.py:376
  91.2 3.3 %collective-permute-start.20 = (bf16[80,256]{1,0:T(8,128)(2,1)S(1)}, bf16[80,256]{1,0:T(8,128)(2,1)S(1)}, u32[]{:S(2)}, u32[]{:S(2)}) collective-permute-start(bf16[80,256]{1,0:T(8,128)(2,1)S(1)} %get-tuple-element.69), channel_id=1, source_target_pairs={{0,96},{32,0},{64,32},{96,64},{1,97},{33,1},{65,33},{97,65},{2,98}... | collective-permute-start | bytes 122888 | tf_op jit(solution)/shard_map/ppermute | solution.py:376
  110.8 7.1 %collective-permute-start.23 = (bf16[80,1024]{1,0:T(8,128)(2,1)S(1)}, bf16[80,1024]{1,0:T(8,128)(2,1)S(1)}, u32[]{:S(2)}, u32[]{:S(2)}) collective-permute-start(bf16[80,1024]{1,0:T(8,128)(2,1)S(1)} %join.1.o0), channel_id=1, source_target_pairs={{0,24},{8,0},{16,8},{24,16},{1,25},{9,1},{17,9},{25,17},{2,26},{10... | collective-permute-start | bytes 491528 | tf_op jit(solution)/shard_map/ppermute | solution.py:376
  113.2 8.2 %collective-permute-start.22 = (bf16[80,1024]{1,0:T(8,128)(2,1)S(1)}, bf16[80,1024]{1,0:T(8,128)(2,1)S(1)}, u32[]{:S(2)}, u32[]{:S(2)}) collective-permute-start(bf16[80,1024]{1,0:T(8,128)(2,1)S(1)} %join.1.o0), channel_id=1, source_target_pairs={{0,16},{8,24},{16,0},{24,8},{1,17},{9,25},{17,1},{25,9},{2,18},{10... | collective-permute-start | bytes 491528 | tf_op jit(solution)/shard_map/ppermute | solution.py:376
  113.4 10.3 %collective-permute-start.21 = (bf16[80,1024]{1,0:T(8,128)(2,1)S(1)}, bf16[80,1024]{1,0:T(8,128)(2,1)S(1)}, u32[]{:S(2)}, u32[]{:S(2)}) collective-permute-start(bf16[80,1024]{1,0:T(8,128)(2,1)S(1)} %join.1.o0), channel_id=1, source_target_pairs={{0,8},{8,16},{16,24},{24,0},{1,9},{9,17},{17,25},{25,1},{2,10},{10... | collective-permute-start | bytes 491528 | tf_op jit(solution)/shard_map/ppermute | solution.py:376
  113.9 11.5 %collective-permute-start.24 = (bf16[80,1024]{1,0:T(8,128)(2,1)S(1)}, bf16[80,1024]{1,0:T(8,128)(2,1)S(1)}, u32[]{:S(2)}, u32[]{:S(2)}) collective-permute-start(bf16[80,1024]{1,0:T(8,128)(2,1)S(1)} %join.1.o0), channel_id=1, source_target_pairs={{0,4},{4,0},{1,5},{5,1},{2,6},{6,2},{3,7},{7,3},{8,12},{12,8},{9,1... | collective-permute-start | bytes 491528 | tf_op jit(solution)/shard_map/ppermute | solution.py:376
  117.9 7.5 %collective-permute-start.27 = (bf16[80,1024]{1,0:T(8,128)(2,1)S(1)}, bf16[80,1024]{1,0:T(8,128)(2,1)S(1)}, u32[]{:S(2)}, u32[]{:S(2)}) collective-permute-start(bf16[80,1024]{1,0:T(8,128)(2,1)S(1)} %collective-permute-done.23.o3), channel_id=1, source_target_pairs={{0,4},{4,0},{1,5},{5,1},{2,6},{6,2},{3,7},{7,3},{8,12},{12,8},{9,1... | collective-permute-start | bytes 491528 | tf_op jit(solution)/shard_map/ppermute | solution.py:376
  121.5 4.0 %collective-permute-start.26 = (bf16[80,1024]{1,0:T(8,128)(2,1)S(1)}, bf16[80,1024]{1,0:T(8,128)(2,1)S(1)}, u32[]{:S(2)}, u32[]{:S(2)}) collective-permute-start(bf16[80,1024]{1,0:T(8,128)(2,1)S(1)} %collective-permute-done.22.o2), channel_id=1, source_target_pairs={{0,4},{4,0},{1,5},{5,1},{2,6},{6,2},{3,7},{7,3},{8,12},{12,8},{9,1... | collective-permute-start | bytes 491528 | tf_op jit(solution)/shard_map/ppermute | solution.py:376
  123.8 2.7 %collective-permute-start.25 = (bf16[80,1024]{1,0:T(8,128)(2,1)S(1)}, bf16[80,1024]{1,0:T(8,128)(2,1)S(1)}, u32[]{:S(2)}, u32[]{:S(2)}) collective-permute-start(bf16[80,1024]{1,0:T(8,128)(2,1)S(1)} %collective-permute-done.21.o1), channel_id=1, source_target_pairs={{0,4},{4,0},{1,5},{5,1},{2,6},{6,2},{3,7},{7,3},{8,12},{12,8},{9,1... | collective-permute-start | bytes 491528 | tf_op jit(solution)/shard_map/ppermute | solution.py:376
  (4 other events, 78.9 us)

commit v6 on v5

--- a/solution.py
+++ b/solution.py
@@ -260,6 +260,21 @@
         dpre[1, :, 512 + lo : 512 + hi] = (dk * dsilu[1, :, 512 + lo : 512 + hi]).astype(BF16)
     kept[...] = dpre[c]
     sent[...] = dpre[1 - c]
+
+
+def layer_body(
+    blocks_ref, owners_ref, arrived, cot, w_in, w_out, a1, a2, a3, a4, b1, b2, b3, b4,
+    shared, rstd, out, kept, sent,
+    owned, act, dsilu, hat, att_rstd, weights, dscore, w_full, wide, pre, dpre, dmixed, datt,
+):
+    forward_body(
+        blocks_ref, owners_ref, arrived, cot, w_in, w_out, a1, a2, a3, a4, b1, b2, b3, b4,
+        shared, owned, rstd, act, dsilu, hat, att_rstd, weights, dscore, w_full, wide, pre,
+    )
+    backward_body(
+        shared, owned, cot, act, dsilu, hat, att_rstd, weights, dscore, w_full,
+        out, kept, sent, dpre, dmixed, datt,
+    )
 
 
 def rest_body(
@@ -413,12 +428,19 @@
     ).reshape(1024, 256)
     own = [left, right, shift(left[:160], "x", 4, 1), shift(right[160:], "x", 4, 3)]
     weights = (w_in, w_out, *own, *[shift(a, "c", 2, 1) for a in own])
-    shared, owned, rstd, act, dsilu, hat, att_rstd, scores, dscore, w_full = call(
-        forward_body,
+    shared, rstd, layer_out, kept, sent = call(
+        layer_body,
         [
             ((4, 256, 512), BF16),
+            ((256, 128), F32),
             ((256, 1024), BF16),
-            ((256, 128), F32),
+            ((256, 1024), BF16),
+            ((256, 1024), BF16),
+        ],
+        (hist_blocks, owner, arrived, cot) + weights,
+        "layer",
+        scratch=[
+            ((256, 1024), BF16),
             ((2, 256, 1024), BF16),
             ((2, 256, 1024), F32),
             ((256, 512), F32),
@@ -426,21 +448,15 @@
             ((4, 256, 256), BF16),
             ((4, 256, 256), F32),
             ((4, 128, 1024), BF16),
+            ((2, 1024, 128), F32),
+            ((2, 256, 1024), F32),
+            ((2, 256, 1024), BF16),
+            ((256, 512), BF16),
+            ((256, 512), BF16),
         ],
-        (hist_blocks, owner, arrived, cot) + weights,
-        "forward",
-        scratch=[((2, 1024, 128), F32), ((2, 256, 1024), F32)],
-        mib=20,
+        mib=28,
     )
     other = shift(shared, "c", 2, 1)
-    layer_out, kept, sent = call(
-        backward_body,
-        [((256, 1024), BF16)] * 3,
-        (shared, owned, cot, act, dsilu, hat, att_rstd, scores, dscore, w_full),
-        "backward",
-        scratch=[((2, 256, 1024), BF16), ((256, 512), BF16), ((256, 512), BF16)],
-        mib=12,
-    )
     received = shift(sent, "c", 2, 1)
     same, across = call(
         rest_body,

time: 129 us -> 126 us (0.977)
  starting transfers between devices: 61.2 us -> 55 us
  waiting for transfers between devices: 24.8 us -> 28.6 us
    ppermute x21, starting transfers between devices: 31.9 us -> 27.3 us  [shift(): return lax.ppermute(a, axis, [(i, (i + s) % n) for i in range(n)])]
    all_to_all x1, waiting for transfers between devices: 3.01 us -> 6.05 us  [on_device(): lax.all_to_all(outgoing.reshape(64, 16, 256), DP, split_axis=0, concat_ax...]
    all_to_all x1, starting transfers between devices: 7.26 us -> 5.38 us  [on_device(): lax.all_to_all(backward, ('zh', 'zl', 'y'), split_axis=0, concat_axis=0,...]
    pallas_call x13 -> x12, Pallas kernels: 21.4 us -> 20.9 us  [call(): pl.pallas_call(body, out_shape=[jax.ShapeDtypeStruct(s, d) for s, d in ou...]
  transfers between devices with their start and end apart: 30 -> 30, of which waited for: 11 -> 10; matrix products, arithmetic and copies ran while one was open for 0% -> 0% of each run, Pallas kernels for 11% -> 9%
where the time goes in v6:
time: 126 us; the launch traced here: 125 us
  starting transfers between devices  55 us (44%)
  waiting for transfers between devices  28.6 us (23%)
  Pallas kernels  22.9 us (18%)
  blocking collectives  16 us (13%)
  local copies, waits for them, and re-layouts  1.8 us (1%)
    ppermute x21, starting transfers between devices, shift(): return lax.ppermute(a, axis, [(i, (i + s) % n) for i in range(n)])  27.3 us
    pallas_call x12, Pallas kernels, call(): pl.pallas_call(body, out_shape=[jax.ShapeDtypeStruct(s, d) for s, d in ou...  20.9 us
    all_to_all x1, blocking collectives, on_device(): parts = lax.all_to_all(summed, Z, split_axis=0, concat_axis=0, tiled=True)  16 us
    all_to_all x1, starting transfers between devices, on_device(): lax.all_to_all(outgoing.reshape(64, 16, 256), DP, split_axis=0, concat_ax...  13 us
    ppermute x7, waiting for transfers between devices, crossed(): return lax.ppermute(a, ('zh', 'zl', 'y', 'c', 'x'), pairs)  13 us
    ppermute x21, waiting for transfers between devices, shift(): return lax.ppermute(a, axis, [(i, (i + s) % n) for i in range(n)])  9.57 us
    ppermute x7, starting transfers between devices, crossed(): return lax.ppermute(a, ('zh', 'zl', 'y', 'c', 'x'), pairs)  9.31 us
    all_to_all x1, waiting for transfers between devices, on_device(): lax.all_to_all(outgoing.reshape(64, 16, 256), DP, split_axis=0, concat_ax...  6.05 us
  transfers between devices with their start and end apart: 30, of which 10 were waited for; matrix products, arithmetic and copies ran while one was open for 0% of the time, Pallas kernels for 9%

profile of v6, /device:TPU:1, one launch (start us, length us, event | category | flops | bytes accessed | tf_op | source)
XLA Modules:
  0.0 125.1 jit_solution(18387642441354713964)
XLA Ops:
  0.7 2.0 %pack.1 = bf16[320,1024]{1,0:T(8,128)(2,1)} custom-call(bf16[256,2048]{1,0:T(8,128)(2,1)} %w_in.5, bf16[128,1024]{1,0:T(8,128)(2,1)} %w_out.3), custom_call_target="tpu_custom_call" | custom-call | tf_op jit(solution)/shard_map/pack/pallas_call | solution.py:409
  2.7 2.1 %collective-permute-start = (bf16[320,1024]{1,0:T(8,128)(2,1)}, bf16[320,1024]{1,0:T(8,128)(2,1)S(1)}, u32[]{:S(2)}, u32[]{:S(2)}) collective-permute-start(bf16[320,1024]{1,0:T(8,128)(2,1)} %pack.1), channel_id=1, source_target_pairs={{0,1},{1,2},{2,3},{3,0},{4,5},{5,6},{6,7},{7,4},{8,9},{9,10},{10,1... | collective-permute-start | bytes 1966088 | tf_op jit(solution)/shard_map/ppermute | solution.py:391
  4.8 1.4 %collective-permute-start.1 = (bf16[320,1024]{1,0:T(8,128)(2,1)}, bf16[320,1024]{1,0:T(8,128)(2,1)S(1)}, u32[]{:S(2)}, u32[]{:S(2)}) collective-permute-start(bf16[320,1024]{1,0:T(8,128)(2,1)} %pack.1), channel_id=1, source_target_pairs={{0,3},{1,0},{2,1},{3,2},{4,7},{5,4},{6,5},{7,6},{8,11},{9,8},{10,9... | collective-permute-start | bytes 1966088 | tf_op jit(solution)/shard_map/ppermute | solution.py:391
  6.2 2.6 %rows_out.1 = bf16[1024,256]{1,0:T(8,128)(2,1)} custom-call(s32[1,64]{1,0:T(1,128)} %blocks_ref.3, s32[1,64]{1,0:T(1,128)} %owners_ref.3, bf16[128,1024]{1,0:T(8,128)(2,1)} %bitcast.13), custom_call_target="tpu_custom_call" | custom-call | tf_op jit(solution)/shard_map/rows_out/pallas_call | solution.py:31
  8.8 13.0 %all-to-all-start = ((bf16[64,16,256]{2,1,0:T(8,128)(2,1)}), bf16[64,16,256]{2,1,0:T(8,128)(2,1)S(1)}, u32[]{:S(2)}, u32[]{:S(2)}) async-start(bf16[64,16,256]{2,1,0:T(8,128)(2,1)} %bitcast.12), calls=%async_computation | async-start | bytes 1048576 | tf_op jit(solution)/shard_map/all_to_all | solution.py:426
  22.8 2.8 %collective-permute-start.3 = (bf16[160,1024]{1,0:T(8,128)(2,1)S(1)}, bf16[160,1024]{1,0:T(8,128)(2,1)}, u32[]{:S(2)}, u32[]{:S(2)}) collective-permute-start(bf16[160,1024]{1,0:T(8,128)(2,1)S(1)} %slice.9), channel_id=1, source_target_pairs={{0,3},{1,0},{2,1},{3,2},{4,7},{5,4},{6,5},{7,6},{8,11},{9,8},{10,9... | collective-permute-start | bytes 983048 | tf_op jit(solution)/shard_map/ppermute | solution.py:391
  25.6 6.5 %collective-permute-done.2.a3 = bf16[160,1024]{1,0:T(8,128)(2,1)} collective-permute-done((bf16[160,1024]{1,0:T(8,128)(2,1)S(1)}, bf16[160,1024]{1,0:T(8,128)(2,1)}, u32[]{:S(2)}, u32[]{:S(2)}) %collective-permute-start.2) | collective-permute-done | bytes 327712 | tf_op jit(solution)/shard_map/ppermute | solution.py:391
  32.1 1.3 %collective-permute-start.6 = (bf16[160,1024]{1,0:T(8,128)(2,1)}, bf16[160,1024]{1,0:T(8,128)(2,1)}, u32[]{:S(2)}, u32[]{:S(2)}) collective-permute-start(bf16[160,1024]{1,0:T(8,128)(2,1)} %collective-permute-done.2.a3), channel_id=1, source_target_pairs={{0,4},{4,0},{1,5},{5,1},{2,6},{6,2},{3,7},{7,3},{8,12},{12,8},{9,1... | collective-permute-start | bytes 983048 | tf_op jit(solution)/shard_map/ppermute | solution.py:391
  33.5 6.1 %all-to-all-done = bf16[64,16,256]{2,1,0:T(8,128)(2,1)S(1)} async-done(((bf16[64,16,256]{2,1,0:T(8,128)(2,1)}), bf16[64,16,256]{2,1,0:T(8,128)(2,1)S(1)}, u32[]{:S(2)}, u32[]{:S(2)}) %all-to-all-start) | async-done | bytes 524320 | tf_op jit(solution)/shard_map/all_to_all | solution.py:426
  40.6 7.2 %layer.1 = (bf16[4,256,512]{2,1,0:T(8,128)(2,1)S(1)}, f32[256,128]{1,0:T(8,128)S(1)}, bf16[256,1024]{1,0:T(8,128)(2,1)}, bf16[256,1024]{1,0:T(8,128)(2,1)S(1)}, bf16[256,1024]{1,0:T(8,128)(2,1)S(1)}) custom-call(s32[1,64]{1,0:T(1,128)S(1)} %copy-done.4, s32[1,64]{1,0:T(1,128)S(1)} %copy-done.5, bf16[1024,256]{1,0:T(8,128)(2,1)S(1)} %bitcast.11, ...), custom_call_target="tpu_custom_call" | custom-call | tf_op jit(solution)/shard_map/layer/pallas_call | solution.py:31
  48.5 3.8 %rest.1 = (bf16[32,16,256]{2,1,0:T(8,128)(2,1)S(1)}, bf16[32,16,256]{2,1,0:T(8,128)(2,1)S(1)}) custom-call(bf16[4,256,512]{2,1,0:T(8,128)(2,1)S(1)} %get-tuple-element.31.shared, f32[256,128]{1,0:T(8,128)S(1)} %get-tuple-element.32.rstd, bf16[256,1024]{1,0:T(8,128)(2,1)S(1)} %bitcast.8, bf16[256,1024]{1,0:T(8,128)(2,1)S(1)} %get-tuple-element.33.kept, ...), custom_call_target="tpu_custom_call" | custom-call | tf_op jit(solution)/shard_map/rest/pallas_call | solution.py:31
  52.8 2.7 %sum_pair.1 = (bf16[2,2,80,1024]{3,2,1,0:T(8,128)(2,1)}, bf16[2,2,80,1024]{3,2,1,0:T(8,128)(2,1)}, bf16[8,80,1024]{2,1,0:T(8,128)(2,1)S(1)}) custom-call(bf16[4,256,512]{2,1,0:T(8,128)(2,1)S(1)} %get-tuple-element.31.shared, bf16[4,256,512]{2,1,0:T(8,128)(2,1)S(1)} %collective-permute-done.9.other, bf16[256,1024]{1,0:T(8,128)(2,1)S(1)} %get-tuple-element.33.kept, ...), custom_call_target="tpu_custom_call" | custom-call | tf_op jit(solution)/shard_map/sum_pair/pallas_call | solution.py:31
  55.5 1.2 collective-permute-start.11
  56.7 1.5 %collective-permute-start.12 = (bf16[2,2,80,1024]{3,2,1,0:T(8,128)(2,1)}, bf16[2,2,80,1024]{3,2,1,0:T(8,128)(2,1)S(1)}, u32[]{:S(2)}, u32[]{:S(2)}) collective-permute-start(bf16[2,2,80,1024]{3,2,1,0:T(8,128)(2,1)} %get-tuple-element.41), channel_id=1, source_target_pairs={{0,3},{1,0},{2,1},{3,2},{4,28},{5,29},{6,30},{7,31},{8,11},{9,8},{... | collective-permute-start | bytes 1966088 | tf_op jit(solution)/shard_map/ppermute | solution.py:404
  59.0 5.4 %all-to-all-start.1 = ((bf16[32,32,256]{2,1,0:T(8,128)(2,1)}), bf16[32,32,256]{2,1,0:T(8,128)(2,1)S(1)}, u32[]{:S(2)}, u32[]{:S(2)}) async-start(bf16[32,32,256]{2,1,0:T(8,128)(2,1)} %copy-done.2), calls=%async_computation.1 | async-start | bytes 1048576 | tf_op jit(solution)/shard_map/all_to_all | solution.py:481
  64.4 2.2 %collective-permute-done.11.ahead = bf16[2,2,80,1024]{3,2,1,0:T(8,128)(2,1)S(1)} collective-permute-done((bf16[2,2,80,1024]{3,2,1,0:T(8,128)(2,1)}, bf16[2,2,80,1024]{3,2,1,0:T(8,128)(2,1)S(1)}, u32[]{:S(2)}, u32[]{:S(2)}) %collective-permute-start.11) | collective-permute-done | bytes 655392 | tf_op jit(solution)/shard_map/ppermute | solution.py:404
  66.8 1.3 %collective-permute-start.13 = (bf16[2,80,1024]{2,1,0:T(8,128)(2,1)S(1)}, bf16[2,80,1024]{2,1,0:T(8,128)(2,1)S(1)}, u32[]{:S(2)}, u32[]{:S(2)}) collective-permute-start(bf16[2,80,1024]{2,1,0:T(8,128)(2,1)S(1)} %get-tuple-element.42), channel_id=1, source_target_pairs={{0,1},{1,2},{2,3},{3,0},{4,12},{5,13},{6,14},{7,15},{8,9},{9,10},{... | collective-permute-start | bytes 983048 | tf_op jit(solution)/shard_map/ppermute | solution.py:404
  68.0 1.6 %collective-permute-start.14 = (bf16[2,80,1024]{2,1,0:T(8,128)(2,1)S(1)}, bf16[2,80,1024]{2,1,0:T(8,128)(2,1)S(1)}, u32[]{:S(2)}, u32[]{:S(2)}) collective-permute-start(bf16[2,80,1024]{2,1,0:T(8,128)(2,1)S(1)} %get-tuple-element.43), channel_id=1, source_target_pairs={{0,3},{1,0},{2,1},{3,2},{4,28},{5,29},{6,30},{7,31},{8,11},{9,8},{... | collective-permute-start | bytes 983048 | tf_op jit(solution)/shard_map/ppermute | solution.py:404
  69.6 8.1 %collective-permute-done.13.forth = bf16[2,80,1024]{2,1,0:T(8,128)(2,1)S(1)} collective-permute-done((bf16[2,80,1024]{2,1,0:T(8,128)(2,1)S(1)}, bf16[2,80,1024]{2,1,0:T(8,128)(2,1)S(1)}, u32[]{:S(2)}, u32[]{:S(2)}) %collective-permute-start.13) | collective-permute-done | bytes 327712 | tf_op jit(solution)/shard_map/ppermute | solution.py:404
  78.6 2.5 %collective-permute-start.16 = (bf16[80,1024]{1,0:T(8,128)(2,1)}, bf16[80,1024]{1,0:T(8,128)(2,1)S(1)}, u32[]{:S(2)}, u32[]{:S(2)}) collective-permute-start(bf16[80,1024]{1,0:T(8,128)(2,1)} %get-tuple-element.48), channel_id=1, source_target_pairs={{0,16},{1,17},{2,18},{3,19},{4,6},{5,7},{6,4},{7,5},{8,24},{9,25},... | collective-permute-start | bytes 491528 | tf_op jit(solution)/shard_map/ppermute | solution.py:404
  81.1 1.2 collective-permute-start.17
  82.4 1.5 %rows_back.1 = bf16[128,1024]{1,0:T(8,128)(2,1)} custom-call(s32[1,64]{1,0:T(1,128)S(1)} %copy-done.4, s32[1,64]{1,0:T(1,128)S(1)} %copy-done.5, bf16[1024,256]{1,0:T(8,128)(2,1)S(1)} %bitcast.10), custom_call_target="tpu_custom_call" | custom-call | tf_op jit(solution)/shard_map/rows_back/pallas_call | solution.py:31
  83.9 2.1 %collective-permute-done.15.a1 = bf16[80,1024]{1,0:T(8,128)(2,1)S(1)} collective-permute-done((bf16[80,1024]{1,0:T(8,128)(2,1)}, bf16[80,1024]{1,0:T(8,128)(2,1)S(1)}, u32[]{:S(2)}, u32[]{:S(2)}) %collective-permute-start.15) | collective-permute-done | bytes 163872 | tf_op jit(solution)/shard_map/ppermute | solution.py:404
  87.8 1.5 %collective-permute-start.19 = (bf16[80,256]{1,0:T(8,128)(2,1)S(1)}, bf16[80,256]{1,0:T(8,128)(2,1)S(1)}, u32[]{:S(2)}, u32[]{:S(2)}) collective-permute-start(bf16[80,256]{1,0:T(8,128)(2,1)S(1)} %get-tuple-element.52), channel_id=1, source_target_pairs={{0,64},{32,96},{64,0},{96,32},{1,65},{33,97},{65,1},{97,33},{2,66}... | collective-permute-start | bytes 122888 | tf_op jit(solution)/shard_map/ppermute | solution.py:391
  89.3 2.0 %collective-permute-start.20 = (bf16[80,256]{1,0:T(8,128)(2,1)S(1)}, bf16[80,256]{1,0:T(8,128)(2,1)S(1)}, u32[]{:S(2)}, u32[]{:S(2)}) collective-permute-start(bf16[80,256]{1,0:T(8,128)(2,1)S(1)} %get-tuple-element.53), channel_id=1, source_target_pairs={{0,96},{32,0},{64,32},{96,64},{1,97},{33,1},{65,33},{97,65},{2,98}... | collective-permute-start | bytes 122888 | tf_op jit(solution)/shard_map/ppermute | solution.py:391
  91.4 1.8 %collective-permute-done.19.a2 = bf16[80,256]{1,0:T(8,128)(2,1)S(1)} collective-permute-done((bf16[80,256]{1,0:T(8,128)(2,1)S(1)}, bf16[80,256]{1,0:T(8,128)(2,1)S(1)}, u32[]{:S(2)}, u32[]{:S(2)}) %collective-permute-start.19) | collective-permute-done | bytes 40992 | tf_op jit(solution)/shard_map/ppermute | solution.py:391
  93.3 16.0 %all_to_all.15.parts = bf16[8,80,256]{2,1,0:T(8,128)(2,1)S(1)} all-to-all(bf16[8,80,256]{2,1,0:T(8,128)(2,1)S(1)} %add_near.1), channel_id=1, replica_groups=mesh['zh'=2,'zl'=4,'y'=4,'c'=2,'x'=4] {'zh','zl'}, dimensions={0} | all-to-all | bytes 655360 | tf_op jit(solution)/shard_map/all_to_all | solution.py:505
  110.4 2.3 %collective-permute-start.22 = (bf16[80,1024]{1,0:T(8,128)(2,1)S(1)}, bf16[80,1024]{1,0:T(8,128)(2,1)S(1)}, u32[]{:S(2)}, u32[]{:S(2)}) collective-permute-start(bf16[80,1024]{1,0:T(8,128)(2,1)S(1)} %join.1.o0), channel_id=1, source_target_pairs={{0,16},{8,24},{16,0},{24,8},{1,17},{9,25},{17,1},{25,9},{2,18},{10... | collective-permute-start | bytes 491528 | tf_op jit(solution)/shard_map/ppermute | solution.py:391
  113.5 4.4 %collective-permute-start.24 = (bf16[80,1024]{1,0:T(8,128)(2,1)S(1)}, bf16[80,1024]{1,0:T(8,128)(2,1)S(1)}, u32[]{:S(2)}, u32[]{:S(2)}) collective-permute-start(bf16[80,1024]{1,0:T(8,128)(2,1)S(1)} %join.1.o0), channel_id=1, source_target_pairs={{0,4},{4,0},{1,5},{5,1},{2,6},{6,2},{3,7},{7,3},{8,12},{12,8},{9,1... | collective-permute-start | bytes 491528 | tf_op jit(solution)/shard_map/ppermute | solution.py:391
  117.9 1.7 %collective-permute-start.25 = (bf16[80,1024]{1,0:T(8,128)(2,1)S(1)}, bf16[80,1024]{1,0:T(8,128)(2,1)S(1)}, u32[]{:S(2)}, u32[]{:S(2)}) collective-permute-start(bf16[80,1024]{1,0:T(8,128)(2,1)S(1)} %collective-permute-done.21.o1), channel_id=1, source_target_pairs={{0,4},{4,0},{1,5},{5,1},{2,6},{6,2},{3,7},{7,3},{8,12},{12,8},{9,1... | collective-permute-start | bytes 491528 | tf_op jit(solution)/shard_map/ppermute | solution.py:391
  119.6 2.3 %collective-permute-start.26 = (bf16[80,1024]{1,0:T(8,128)(2,1)S(1)}, bf16[80,1024]{1,0:T(8,128)(2,1)S(1)}, u32[]{:S(2)}, u32[]{:S(2)}) collective-permute-start(bf16[80,1024]{1,0:T(8,128)(2,1)S(1)} %collective-permute-done.22.o2), channel_id=1, source_target_pairs={{0,4},{4,0},{1,5},{5,1},{2,6},{6,2},{3,7},{7,3},{8,12},{12,8},{9,1... | collective-permute-start | bytes 491528 | tf_op jit(solution)/shard_map/ppermute | solution.py:391
  123.3 1.8 %place.1 = (f32[256,2048]{1,0:T(8,128)}, f32[128,1024]{1,0:T(8,128)}) custom-call(bf16[80,1024]{1,0:T(8,128)(2,1)S(1)} %join.1.o0, bf16[80,1024]{1,0:T(8,128)(2,1)S(1)} %collective-permute-done.21.o1, bf16[80,1024]{1,0:T(8,128)(2,1)S(1)} %collective-permute-done.22.o2, bf16[80,1024]{1,0:T(8,128)(2,1)S(1)} %collective-permute-done.23.o3, ...), custom_call_target="tpu_custom_call" | custom-call | tf_op jit(solution)/shard_map/place/pallas_call | solution.py:31
  (56 shorter events, 10.3 us)
Async XLA Ops:
  0.6 38.9 %copy-start = (bf16[256,2048]{1,0:T(8,128)(2,1)S(1)}, bf16[256,2048]{1,0:T(8,128)(2,1)}, u32[]{:S(2)}) copy-start(bf16[256,2048]{1,0:T(8,128)(2,1)} %w_in.5) | copy-start | bytes 3145732
  0.6 38.9 %copy-start.4 = (s32[1,64]{1,0:T(1,128)S(1)}, s32[1,64]{1,0:T(1,128)}, u32[]{:S(2)}) copy-start(s32[1,64]{1,0:T(1,128)} %blocks_ref.3) | copy-start | bytes 772
  2.7 19.1 %collective-permute-start = (bf16[320,1024]{1,0:T(8,128)(2,1)}, bf16[320,1024]{1,0:T(8,128)(2,1)S(1)}, u32[]{:S(2)}, u32[]{:S(2)}) collective-permute-start(bf16[320,1024]{1,0:T(8,128)(2,1)} %pack.1), channel_id=1, source_target_pairs={{0,1},{1,2},{2,3},{3,0},{4,5},{5,6},{6,7},{7,4},{8,9},{9,10},{10,1... | collective-permute-start | bytes 1966088 | tf_op jit(solution)/shard_map/ppermute | solution.py:391
  4.8 17.8 %collective-permute-start.1 = (bf16[320,1024]{1,0:T(8,128)(2,1)}, bf16[320,1024]{1,0:T(8,128)(2,1)S(1)}, u32[]{:S(2)}, u32[]{:S(2)}) collective-permute-start(bf16[320,1024]{1,0:T(8,128)(2,1)} %pack.1), channel_id=1, source_target_pairs={{0,3},{1,0},{2,1},{3,2},{4,7},{5,4},{6,5},{7,6},{8,11},{9,8},{10,9... | collective-permute-start | bytes 1966088 | tf_op jit(solution)/shard_map/ppermute | solution.py:391
  8.8 30.7 %all-to-all-start = ((bf16[64,16,256]{2,1,0:T(8,128)(2,1)}), bf16[64,16,256]{2,1,0:T(8,128)(2,1)S(1)}, u32[]{:S(2)}, u32[]{:S(2)}) async-start(bf16[64,16,256]{2,1,0:T(8,128)(2,1)} %bitcast.12), calls=%async_computation | async-start | bytes 1048576 | tf_op jit(solution)/shard_map/all_to_all | solution.py:426
  21.9 10.2 %collective-permute-start.2 = (bf16[160,1024]{1,0:T(8,128)(2,1)S(1)}, bf16[160,1024]{1,0:T(8,128)(2,1)}, u32[]{:S(2)}, u32[]{:S(2)}) collective-permute-start(bf16[160,1024]{1,0:T(8,128)(2,1)S(1)} %slice.8), channel_id=1, source_target_pairs={{0,1},{1,2},{2,3},{3,0},{4,5},{5,6},{6,7},{7,4},{8,9},{9,10},{10,1... | collective-permute-start | bytes 983048 | tf_op jit(solution)/shard_map/ppermute | solution.py:391
  22.0 17.6 %collective-permute-start.4 = (bf16[320,1024]{1,0:T(8,128)(2,1)S(1)}, bf16[320,1024]{1,0:T(8,128)(2,1)}, u32[]{:S(2)}, u32[]{:S(2)}) collective-permute-start(bf16[320,1024]{1,0:T(8,128)(2,1)S(1)} %collective-permute-done.a1), channel_id=1, source_target_pairs={{0,4},{4,0},{1,5},{5,1},{2,6},{6,2},{3,7},{7,3},{8,12},{12,8},{9,1... | collective-permute-start | bytes 1966088 | tf_op jit(solution)/shard_map/ppermute | solution.py:391
  22.7 16.8 %collective-permute-start.5 = (bf16[320,1024]{1,0:T(8,128)(2,1)S(1)}, bf16[320,1024]{1,0:T(8,128)(2,1)}, u32[]{:S(2)}, u32[]{:S(2)}) collective-permute-start(bf16[320,1024]{1,0:T(8,128)(2,1)S(1)} %collective-permute-done.1.a2), channel_id=1, source_target_pairs={{0,4},{4,0},{1,5},{5,1},{2,6},{6,2},{3,7},{7,3},{8,12},{12,8},{9,1... | collective-permute-start | bytes 1966088 | tf_op jit(solution)/shard_map/ppermute | solution.py:391
  22.8 10.6 %collective-permute-start.3 = (bf16[160,1024]{1,0:T(8,128)(2,1)S(1)}, bf16[160,1024]{1,0:T(8,128)(2,1)}, u32[]{:S(2)}, u32[]{:S(2)}) collective-permute-start(bf16[160,1024]{1,0:T(8,128)(2,1)S(1)} %slice.9), channel_id=1, source_target_pairs={{0,3},{1,0},{2,1},{3,2},{4,7},{5,4},{6,5},{7,6},{8,11},{9,8},{10,9... | collective-permute-start | bytes 983048 | tf_op jit(solution)/shard_map/ppermute | solution.py:391
  32.1 7.5 %collective-permute-start.6 = (bf16[160,1024]{1,0:T(8,128)(2,1)}, bf16[160,1024]{1,0:T(8,128)(2,1)}, u32[]{:S(2)}, u32[]{:S(2)}) collective-permute-start(bf16[160,1024]{1,0:T(8,128)(2,1)} %collective-permute-done.2.a3), channel_id=1, source_target_pairs={{0,4},{4,0},{1,5},{5,1},{2,6},{6,2},{3,7},{7,3},{8,12},{12,8},{9,1... | collective-permute-start | bytes 983048 | tf_op jit(solution)/shard_map/ppermute | solution.py:391
  33.4 6.2 %collective-permute-start.7 = (bf16[160,1024]{1,0:T(8,128)(2,1)}, bf16[160,1024]{1,0:T(8,128)(2,1)}, u32[]{:S(2)}, u32[]{:S(2)}) collective-permute-start(bf16[160,1024]{1,0:T(8,128)(2,1)} %collective-permute-done.3.a4), channel_id=1, source_target_pairs={{0,4},{4,0},{1,5},{5,1},{2,6},{6,2},{3,7},{7,3},{8,12},{12,8},{9,1... | collective-permute-start | bytes 983048 | tf_op jit(solution)/shard_map/ppermute | solution.py:391
  47.8 5.0 %collective-permute-start.9 = (bf16[4,256,512]{2,1,0:T(8,128)(2,1)S(1)}, bf16[4,256,512]{2,1,0:T(8,128)(2,1)S(1)}, u32[]{:S(2)}, u32[]{:S(2)}) collective-permute-start(bf16[4,256,512]{2,1,0:T(8,128)(2,1)S(1)} %get-tuple-element.31.shared), channel_id=1, source_target_pairs={{0,4},{4,0},{1,5},{5,1},{2,6},{6,2},{3,7},{7,3},{8,12},{12,8},{9,1... | collective-permute-start | bytes 3145736 | tf_op jit(solution)/shard_map/ppermute | solution.py:391
  48.4 4.4 %collective-permute-start.10 = (bf16[256,1024]{1,0:T(8,128)(2,1)S(1)}, bf16[256,1024]{1,0:T(8,128)(2,1)S(1)}, u32[]{:S(2)}, u32[]{:S(2)}) collective-permute-start(bf16[256,1024]{1,0:T(8,128)(2,1)S(1)} %get-tuple-element.34.sent), channel_id=1, source_target_pairs={{0,4},{4,0},{1,5},{5,1},{2,6},{6,2},{3,7},{7,3},{8,12},{12,8},{9,1... | collective-permute-start | bytes 1572872 | tf_op jit(solution)/shard_map/ppermute | solution.py:391
  52.4 5.8 %collective-permute-start.8 = (bf16[32,16,256]{2,1,0:T(8,128)(2,1)S(1)}, bf16[32,16,256]{2,1,0:T(8,128)(2,1)S(1)}, u32[]{:S(2)}, u32[]{:S(2)}) collective-permute-start(bf16[32,16,256]{2,1,0:T(8,128)(2,1)S(1)} %get-tuple-element.36), channel_id=1, source_target_pairs={{0,4},{4,0},{1,5},{5,1},{2,6},{6,2},{3,7},{7,3},{8,12},{12,8},{9,1... | collective-permute-start | bytes 786440 | tf_op jit(solution)/shard_map/ppermute | solution.py:391
  55.5 11.2 %collective-permute-start.11 = (bf16[2,2,80,1024]{3,2,1,0:T(8,128)(2,1)}, bf16[2,2,80,1024]{3,2,1,0:T(8,128)(2,1)S(1)}, u32[]{:S(2)}, u32[]{:S(2)}) collective-permute-start(bf16[2,2,80,1024]{3,2,1,0:T(8,128)(2,1)} %get-tuple-element.40), channel_id=1, source_target_pairs={{0,1},{1,2},{2,3},{3,0},{4,12},{5,13},{6,14},{7,15},{8,9},{9,10},{... | collective-permute-start | bytes 1966088 | tf_op jit(solution)/shard_map/ppermute | solution.py:404
  56.7 10.0 %collective-permute-start.12 = (bf16[2,2,80,1024]{3,2,1,0:T(8,128)(2,1)}, bf16[2,2,80,1024]{3,2,1,0:T(8,128)(2,1)S(1)}, u32[]{:S(2)}, u32[]{:S(2)}) collective-permute-start(bf16[2,2,80,1024]{3,2,1,0:T(8,128)(2,1)} %get-tuple-element.41), channel_id=1, source_target_pairs={{0,3},{1,0},{2,1},{3,2},{4,28},{5,29},{6,30},{7,31},{8,11},{9,8},{... | collective-permute-start | bytes 1966088 | tf_op jit(solution)/shard_map/ppermute | solution.py:404
  59.0 23.4 %all-to-all-start.1 = ((bf16[32,32,256]{2,1,0:T(8,128)(2,1)}), bf16[32,32,256]{2,1,0:T(8,128)(2,1)S(1)}, u32[]{:S(2)}, u32[]{:S(2)}) async-start(bf16[32,32,256]{2,1,0:T(8,128)(2,1)} %copy-done.2), calls=%async_computation.1 | async-start | bytes 1048576 | tf_op jit(solution)/shard_map/all_to_all | solution.py:481
  66.8 10.9 %collective-permute-start.13 = (bf16[2,80,1024]{2,1,0:T(8,128)(2,1)S(1)}, bf16[2,80,1024]{2,1,0:T(8,128)(2,1)S(1)}, u32[]{:S(2)}, u32[]{:S(2)}) collective-permute-start(bf16[2,80,1024]{2,1,0:T(8,128)(2,1)S(1)} %get-tuple-element.42), channel_id=1, source_target_pairs={{0,1},{1,2},{2,3},{3,0},{4,12},{5,13},{6,14},{7,15},{8,9},{9,10},{... | collective-permute-start | bytes 983048 | tf_op jit(solution)/shard_map/ppermute | solution.py:404
  68.0 9.7 %collective-permute-start.14 = (bf16[2,80,1024]{2,1,0:T(8,128)(2,1)S(1)}, bf16[2,80,1024]{2,1,0:T(8,128)(2,1)S(1)}, u32[]{:S(2)}, u32[]{:S(2)}) collective-permute-start(bf16[2,80,1024]{2,1,0:T(8,128)(2,1)S(1)} %get-tuple-element.43), channel_id=1, source_target_pairs={{0,3},{1,0},{2,1},{3,2},{4,28},{5,29},{6,30},{7,31},{8,11},{9,8},{... | collective-permute-start | bytes 983048 | tf_op jit(solution)/shard_map/ppermute | solution.py:404
  78.6 7.4 %collective-permute-start.15 = (bf16[80,1024]{1,0:T(8,128)(2,1)}, bf16[80,1024]{1,0:T(8,128)(2,1)S(1)}, u32[]{:S(2)}, u32[]{:S(2)}) collective-permute-start(bf16[80,1024]{1,0:T(8,128)(2,1)} %get-tuple-element.44), channel_id=1, source_target_pairs={{0,8},{1,9},{2,10},{3,11},{4,5},{5,6},{6,7},{7,4},{8,16},{9,17},{1... | collective-permute-start | bytes 491528 | tf_op jit(solution)/shard_map/ppermute | solution.py:404
  78.6 7.4 %collective-permute-start.16 = (bf16[80,1024]{1,0:T(8,128)(2,1)}, bf16[80,1024]{1,0:T(8,128)(2,1)S(1)}, u32[]{:S(2)}, u32[]{:S(2)}) collective-permute-start(bf16[80,1024]{1,0:T(8,128)(2,1)} %get-tuple-element.48), channel_id=1, source_target_pairs={{0,16},{1,17},{2,18},{3,19},{4,6},{5,7},{6,4},{7,5},{8,24},{9,25},... | collective-permute-start | bytes 491528 | tf_op jit(solution)/shard_map/ppermute | solution.py:404
  81.1 5.4 %collective-permute-start.17 = (bf16[80,1024]{1,0:T(8,128)(2,1)}, bf16[80,1024]{1,0:T(8,128)(2,1)S(1)}, u32[]{:S(2)}, u32[]{:S(2)}) collective-permute-start(bf16[80,1024]{1,0:T(8,128)(2,1)} %get-tuple-element.49), channel_id=1, source_target_pairs={{0,24},{1,25},{2,26},{3,27},{4,7},{5,4},{6,5},{7,6},{8,0},{9,1},{1... | collective-permute-start | bytes 491528 | tf_op jit(solution)/shard_map/ppermute | solution.py:404
  86.7 4.8 %collective-permute-start.18 = (bf16[80,256]{1,0:T(8,128)(2,1)S(1)}, bf16[80,256]{1,0:T(8,128)(2,1)S(1)}, u32[]{:S(2)}, u32[]{:S(2)}) collective-permute-start(bf16[80,256]{1,0:T(8,128)(2,1)S(1)} %get-tuple-element.51), channel_id=1, source_target_pairs={{0,32},{32,64},{64,96},{96,0},{1,33},{33,65},{65,97},{97,1},{2,34}... | collective-permute-start | bytes 122888 | tf_op jit(solution)/shard_map/ppermute | solution.py:391
  87.8 5.4 %collective-permute-start.19 = (bf16[80,256]{1,0:T(8,128)(2,1)S(1)}, bf16[80,256]{1,0:T(8,128)(2,1)S(1)}, u32[]{:S(2)}, u32[]{:S(2)}) collective-permute-start(bf16[80,256]{1,0:T(8,128)(2,1)S(1)} %get-tuple-element.52), channel_id=1, source_target_pairs={{0,64},{32,96},{64,0},{96,32},{1,65},{33,97},{65,1},{97,33},{2,66}... | collective-permute-start | bytes 122888 | tf_op jit(solution)/shard_map/ppermute | solution.py:391
  89.3 3.9 %collective-permute-start.20 = (bf16[80,256]{1,0:T(8,128)(2,1)S(1)}, bf16[80,256]{1,0:T(8,128)(2,1)S(1)}, u32[]{:S(2)}, u32[]{:S(2)}) collective-permute-start(bf16[80,256]{1,0:T(8,128)(2,1)S(1)} %get-tuple-element.53), channel_id=1, source_target_pairs={{0,96},{32,0},{64,32},{96,64},{1,97},{33,1},{65,33},{97,65},{2,98}... | collective-permute-start | bytes 122888 | tf_op jit(solution)/shard_map/ppermute | solution.py:391
  109.3 8.6 %collective-permute-start.21 = (bf16[80,1024]{1,0:T(8,128)(2,1)S(1)}, bf16[80,1024]{1,0:T(8,128)(2,1)S(1)}, u32[]{:S(2)}, u32[]{:S(2)}) collective-permute-start(bf16[80,1024]{1,0:T(8,128)(2,1)S(1)} %join.1.o0), channel_id=1, source_target_pairs={{0,8},{8,16},{16,24},{24,0},{1,9},{9,17},{17,25},{25,1},{2,10},{10... | collective-permute-start | bytes 491528 | tf_op jit(solution)/shard_map/ppermute | solution.py:391
  110.4 9.2 %collective-permute-start.22 = (bf16[80,1024]{1,0:T(8,128)(2,1)S(1)}, bf16[80,1024]{1,0:T(8,128)(2,1)S(1)}, u32[]{:S(2)}, u32[]{:S(2)}) collective-permute-start(bf16[80,1024]{1,0:T(8,128)(2,1)S(1)} %join.1.o0), channel_id=1, source_target_pairs={{0,16},{8,24},{16,0},{24,8},{1,17},{9,25},{17,1},{25,9},{2,18},{10... | collective-permute-start | bytes 491528 | tf_op jit(solution)/shard_map/ppermute | solution.py:391
  112.7 9.2 %collective-permute-start.23 = (bf16[80,1024]{1,0:T(8,128)(2,1)S(1)}, bf16[80,1024]{1,0:T(8,128)(2,1)S(1)}, u32[]{:S(2)}, u32[]{:S(2)}) collective-permute-start(bf16[80,1024]{1,0:T(8,128)(2,1)S(1)} %join.1.o0), channel_id=1, source_target_pairs={{0,24},{8,0},{16,8},{24,16},{1,25},{9,1},{17,9},{25,17},{2,26},{10... | collective-permute-start | bytes 491528 | tf_op jit(solution)/shard_map/ppermute | solution.py:391
  113.5 8.7 %collective-permute-start.24 = (bf16[80,1024]{1,0:T(8,128)(2,1)S(1)}, bf16[80,1024]{1,0:T(8,128)(2,1)S(1)}, u32[]{:S(2)}, u32[]{:S(2)}) collective-permute-start(bf16[80,1024]{1,0:T(8,128)(2,1)S(1)} %join.1.o0), channel_id=1, source_target_pairs={{0,4},{4,0},{1,5},{5,1},{2,6},{6,2},{3,7},{7,3},{8,12},{12,8},{9,1... | collective-permute-start | bytes 491528 | tf_op jit(solution)/shard_map/ppermute | solution.py:391
  117.9 4.3 %collective-permute-start.25 = (bf16[80,1024]{1,0:T(8,128)(2,1)S(1)}, bf16[80,1024]{1,0:T(8,128)(2,1)S(1)}, u32[]{:S(2)}, u32[]{:S(2)}) collective-permute-start(bf16[80,1024]{1,0:T(8,128)(2,1)S(1)} %collective-permute-done.21.o1), channel_id=1, source_target_pairs={{0,4},{4,0},{1,5},{5,1},{2,6},{6,2},{3,7},{7,3},{8,12},{12,8},{9,1... | collective-permute-start | bytes 491528 | tf_op jit(solution)/shard_map/ppermute | solution.py:391
  119.6 3.3 %collective-permute-start.26 = (bf16[80,1024]{1,0:T(8,128)(2,1)S(1)}, bf16[80,1024]{1,0:T(8,128)(2,1)S(1)}, u32[]{:S(2)}, u32[]{:S(2)}) collective-permute-start(bf16[80,1024]{1,0:T(8,128)(2,1)S(1)} %collective-permute-done.22.o2), channel_id=1, source_target_pairs={{0,4},{4,0},{1,5},{5,1},{2,6},{6,2},{3,7},{7,3},{8,12},{12,8},{9,1... | collective-permute-start | bytes 491528 | tf_op jit(solution)/shard_map/ppermute | solution.py:391
  121.9 1.4 %collective-permute-start.27 = (bf16[80,1024]{1,0:T(8,128)(2,1)S(1)}, bf16[80,1024]{1,0:T(8,128)(2,1)S(1)}, u32[]{:S(2)}, u32[]{:S(2)}) collective-permute-start(bf16[80,1024]{1,0:T(8,128)(2,1)S(1)} %collective-permute-done.23.o3), channel_id=1, source_target_pairs={{0,4},{4,0},{1,5},{5,1},{2,6},{6,2},{3,7},{7,3},{8,12},{12,8},{9,1... | collective-permute-start | bytes 491528 | tf_op jit(solution)/shard_map/ppermute | solution.py:391
  (4 other events, 79.6 us)

commit v7 on v6

--- a/solution.py
+++ b/solution.py
@@ -141,7 +141,7 @@
 def forward_body(
     blocks_ref, owners_ref, arrived, cot, w_in, w_out, a1, a2, a3, a4, b1, b2, b3, b4,
     shared, owned, rstd, act, dsilu, hat, att_rstd, weights, dscore, w_full,
-    wide, pre,
+    wide, pre, dmixed,
 ):
     x, y, c = lax.axis_index("x"), lax.axis_index("y"), lax.axis_index("c")
     me = ((lax.axis_index("zh") * 4 + lax.axis_index("zl")) * 4 + y) * 2 + c
@@ -186,6 +186,7 @@
             act[h, rows, :] = (v * sig).astype(BF16)
             dsilu[h, rows, :] = sig * (1.0 + v * (1.0 - sig))
 
+    dmixed[...] = dot(cot[...], w_full[...].reshape(512, 1024), NT).astype(BF16)
     activate(pl.ds(0, ROWS))
 
     n_row, o_row, n_col, o_col, _, before_col, before_row = histories(blocks_ref, owners_ref)
@@ -233,7 +234,6 @@
     w_out = w_full[...].reshape(512, 1024)
     mixed = jnp.concatenate([shared[h, :, 256:384] for h in range(4)], axis=1)
     out[...] = (dot(mixed, w_out) + owned[...].astype(F32)).astype(BF16)
-    dmixed[...] = dot(cot[...], w_out, NT).astype(BF16)
 
     def unmix_rows(rows):
         dm = dmixed[rows, :].astype(F32)
@@ -269,7 +269,7 @@
 ):
     forward_body(
         blocks_ref, owners_ref, arrived, cot, w_in, w_out, a1, a2, a3, a4, b1, b2, b3, b4,
-        shared, owned, rstd, act, dsilu, hat, att_rstd, weights, dscore, w_full, wide, pre,
+        shared, owned, rstd, act, dsilu, hat, att_rstd, weights, dscore, w_full, wide, pre, dmixed,
     )
     backward_body(
         shared, owned, cot, act, dsilu, hat, att_rstd, weights, dscore, w_full,

time: 126 us -> 125 us (level)
  no operation moved by 1% of the time
where the time goes in v7:
time: 125 us
  starting transfers between devices  54.9 us (44%)
  waiting for transfers between devices  28.6 us (23%)
  Pallas kernels  22.8 us (18%)
  blocking collectives  16 us (13%)
  local copies, waits for them, and re-layouts  1.8 us (1%)
    ppermute x21, starting transfers between devices, shift(): return lax.ppermute(a, axis, [(i, (i + s) % n) for i in range(n)])  27.3 us
    pallas_call x12, Pallas kernels, call(): pl.pallas_call(body, out_shape=[jax.ShapeDtypeStruct(s, d) for s, d in ou...  20.8 us
    all_to_all x1, blocking collectives, on_device(): parts = lax.all_to_all(summed, Z, split_axis=0, concat_axis=0, tiled=True)  16 us
    all_to_all x1, starting transfers between devices, on_device(): lax.all_to_all(outgoing.reshape(64, 16, 256), DP, split_axis=0, concat_ax...  13 us
    ppermute x7, waiting for transfers between devices, crossed(): return lax.ppermute(a, ('zh', 'zl', 'y', 'c', 'x'), pairs)  13 us
    ppermute x21, waiting for transfers between devices, shift(): return lax.ppermute(a, axis, [(i, (i + s) % n) for i in range(n)])  9.54 us
    ppermute x7, starting transfers between devices, crossed(): return lax.ppermute(a, ('zh', 'zl', 'y', 'c', 'x'), pairs)  9.3 us
    all_to_all x1, waiting for transfers between devices, on_device(): lax.all_to_all(outgoing.reshape(64, 16, 256), DP, split_axis=0, concat_ax...  6.05 us
  transfers between devices with their start and end apart: 30, of which 10 were waited for; matrix products, arithmetic and copies ran while one was open for 0% of the time, Pallas kernels for 9%

profile of v7, /device:TPU:1, one launch (start us, length us, event | category | flops | bytes accessed | tf_op | source)
XLA Modules:
  0.0 125.0 jit_solution(2402133782040047786)
XLA Ops:
  0.7 2.0 %pack.1 = bf16[320,1024]{1,0:T(8,128)(2,1)} custom-call(bf16[256,2048]{1,0:T(8,128)(2,1)} %w_in.5, bf16[128,1024]{1,0:T(8,128)(2,1)} %w_out.3), custom_call_target="tpu_custom_call" | custom-call | tf_op jit(solution)/shard_map/pack/pallas_call | solution.py:409
  2.7 2.1 %collective-permute-start = (bf16[320,1024]{1,0:T(8,128)(2,1)}, bf16[320,1024]{1,0:T(8,128)(2,1)S(1)}, u32[]{:S(2)}, u32[]{:S(2)}) collective-permute-start(bf16[320,1024]{1,0:T(8,128)(2,1)} %pack.1), channel_id=1, source_target_pairs={{0,1},{1,2},{2,3},{3,0},{4,5},{5,6},{6,7},{7,4},{8,9},{9,10},{10,1... | collective-permute-start | bytes 1966088 | tf_op jit(solution)/shard_map/ppermute | solution.py:391
  4.8 1.4 %collective-permute-start.1 = (bf16[320,1024]{1,0:T(8,128)(2,1)}, bf16[320,1024]{1,0:T(8,128)(2,1)S(1)}, u32[]{:S(2)}, u32[]{:S(2)}) collective-permute-start(bf16[320,1024]{1,0:T(8,128)(2,1)} %pack.1), channel_id=1, source_target_pairs={{0,3},{1,0},{2,1},{3,2},{4,7},{5,4},{6,5},{7,6},{8,11},{9,8},{10,9... | collective-permute-start | bytes 1966088 | tf_op jit(solution)/shard_map/ppermute | solution.py:391
  6.2 2.6 %rows_out.1 = bf16[1024,256]{1,0:T(8,128)(2,1)} custom-call(s32[1,64]{1,0:T(1,128)} %blocks_ref.3, s32[1,64]{1,0:T(1,128)} %owners_ref.3, bf16[128,1024]{1,0:T(8,128)(2,1)} %bitcast.13), custom_call_target="tpu_custom_call" | custom-call | tf_op jit(solution)/shard_map/rows_out/pallas_call | solution.py:31
  8.8 13.0 %all-to-all-start = ((bf16[64,16,256]{2,1,0:T(8,128)(2,1)}), bf16[64,16,256]{2,1,0:T(8,128)(2,1)S(1)}, u32[]{:S(2)}, u32[]{:S(2)}) async-start(bf16[64,16,256]{2,1,0:T(8,128)(2,1)} %bitcast.12), calls=%async_computation | async-start | bytes 1048576 | tf_op jit(solution)/shard_map/all_to_all | solution.py:426
  22.8 2.8 %collective-permute-start.3 = (bf16[160,1024]{1,0:T(8,128)(2,1)S(1)}, bf16[160,1024]{1,0:T(8,128)(2,1)}, u32[]{:S(2)}, u32[]{:S(2)}) collective-permute-start(bf16[160,1024]{1,0:T(8,128)(2,1)S(1)} %slice.9), channel_id=1, source_target_pairs={{0,3},{1,0},{2,1},{3,2},{4,7},{5,4},{6,5},{7,6},{8,11},{9,8},{10,9... | collective-permute-start | bytes 983048 | tf_op jit(solution)/shard_map/ppermute | solution.py:391
  25.6 6.5 %collective-permute-done.2.a3 = bf16[160,1024]{1,0:T(8,128)(2,1)} collective-permute-done((bf16[160,1024]{1,0:T(8,128)(2,1)S(1)}, bf16[160,1024]{1,0:T(8,128)(2,1)}, u32[]{:S(2)}, u32[]{:S(2)}) %collective-permute-start.2) | collective-permute-done | bytes 327712 | tf_op jit(solution)/shard_map/ppermute | solution.py:391
  32.1 1.3 %collective-permute-start.6 = (bf16[160,1024]{1,0:T(8,128)(2,1)}, bf16[160,1024]{1,0:T(8,128)(2,1)}, u32[]{:S(2)}, u32[]{:S(2)}) collective-permute-start(bf16[160,1024]{1,0:T(8,128)(2,1)} %collective-permute-done.2.a3), channel_id=1, source_target_pairs={{0,4},{4,0},{1,5},{5,1},{2,6},{6,2},{3,7},{7,3},{8,12},{12,8},{9,1... | collective-permute-start | bytes 983048 | tf_op jit(solution)/shard_map/ppermute | solution.py:391
  33.5 6.1 %all-to-all-done = bf16[64,16,256]{2,1,0:T(8,128)(2,1)S(1)} async-done(((bf16[64,16,256]{2,1,0:T(8,128)(2,1)}), bf16[64,16,256]{2,1,0:T(8,128)(2,1)S(1)}, u32[]{:S(2)}, u32[]{:S(2)}) %all-to-all-start) | async-done | bytes 524320 | tf_op jit(solution)/shard_map/all_to_all | solution.py:426
  40.6 7.1 %layer.1 = (bf16[4,256,512]{2,1,0:T(8,128)(2,1)S(1)}, f32[256,128]{1,0:T(8,128)S(1)}, bf16[256,1024]{1,0:T(8,128)(2,1)}, bf16[256,1024]{1,0:T(8,128)(2,1)S(1)}, bf16[256,1024]{1,0:T(8,128)(2,1)S(1)}) custom-call(s32[1,64]{1,0:T(1,128)S(1)} %copy-done.4, s32[1,64]{1,0:T(1,128)S(1)} %copy-done.5, bf16[1024,256]{1,0:T(8,128)(2,1)S(1)} %bitcast.11, ...), custom_call_target="tpu_custom_call" | custom-call | tf_op jit(solution)/shard_map/layer/pallas_call | solution.py:31
  48.4 3.8 %rest.1 = (bf16[32,16,256]{2,1,0:T(8,128)(2,1)S(1)}, bf16[32,16,256]{2,1,0:T(8,128)(2,1)S(1)}) custom-call(bf16[4,256,512]{2,1,0:T(8,128)(2,1)S(1)} %get-tuple-element.31.shared, f32[256,128]{1,0:T(8,128)S(1)} %get-tuple-element.32.rstd, bf16[256,1024]{1,0:T(8,128)(2,1)S(1)} %bitcast.8, bf16[256,1024]{1,0:T(8,128)(2,1)S(1)} %get-tuple-element.33.kept, ...), custom_call_target="tpu_custom_call" | custom-call | tf_op jit(solution)/shard_map/rest/pallas_call | solution.py:31
  52.7 2.7 %sum_pair.1 = (bf16[2,2,80,1024]{3,2,1,0:T(8,128)(2,1)}, bf16[2,2,80,1024]{3,2,1,0:T(8,128)(2,1)}, bf16[8,80,1024]{2,1,0:T(8,128)(2,1)S(1)}) custom-call(bf16[4,256,512]{2,1,0:T(8,128)(2,1)S(1)} %get-tuple-element.31.shared, bf16[4,256,512]{2,1,0:T(8,128)(2,1)S(1)} %collective-permute-done.9.other, bf16[256,1024]{1,0:T(8,128)(2,1)S(1)} %get-tuple-element.33.kept, ...), custom_call_target="tpu_custom_call" | custom-call | tf_op jit(solution)/shard_map/sum_pair/pallas_call | solution.py:31
  55.3 1.2 collective-permute-start.11
  56.5 1.5 %collective-permute-start.12 = (bf16[2,2,80,1024]{3,2,1,0:T(8,128)(2,1)}, bf16[2,2,80,1024]{3,2,1,0:T(8,128)(2,1)S(1)}, u32[]{:S(2)}, u32[]{:S(2)}) collective-permute-start(bf16[2,2,80,1024]{3,2,1,0:T(8,128)(2,1)} %get-tuple-element.41), channel_id=1, source_target_pairs={{0,3},{1,0},{2,1},{3,2},{4,28},{5,29},{6,30},{7,31},{8,11},{9,8},{... | collective-permute-start | bytes 1966088 | tf_op jit(solution)/shard_map/ppermute | solution.py:404
  58.8 5.4 %all-to-all-start.1 = ((bf16[32,32,256]{2,1,0:T(8,128)(2,1)}), bf16[32,32,256]{2,1,0:T(8,128)(2,1)S(1)}, u32[]{:S(2)}, u32[]{:S(2)}) async-start(bf16[32,32,256]{2,1,0:T(8,128)(2,1)} %copy-done.2), calls=%async_computation.1 | async-start | bytes 1048576 | tf_op jit(solution)/shard_map/all_to_all | solution.py:481
  64.2 2.2 %collective-permute-done.11.ahead = bf16[2,2,80,1024]{3,2,1,0:T(8,128)(2,1)S(1)} collective-permute-done((bf16[2,2,80,1024]{3,2,1,0:T(8,128)(2,1)}, bf16[2,2,80,1024]{3,2,1,0:T(8,128)(2,1)S(1)}, u32[]{:S(2)}, u32[]{:S(2)}) %collective-permute-start.11) | collective-permute-done | bytes 655392 | tf_op jit(solution)/shard_map/ppermute | solution.py:404
  66.6 1.3 %collective-permute-start.13 = (bf16[2,80,1024]{2,1,0:T(8,128)(2,1)S(1)}, bf16[2,80,1024]{2,1,0:T(8,128)(2,1)S(1)}, u32[]{:S(2)}, u32[]{:S(2)}) collective-permute-start(bf16[2,80,1024]{2,1,0:T(8,128)(2,1)S(1)} %get-tuple-element.42), channel_id=1, source_target_pairs={{0,1},{1,2},{2,3},{3,0},{4,12},{5,13},{6,14},{7,15},{8,9},{9,10},{... | collective-permute-start | bytes 983048 | tf_op jit(solution)/shard_map/ppermute | solution.py:404
  67.9 1.6 %collective-permute-start.14 = (bf16[2,80,1024]{2,1,0:T(8,128)(2,1)S(1)}, bf16[2,80,1024]{2,1,0:T(8,128)(2,1)S(1)}, u32[]{:S(2)}, u32[]{:S(2)}) collective-permute-start(bf16[2,80,1024]{2,1,0:T(8,128)(2,1)S(1)} %get-tuple-element.43), channel_id=1, source_target_pairs={{0,3},{1,0},{2,1},{3,2},{4,28},{5,29},{6,30},{7,31},{8,11},{9,8},{... | collective-permute-start | bytes 983048 | tf_op jit(solution)/shard_map/ppermute | solution.py:404
  69.5 8.1 %collective-permute-done.13.forth = bf16[2,80,1024]{2,1,0:T(8,128)(2,1)S(1)} collective-permute-done((bf16[2,80,1024]{2,1,0:T(8,128)(2,1)S(1)}, bf16[2,80,1024]{2,1,0:T(8,128)(2,1)S(1)}, u32[]{:S(2)}, u32[]{:S(2)}) %collective-permute-start.13) | collective-permute-done | bytes 327712 | tf_op jit(solution)/shard_map/ppermute | solution.py:404
  78.5 2.5 %collective-permute-start.16 = (bf16[80,1024]{1,0:T(8,128)(2,1)}, bf16[80,1024]{1,0:T(8,128)(2,1)S(1)}, u32[]{:S(2)}, u32[]{:S(2)}) collective-permute-start(bf16[80,1024]{1,0:T(8,128)(2,1)} %get-tuple-element.48), channel_id=1, source_target_pairs={{0,16},{1,17},{2,18},{3,19},{4,6},{5,7},{6,4},{7,5},{8,24},{9,25},... | collective-permute-start | bytes 491528 | tf_op jit(solution)/shard_map/ppermute | solution.py:404
  81.0 1.2 collective-permute-start.17
  82.3 1.5 %rows_back.1 = bf16[128,1024]{1,0:T(8,128)(2,1)} custom-call(s32[1,64]{1,0:T(1,128)S(1)} %copy-done.4, s32[1,64]{1,0:T(1,128)S(1)} %copy-done.5, bf16[1024,256]{1,0:T(8,128)(2,1)S(1)} %bitcast.10), custom_call_target="tpu_custom_call" | custom-call | tf_op jit(solution)/shard_map/rows_back/pallas_call | solution.py:31
  83.8 2.1 %collective-permute-done.15.a1 = bf16[80,1024]{1,0:T(8,128)(2,1)S(1)} collective-permute-done((bf16[80,1024]{1,0:T(8,128)(2,1)}, bf16[80,1024]{1,0:T(8,128)(2,1)S(1)}, u32[]{:S(2)}, u32[]{:S(2)}) %collective-permute-start.15) | collective-permute-done | bytes 163872 | tf_op jit(solution)/shard_map/ppermute | solution.py:404
  87.7 1.5 %collective-permute-start.19 = (bf16[80,256]{1,0:T(8,128)(2,1)S(1)}, bf16[80,256]{1,0:T(8,128)(2,1)S(1)}, u32[]{:S(2)}, u32[]{:S(2)}) collective-permute-start(bf16[80,256]{1,0:T(8,128)(2,1)S(1)} %get-tuple-element.52), channel_id=1, source_target_pairs={{0,64},{32,96},{64,0},{96,32},{1,65},{33,97},{65,1},{97,33},{2,66}... | collective-permute-start | bytes 122888 | tf_op jit(solution)/shard_map/ppermute | solution.py:391
  89.2 2.0 %collective-permute-start.20 = (bf16[80,256]{1,0:T(8,128)(2,1)S(1)}, bf16[80,256]{1,0:T(8,128)(2,1)S(1)}, u32[]{:S(2)}, u32[]{:S(2)}) collective-permute-start(bf16[80,256]{1,0:T(8,128)(2,1)S(1)} %get-tuple-element.53), channel_id=1, source_target_pairs={{0,96},{32,0},{64,32},{96,64},{1,97},{33,1},{65,33},{97,65},{2,98}... | collective-permute-start | bytes 122888 | tf_op jit(solution)/shard_map/ppermute | solution.py:391
  91.3 1.8 %collective-permute-done.19.a2 = bf16[80,256]{1,0:T(8,128)(2,1)S(1)} collective-permute-done((bf16[80,256]{1,0:T(8,128)(2,1)S(1)}, bf16[80,256]{1,0:T(8,128)(2,1)S(1)}, u32[]{:S(2)}, u32[]{:S(2)}) %collective-permute-start.19) | collective-permute-done | bytes 40992 | tf_op jit(solution)/shard_map/ppermute | solution.py:391
  93.1 16.0 %all_to_all.15.parts = bf16[8,80,256]{2,1,0:T(8,128)(2,1)S(1)} all-to-all(bf16[8,80,256]{2,1,0:T(8,128)(2,1)S(1)} %add_near.1), channel_id=1, replica_groups=mesh['zh'=2,'zl'=4,'y'=4,'c'=2,'x'=4] {'zh','zl'}, dimensions={0} | all-to-all | bytes 655360 | tf_op jit(solution)/shard_map/all_to_all | solution.py:505
  110.2 2.4 %collective-permute-start.22 = (bf16[80,1024]{1,0:T(8,128)(2,1)S(1)}, bf16[80,1024]{1,0:T(8,128)(2,1)S(1)}, u32[]{:S(2)}, u32[]{:S(2)}) collective-permute-start(bf16[80,1024]{1,0:T(8,128)(2,1)S(1)} %join.1.o0), channel_id=1, source_target_pairs={{0,16},{8,24},{16,0},{24,8},{1,17},{9,25},{17,1},{25,9},{2,18},{10... | collective-permute-start | bytes 491528 | tf_op jit(solution)/shard_map/ppermute | solution.py:391
  113.4 4.4 %collective-permute-start.24 = (bf16[80,1024]{1,0:T(8,128)(2,1)S(1)}, bf16[80,1024]{1,0:T(8,128)(2,1)S(1)}, u32[]{:S(2)}, u32[]{:S(2)}) collective-permute-start(bf16[80,1024]{1,0:T(8,128)(2,1)S(1)} %join.1.o0), channel_id=1, source_target_pairs={{0,4},{4,0},{1,5},{5,1},{2,6},{6,2},{3,7},{7,3},{8,12},{12,8},{9,1... | collective-permute-start | bytes 491528 | tf_op jit(solution)/shard_map/ppermute | solution.py:391
  117.8 1.7 %collective-permute-start.25 = (bf16[80,1024]{1,0:T(8,128)(2,1)S(1)}, bf16[80,1024]{1,0:T(8,128)(2,1)S(1)}, u32[]{:S(2)}, u32[]{:S(2)}) collective-permute-start(bf16[80,1024]{1,0:T(8,128)(2,1)S(1)} %collective-permute-done.21.o1), channel_id=1, source_target_pairs={{0,4},{4,0},{1,5},{5,1},{2,6},{6,2},{3,7},{7,3},{8,12},{12,8},{9,1... | collective-permute-start | bytes 491528 | tf_op jit(solution)/shard_map/ppermute | solution.py:391
  119.5 2.3 %collective-permute-start.26 = (bf16[80,1024]{1,0:T(8,128)(2,1)S(1)}, bf16[80,1024]{1,0:T(8,128)(2,1)S(1)}, u32[]{:S(2)}, u32[]{:S(2)}) collective-permute-start(bf16[80,1024]{1,0:T(8,128)(2,1)S(1)} %collective-permute-done.22.o2), channel_id=1, source_target_pairs={{0,4},{4,0},{1,5},{5,1},{2,6},{6,2},{3,7},{7,3},{8,12},{12,8},{9,1... | collective-permute-start | bytes 491528 | tf_op jit(solution)/shard_map/ppermute | solution.py:391
  123.2 1.8 %place.1 = (f32[256,2048]{1,0:T(8,128)}, f32[128,1024]{1,0:T(8,128)}) custom-call(bf16[80,1024]{1,0:T(8,128)(2,1)S(1)} %join.1.o0, bf16[80,1024]{1,0:T(8,128)(2,1)S(1)} %collective-permute-done.21.o1, bf16[80,1024]{1,0:T(8,128)(2,1)S(1)} %collective-permute-done.22.o2, bf16[80,1024]{1,0:T(8,128)(2,1)S(1)} %collective-permute-done.23.o3, ...), custom_call_target="tpu_custom_call" | custom-call | tf_op jit(solution)/shard_map/place/pallas_call | solution.py:31
  (56 shorter events, 10.2 us)
Async XLA Ops:
  0.6 38.9 %copy-start = (bf16[256,2048]{1,0:T(8,128)(2,1)S(1)}, bf16[256,2048]{1,0:T(8,128)(2,1)}, u32[]{:S(2)}) copy-start(bf16[256,2048]{1,0:T(8,128)(2,1)} %w_in.5) | copy-start | bytes 3145732
  0.6 38.9 %copy-start.4 = (s32[1,64]{1,0:T(1,128)S(1)}, s32[1,64]{1,0:T(1,128)}, u32[]{:S(2)}) copy-start(s32[1,64]{1,0:T(1,128)} %blocks_ref.3) | copy-start | bytes 772
  2.7 19.1 %collective-permute-start = (bf16[320,1024]{1,0:T(8,128)(2,1)}, bf16[320,1024]{1,0:T(8,128)(2,1)S(1)}, u32[]{:S(2)}, u32[]{:S(2)}) collective-permute-start(bf16[320,1024]{1,0:T(8,128)(2,1)} %pack.1), channel_id=1, source_target_pairs={{0,1},{1,2},{2,3},{3,0},{4,5},{5,6},{6,7},{7,4},{8,9},{9,10},{10,1... | collective-permute-start | bytes 1966088 | tf_op jit(solution)/shard_map/ppermute | solution.py:391
  4.8 17.8 %collective-permute-start.1 = (bf16[320,1024]{1,0:T(8,128)(2,1)}, bf16[320,1024]{1,0:T(8,128)(2,1)S(1)}, u32[]{:S(2)}, u32[]{:S(2)}) collective-permute-start(bf16[320,1024]{1,0:T(8,128)(2,1)} %pack.1), channel_id=1, source_target_pairs={{0,3},{1,0},{2,1},{3,2},{4,7},{5,4},{6,5},{7,6},{8,11},{9,8},{10,9... | collective-permute-start | bytes 1966088 | tf_op jit(solution)/shard_map/ppermute | solution.py:391
  8.8 30.7 %all-to-all-start = ((bf16[64,16,256]{2,1,0:T(8,128)(2,1)}), bf16[64,16,256]{2,1,0:T(8,128)(2,1)S(1)}, u32[]{:S(2)}, u32[]{:S(2)}) async-start(bf16[64,16,256]{2,1,0:T(8,128)(2,1)} %bitcast.12), calls=%async_computation | async-start | bytes 1048576 | tf_op jit(solution)/shard_map/all_to_all | solution.py:426
  21.9 10.2 %collective-permute-start.2 = (bf16[160,1024]{1,0:T(8,128)(2,1)S(1)}, bf16[160,1024]{1,0:T(8,128)(2,1)}, u32[]{:S(2)}, u32[]{:S(2)}) collective-permute-start(bf16[160,1024]{1,0:T(8,128)(2,1)S(1)} %slice.8), channel_id=1, source_target_pairs={{0,1},{1,2},{2,3},{3,0},{4,5},{5,6},{6,7},{7,4},{8,9},{9,10},{10,1... | collective-permute-start | bytes 983048 | tf_op jit(solution)/shard_map/ppermute | solution.py:391
  22.0 17.6 %collective-permute-start.4 = (bf16[320,1024]{1,0:T(8,128)(2,1)S(1)}, bf16[320,1024]{1,0:T(8,128)(2,1)}, u32[]{:S(2)}, u32[]{:S(2)}) collective-permute-start(bf16[320,1024]{1,0:T(8,128)(2,1)S(1)} %collective-permute-done.a1), channel_id=1, source_target_pairs={{0,4},{4,0},{1,5},{5,1},{2,6},{6,2},{3,7},{7,3},{8,12},{12,8},{9,1... | collective-permute-start | bytes 1966088 | tf_op jit(solution)/shard_map/ppermute | solution.py:391
  22.7 16.8 %collective-permute-start.5 = (bf16[320,1024]{1,0:T(8,128)(2,1)S(1)}, bf16[320,1024]{1,0:T(8,128)(2,1)}, u32[]{:S(2)}, u32[]{:S(2)}) collective-permute-start(bf16[320,1024]{1,0:T(8,128)(2,1)S(1)} %collective-permute-done.1.a2), channel_id=1, source_target_pairs={{0,4},{4,0},{1,5},{5,1},{2,6},{6,2},{3,7},{7,3},{8,12},{12,8},{9,1... | collective-permute-start | bytes 1966088 | tf_op jit(solution)/shard_map/ppermute | solution.py:391
  22.8 10.6 %collective-permute-start.3 = (bf16[160,1024]{1,0:T(8,128)(2,1)S(1)}, bf16[160,1024]{1,0:T(8,128)(2,1)}, u32[]{:S(2)}, u32[]{:S(2)}) collective-permute-start(bf16[160,1024]{1,0:T(8,128)(2,1)S(1)} %slice.9), channel_id=1, source_target_pairs={{0,3},{1,0},{2,1},{3,2},{4,7},{5,4},{6,5},{7,6},{8,11},{9,8},{10,9... | collective-permute-start | bytes 983048 | tf_op jit(solution)/shard_map/ppermute | solution.py:391
  32.1 7.5 %collective-permute-start.6 = (bf16[160,1024]{1,0:T(8,128)(2,1)}, bf16[160,1024]{1,0:T(8,128)(2,1)}, u32[]{:S(2)}, u32[]{:S(2)}) collective-permute-start(bf16[160,1024]{1,0:T(8,128)(2,1)} %collective-permute-done.2.a3), channel_id=1, source_target_pairs={{0,4},{4,0},{1,5},{5,1},{2,6},{6,2},{3,7},{7,3},{8,12},{12,8},{9,1... | collective-permute-start | bytes 983048 | tf_op jit(solution)/shard_map/ppermute | solution.py:391
  33.4 6.2 %collective-permute-start.7 = (bf16[160,1024]{1,0:T(8,128)(2,1)}, bf16[160,1024]{1,0:T(8,128)(2,1)}, u32[]{:S(2)}, u32[]{:S(2)}) collective-permute-start(bf16[160,1024]{1,0:T(8,128)(2,1)} %collective-permute-done.3.a4), channel_id=1, source_target_pairs={{0,4},{4,0},{1,5},{5,1},{2,6},{6,2},{3,7},{7,3},{8,12},{12,8},{9,1... | collective-permute-start | bytes 983048 | tf_op jit(solution)/shard_map/ppermute | solution.py:391
  47.6 5.0 %collective-permute-start.9 = (bf16[4,256,512]{2,1,0:T(8,128)(2,1)S(1)}, bf16[4,256,512]{2,1,0:T(8,128)(2,1)S(1)}, u32[]{:S(2)}, u32[]{:S(2)}) collective-permute-start(bf16[4,256,512]{2,1,0:T(8,128)(2,1)S(1)} %get-tuple-element.31.shared), channel_id=1, source_target_pairs={{0,4},{4,0},{1,5},{5,1},{2,6},{6,2},{3,7},{7,3},{8,12},{12,8},{9,1... | collective-permute-start | bytes 3145736 | tf_op jit(solution)/shard_map/ppermute | solution.py:391
  48.2 4.4 %collective-permute-start.10 = (bf16[256,1024]{1,0:T(8,128)(2,1)S(1)}, bf16[256,1024]{1,0:T(8,128)(2,1)S(1)}, u32[]{:S(2)}, u32[]{:S(2)}) collective-permute-start(bf16[256,1024]{1,0:T(8,128)(2,1)S(1)} %get-tuple-element.34.sent), channel_id=1, source_target_pairs={{0,4},{4,0},{1,5},{5,1},{2,6},{6,2},{3,7},{7,3},{8,12},{12,8},{9,1... | collective-permute-start | bytes 1572872 | tf_op jit(solution)/shard_map/ppermute | solution.py:391
  52.2 5.8 %collective-permute-start.8 = (bf16[32,16,256]{2,1,0:T(8,128)(2,1)S(1)}, bf16[32,16,256]{2,1,0:T(8,128)(2,1)S(1)}, u32[]{:S(2)}, u32[]{:S(2)}) collective-permute-start(bf16[32,16,256]{2,1,0:T(8,128)(2,1)S(1)} %get-tuple-element.36), channel_id=1, source_target_pairs={{0,4},{4,0},{1,5},{5,1},{2,6},{6,2},{3,7},{7,3},{8,12},{12,8},{9,1... | collective-permute-start | bytes 786440 | tf_op jit(solution)/shard_map/ppermute | solution.py:391
  55.3 11.2 %collective-permute-start.11 = (bf16[2,2,80,1024]{3,2,1,0:T(8,128)(2,1)}, bf16[2,2,80,1024]{3,2,1,0:T(8,128)(2,1)S(1)}, u32[]{:S(2)}, u32[]{:S(2)}) collective-permute-start(bf16[2,2,80,1024]{3,2,1,0:T(8,128)(2,1)} %get-tuple-element.40), channel_id=1, source_target_pairs={{0,1},{1,2},{2,3},{3,0},{4,12},{5,13},{6,14},{7,15},{8,9},{9,10},{... | collective-permute-start | bytes 1966088 | tf_op jit(solution)/shard_map/ppermute | solution.py:404
  56.5 10.0 %collective-permute-start.12 = (bf16[2,2,80,1024]{3,2,1,0:T(8,128)(2,1)}, bf16[2,2,80,1024]{3,2,1,0:T(8,128)(2,1)S(1)}, u32[]{:S(2)}, u32[]{:S(2)}) collective-permute-start(bf16[2,2,80,1024]{3,2,1,0:T(8,128)(2,1)} %get-tuple-element.41), channel_id=1, source_target_pairs={{0,3},{1,0},{2,1},{3,2},{4,28},{5,29},{6,30},{7,31},{8,11},{9,8},{... | collective-permute-start | bytes 1966088 | tf_op jit(solution)/shard_map/ppermute | solution.py:404
  58.8 23.4 %all-to-all-start.1 = ((bf16[32,32,256]{2,1,0:T(8,128)(2,1)}), bf16[32,32,256]{2,1,0:T(8,128)(2,1)S(1)}, u32[]{:S(2)}, u32[]{:S(2)}) async-start(bf16[32,32,256]{2,1,0:T(8,128)(2,1)} %copy-done.2), calls=%async_computation.1 | async-start | bytes 1048576 | tf_op jit(solution)/shard_map/all_to_all | solution.py:481
  66.6 10.9 %collective-permute-start.13 = (bf16[2,80,1024]{2,1,0:T(8,128)(2,1)S(1)}, bf16[2,80,1024]{2,1,0:T(8,128)(2,1)S(1)}, u32[]{:S(2)}, u32[]{:S(2)}) collective-permute-start(bf16[2,80,1024]{2,1,0:T(8,128)(2,1)S(1)} %get-tuple-element.42), channel_id=1, source_target_pairs={{0,1},{1,2},{2,3},{3,0},{4,12},{5,13},{6,14},{7,15},{8,9},{9,10},{... | collective-permute-start | bytes 983048 | tf_op jit(solution)/shard_map/ppermute | solution.py:404
  67.9 9.7 %collective-permute-start.14 = (bf16[2,80,1024]{2,1,0:T(8,128)(2,1)S(1)}, bf16[2,80,1024]{2,1,0:T(8,128)(2,1)S(1)}, u32[]{:S(2)}, u32[]{:S(2)}) collective-permute-start(bf16[2,80,1024]{2,1,0:T(8,128)(2,1)S(1)} %get-tuple-element.43), channel_id=1, source_target_pairs={{0,3},{1,0},{2,1},{3,2},{4,28},{5,29},{6,30},{7,31},{8,11},{9,8},{... | collective-permute-start | bytes 983048 | tf_op jit(solution)/shard_map/ppermute | solution.py:404
  78.5 7.4 %collective-permute-start.15 = (bf16[80,1024]{1,0:T(8,128)(2,1)}, bf16[80,1024]{1,0:T(8,128)(2,1)S(1)}, u32[]{:S(2)}, u32[]{:S(2)}) collective-permute-start(bf16[80,1024]{1,0:T(8,128)(2,1)} %get-tuple-element.44), channel_id=1, source_target_pairs={{0,8},{1,9},{2,10},{3,11},{4,5},{5,6},{6,7},{7,4},{8,16},{9,17},{1... | collective-permute-start | bytes 491528 | tf_op jit(solution)/shard_map/ppermute | solution.py:404
  78.5 7.4 %collective-permute-start.16 = (bf16[80,1024]{1,0:T(8,128)(2,1)}, bf16[80,1024]{1,0:T(8,128)(2,1)S(1)}, u32[]{:S(2)}, u32[]{:S(2)}) collective-permute-start(bf16[80,1024]{1,0:T(8,128)(2,1)} %get-tuple-element.48), channel_id=1, source_target_pairs={{0,16},{1,17},{2,18},{3,19},{4,6},{5,7},{6,4},{7,5},{8,24},{9,25},... | collective-permute-start | bytes 491528 | tf_op jit(solution)/shard_map/ppermute | solution.py:404
  81.0 5.4 %collective-permute-start.17 = (bf16[80,1024]{1,0:T(8,128)(2,1)}, bf16[80,1024]{1,0:T(8,128)(2,1)S(1)}, u32[]{:S(2)}, u32[]{:S(2)}) collective-permute-start(bf16[80,1024]{1,0:T(8,128)(2,1)} %get-tuple-element.49), channel_id=1, source_target_pairs={{0,24},{1,25},{2,26},{3,27},{4,7},{5,4},{6,5},{7,6},{8,0},{9,1},{1... | collective-permute-start | bytes 491528 | tf_op jit(solution)/shard_map/ppermute | solution.py:404
  86.5 4.8 %collective-permute-start.18 = (bf16[80,256]{1,0:T(8,128)(2,1)S(1)}, bf16[80,256]{1,0:T(8,128)(2,1)S(1)}, u32[]{:S(2)}, u32[]{:S(2)}) collective-permute-start(bf16[80,256]{1,0:T(8,128)(2,1)S(1)} %get-tuple-element.51), channel_id=1, source_target_pairs={{0,32},{32,64},{64,96},{96,0},{1,33},{33,65},{65,97},{97,1},{2,34}... | collective-permute-start | bytes 122888 | tf_op jit(solution)/shard_map/ppermute | solution.py:391
  87.7 5.4 %collective-permute-start.19 = (bf16[80,256]{1,0:T(8,128)(2,1)S(1)}, bf16[80,256]{1,0:T(8,128)(2,1)S(1)}, u32[]{:S(2)}, u32[]{:S(2)}) collective-permute-start(bf16[80,256]{1,0:T(8,128)(2,1)S(1)} %get-tuple-element.52), channel_id=1, source_target_pairs={{0,64},{32,96},{64,0},{96,32},{1,65},{33,97},{65,1},{97,33},{2,66}... | collective-permute-start | bytes 122888 | tf_op jit(solution)/shard_map/ppermute | solution.py:391
  89.2 3.9 %collective-permute-start.20 = (bf16[80,256]{1,0:T(8,128)(2,1)S(1)}, bf16[80,256]{1,0:T(8,128)(2,1)S(1)}, u32[]{:S(2)}, u32[]{:S(2)}) collective-permute-start(bf16[80,256]{1,0:T(8,128)(2,1)S(1)} %get-tuple-element.53), channel_id=1, source_target_pairs={{0,96},{32,0},{64,32},{96,64},{1,97},{33,1},{65,33},{97,65},{2,98}... | collective-permute-start | bytes 122888 | tf_op jit(solution)/shard_map/ppermute | solution.py:391
  109.2 8.6 %collective-permute-start.21 = (bf16[80,1024]{1,0:T(8,128)(2,1)S(1)}, bf16[80,1024]{1,0:T(8,128)(2,1)S(1)}, u32[]{:S(2)}, u32[]{:S(2)}) collective-permute-start(bf16[80,1024]{1,0:T(8,128)(2,1)S(1)} %join.1.o0), channel_id=1, source_target_pairs={{0,8},{8,16},{16,24},{24,0},{1,9},{9,17},{17,25},{25,1},{2,10},{10... | collective-permute-start | bytes 491528 | tf_op jit(solution)/shard_map/ppermute | solution.py:391
  110.2 9.3 %collective-permute-start.22 = (bf16[80,1024]{1,0:T(8,128)(2,1)S(1)}, bf16[80,1024]{1,0:T(8,128)(2,1)S(1)}, u32[]{:S(2)}, u32[]{:S(2)}) collective-permute-start(bf16[80,1024]{1,0:T(8,128)(2,1)S(1)} %join.1.o0), channel_id=1, source_target_pairs={{0,16},{8,24},{16,0},{24,8},{1,17},{9,25},{17,1},{25,9},{2,18},{10... | collective-permute-start | bytes 491528 | tf_op jit(solution)/shard_map/ppermute | solution.py:391
  112.6 9.2 %collective-permute-start.23 = (bf16[80,1024]{1,0:T(8,128)(2,1)S(1)}, bf16[80,1024]{1,0:T(8,128)(2,1)S(1)}, u32[]{:S(2)}, u32[]{:S(2)}) collective-permute-start(bf16[80,1024]{1,0:T(8,128)(2,1)S(1)} %join.1.o0), channel_id=1, source_target_pairs={{0,24},{8,0},{16,8},{24,16},{1,25},{9,1},{17,9},{25,17},{2,26},{10... | collective-permute-start | bytes 491528 | tf_op jit(solution)/shard_map/ppermute | solution.py:391
  113.4 8.7 %collective-permute-start.24 = (bf16[80,1024]{1,0:T(8,128)(2,1)S(1)}, bf16[80,1024]{1,0:T(8,128)(2,1)S(1)}, u32[]{:S(2)}, u32[]{:S(2)}) collective-permute-start(bf16[80,1024]{1,0:T(8,128)(2,1)S(1)} %join.1.o0), channel_id=1, source_target_pairs={{0,4},{4,0},{1,5},{5,1},{2,6},{6,2},{3,7},{7,3},{8,12},{12,8},{9,1... | collective-permute-start | bytes 491528 | tf_op jit(solution)/shard_map/ppermute | solution.py:391
  117.8 4.3 %collective-permute-start.25 = (bf16[80,1024]{1,0:T(8,128)(2,1)S(1)}, bf16[80,1024]{1,0:T(8,128)(2,1)S(1)}, u32[]{:S(2)}, u32[]{:S(2)}) collective-permute-start(bf16[80,1024]{1,0:T(8,128)(2,1)S(1)} %collective-permute-done.21.o1), channel_id=1, source_target_pairs={{0,4},{4,0},{1,5},{5,1},{2,6},{6,2},{3,7},{7,3},{8,12},{12,8},{9,1... | collective-permute-start | bytes 491528 | tf_op jit(solution)/shard_map/ppermute | solution.py:391
  119.5 3.3 %collective-permute-start.26 = (bf16[80,1024]{1,0:T(8,128)(2,1)S(1)}, bf16[80,1024]{1,0:T(8,128)(2,1)S(1)}, u32[]{:S(2)}, u32[]{:S(2)}) collective-permute-start(bf16[80,1024]{1,0:T(8,128)(2,1)S(1)} %collective-permute-done.22.o2), channel_id=1, source_target_pairs={{0,4},{4,0},{1,5},{5,1},{2,6},{6,2},{3,7},{7,3},{8,12},{12,8},{9,1... | collective-permute-start | bytes 491528 | tf_op jit(solution)/shard_map/ppermute | solution.py:391
  121.8 1.4 %collective-permute-start.27 = (bf16[80,1024]{1,0:T(8,128)(2,1)S(1)}, bf16[80,1024]{1,0:T(8,128)(2,1)S(1)}, u32[]{:S(2)}, u32[]{:S(2)}) collective-permute-start(bf16[80,1024]{1,0:T(8,128)(2,1)S(1)} %collective-permute-done.23.o3), channel_id=1, source_target_pairs={{0,4},{4,0},{1,5},{5,1},{2,6},{6,2},{3,7},{7,3},{8,12},{12,8},{9,1... | collective-permute-start | bytes 491528 | tf_op jit(solution)/shard_map/ppermute | solution.py:391
  (4 other events, 79.6 us)
